TPU v7x, 256 devices: a whole 4x4x8 slice. The times are simulated.
256 devices in a mesh: attn: 16 (over z, core), egrp: 4 (over x), etp: 4 (over y).
Axes of the slice: x: 4, y: 4, z: 8, core: 2. Of those that a mesh axis runs over, the one named last changes fastest.
Arguments:
- queries: bfloat16 [512, 6144], P(('attn', 'egrp'), 'etp'), may hold values from -100 to 100
- cache_keys: bfloat16 [512, 512, 1024], P(('attn', 'egrp'), None, 'etp'), may hold values from -5 to 5
- stored_values: bfloat16 [512, 512, 1024], P(('attn', 'egrp'), None, 'etp'), may hold values from -6 to 6
- lengths: int32 [512], P(('attn', 'egrp')), may hold values from 2 to 512, as said below
- residual_in: bfloat16 [512, 6144], P(('attn', 'egrp'), 'etp'), may hold values from -25 to 25
- norm_gain: bfloat16 [6144], replicated, may hold values from 0.25 to 1.75
- expert_ids: int32 [512, 4], P(('attn', 'egrp')), may hold values from 0 to 7, all different within a row; in each aligned block of 512 rows (0 to 511, 512 to 1023, ...) at most 384 rows name the same one
- expert_scores: float32 [512, 4], P(('attn', 'egrp')), may hold values from 0.05 to 1
- w_gate: bfloat16 [8, 6144, 5376], P('egrp', 'etp', 'attn'), may hold values from -0.078125 to 0.078125
- w_up: bfloat16 [8, 6144, 5376], P('egrp', 'etp', 'attn'), may hold values from -0.078125 to 0.078125
- w_down: bfloat16 [8, 5376, 6144], P('egrp', 'attn', 'etp'), may hold values from -0.078125 to 0.078125
Outputs:
- residual: bfloat16 [512, 6144], P(('attn', 'egrp'), 'etp')
- expert_mix: bfloat16 [512, 6144], P(('attn', 'egrp'), 'etp')
Inputs may be any that keep to these rules, and one draw needn't show every extreme that they name: `expert_ids`: each row names 4 different experts; no expert is named by more than 384 rows, a bound that some block reaches. `lengths`: some row's cache is full in every draw.
All inputs are finite; a program needn't handle non-finite values.
Results may differ from a plain program's by a relative error of at most 0.018.
Values may be sent and summed in bfloat16 or wider, within the bound.
No kernel may reach another device: no remote copies, remote signals or barrier semaphores. Data moves between devices by JAX's collectives and lax.ppermute only.
A program may use at most 64 MiB of HBM per device.

v0:
```python
import math

import jax
import jax.numpy as jnp
from jax import lax
from jax.sharding import PartitionSpec as P

HEAD_SIZE = 128
EXPERTS = 8


epsilon = 1e-05


def attend(queries, cache_keys, stored_values, lengths):
    row_count = queries.shape[0]
    span = cache_keys.shape[1]
    kv_heads = cache_keys.shape[2] // HEAD_SIZE
    query_group = queries.shape[1] // (kv_heads * HEAD_SIZE)
    query_blocks = queries.reshape(row_count, kv_heads, query_group, HEAD_SIZE)
    key_blocks = cache_keys.reshape(row_count, span, kv_heads, HEAD_SIZE)
    value_blocks = stored_values.reshape(row_count, span, kv_heads, HEAD_SIZE)
    scores = jnp.einsum(
        "rhgd,rlhd->rhgl", query_blocks, key_blocks, preferred_element_type=jnp.float32
    ) * (1.0 / math.sqrt(HEAD_SIZE))
    position = lax.broadcasted_iota(jnp.int32, (1, 1, 1, span), 3)
    visible = position < lengths[:, None, None, None]
    scores = jnp.where(visible, scores, -1e30)
    peak = jnp.max(scores, axis=-1, keepdims=True)
    expd = jnp.exp(scores - peak)
    totals = jnp.sum(expd, axis=-1, keepdims=True)
    weights_bf = (expd / totals).astype(jnp.bfloat16)
    attended = jnp.einsum(
        "rhgl,rlhd->rhgd", weights_bf, value_blocks, preferred_element_type=jnp.float32
    )
    return attended.reshape(row_count, kv_heads * query_group * HEAD_SIZE).astype(jnp.bfloat16)


def per_device(
    queries,
    cache_keys,
    stored_values,
    lengths,
    residual_in,
    norm_gain,
    expert_ids,
    expert_scores,
    w_gate,
    w_up,
    w_down,
):
    attended = attend(queries, cache_keys, stored_values, lengths)
    stream = (residual_in.astype(jnp.float32) + attended.astype(jnp.float32)).astype(jnp.bfloat16)
    row_count = stream.shape[0]
    width_dev = stream.shape[1]
    whole_rows = lax.all_gather(stream, "etp", axis=1, tiled=True).astype(jnp.float32)
    row_mean = jnp.mean(whole_rows, axis=1, keepdims=True)
    row_var = jnp.mean(jnp.square(whole_rows - row_mean), axis=1, keepdims=True)
    etp_index = lax.axis_index("etp")
    gain_own = lax.dynamic_slice_in_dim(norm_gain, etp_index * width_dev, width_dev, 0).astype(
        jnp.float32
    )
    normed = (
        (stream.astype(jnp.float32) - row_mean) * lax.rsqrt(row_var + epsilon) * gain_own[None, :]
    ).astype(jnp.bfloat16)
    shares = expert_scores / jnp.sum(expert_scores, axis=1, keepdims=True)
    expert_iota = lax.broadcasted_iota(jnp.int32, (1, 1, EXPERTS), 2)
    route = jnp.sum(
        jnp.where(expert_ids[:, :, None] == expert_iota, shares[:, :, None], 0.0), axis=1
    ).astype(jnp.bfloat16)
    tokens_all, route_all = (
        lax.all_gather(normed, ("attn", "egrp"), axis=0, tiled=True),
        lax.all_gather(route, ("attn", "egrp"), axis=0, tiled=True),
    )
    local_count = w_gate.shape[0]
    route_local = lax.dynamic_slice_in_dim(
        route_all, lax.axis_index("egrp") * local_count, local_count, 1
    ).astype(jnp.float32)
    route_by_expert = route_local.T
    gate_part = jnp.einsum("rd,edf->erf", tokens_all, w_gate, preferred_element_type=jnp.float32)
    up_part = jnp.einsum("rd,edf->erf", tokens_all, w_up, preferred_element_type=jnp.float32)
    gate_sum, up_sum = lax.psum((gate_part, up_part), "etp")
    hidden = (jax.nn.silu(gate_sum) * up_sum * route_by_expert[:, :, None]).astype(jnp.bfloat16)
    reduced = lax.psum_scatter(
        jnp.einsum("erf,efd->rd", hidden, w_down, preferred_element_type=jnp.float32),
        "attn",
        scatter_dimension=0,
        tiled=True,
    )
    returned = lax.all_to_all(
        reduced.reshape(lax.axis_size("egrp"), row_count, width_dev),
        "egrp",
        split_axis=0,
        concat_axis=0,
        tiled=True,
    )
    expert_mix = jnp.sum(returned, axis=0).astype(jnp.bfloat16)
    return (stream, expert_mix)


def solution(mesh):
    placed = (
        P(("attn", "egrp"), "etp"),
        P(("attn", "egrp"), None, "etp"),
        P(("attn", "egrp"), None, "etp"),
        P(("attn", "egrp")),
        P(("attn", "egrp"), "etp"),
        P(),
        P(("attn", "egrp"), None),
        P(("attn", "egrp"), None),
        P("egrp", "etp", "attn"),
        P("egrp", "etp", "attn"),
        P("egrp", "attn", "etp"),
    )
    return jax.shard_map(
        per_device,
        mesh=mesh,
        in_specs=placed,
        out_specs=(P(("attn", "egrp"), "etp"), P(("attn", "egrp"), "etp")),
        check_vma=False,
    )
```

profile of v0, /device:TPU:1, one launch (start us, length us, event | category | flops | bytes accessed | tf_op | source)
XLA Modules:
  0.0 281.4 jit_solution(16740536943535903550)
XLA Ops:
  7.2 0.0 copy-start
  7.2 0.0 all-gather.2.cloned.1.call-start
  7.2 0.9 iota_compare_fusion.1
  8.1 0.7 copy-done
  8.8 1.4 fusion.22
  10.2 0.0 copy-start.2
  10.2 0.2 fusion.38
  10.4 2.0 fusion.28
  12.5 0.0 copy-done.2
  12.5 0.0 copy-start.1
  12.5 10.5 %all_gather.9 = bf16[8,6144]{1,0:T(8,128)(2,1)S(1)} all-gather(bf16[8,1536]{1,0:T(8,128)(2,1)S(1)} %add_convert_fusion), channel_id=1, replica_groups=mesh['attn'=16,'egrp'=4,'etp'=4] {'etp'}, dimensions={1}, use_global_device_ids=true | all-gather | bytes 122880 | tf_op jit(solution)/shard_map/all_gather | solution.py:56
  23.0 0.2 convert_reduce_fusion
  23.1 0.2 fusion.34
  23.4 0.8 dynamic-slice_convert_fusion
  24.2 0.7 multiply_convert_fusion.2
  24.8 0.0 all-gather.2.cloned.1.call-update
  24.9 0.0 all-reduce.3.cloned.1.call-start
  24.9 82.4 %all-gather.2.cloned.1.call-done = bf16[512,1536]{1,0:T(8,128)(2,1)} async-done(((bf16[8,1536]{1,0:T(8,128)(2,1)}), bf16[512,1536]{1,0:T(8,128)(2,1)}) %all-gather.2.cloned.1.call-update) | async-done | bytes 1572880 | tf_op jit(solution)/shard_map/all_gather | solution.py:72
  107.4 0.0 copy-start.5
  107.4 0.0 copy-start.6
  107.4 4.5 %fusion.14 = f32[2,512,336]{1,2,0:T(8,128)} fusion(bf16[2,1536,336]{1,2,0:T(8,128)(2,1)} %param.20, bf16[512,1536]{1,0:T(8,128)(2,1)} %all-gather.2.cloned.1.call-done), kind=kOutput, calls=%fused_computation.13 | convolution fusion | flops 1056964608 | bytes 5013504 | tf_op jit(solution)/shard_map/rd,edf->erf/dot_general | solution.py:81
  111.9 0.0 copy-done.1
  111.9 0.0 copy-done.5
  111.9 0.0 copy-done.6
  111.9 2.3 fusion.11
  114.3 0.0 copy-start.3
  114.3 0.0 copy-start.4
  114.3 0.0 all-reduce.3.cloned.1.call-update
  114.3 0.0 reduce-scatter.2.cloned.1.call-start
  114.3 0.6 copy-done.3
  115.0 0.0 copy-done.4
  115.0 0.1 select_reduce_fusion
  115.1 87.2 %all_gather.11 = bf16[512,8]{1,0:T(8,128)(2,1)S(1)} all-gather(bf16[8,8]{1,0:T(8,128)(2,1)S(1)} %select_reduce_fusion), channel_id=1, replica_groups=mesh['attn'=16,'egrp'=4,'etp'=4] {'attn','egrp'}, dimensions={0}, use_global_device_ids=true | all-gather | bytes 8320 | tf_op jit(solution)/shard_map/all_gather | solution.py:73
  202.2 0.1 convert_bitcast_fusion
  202.4 0.1 copy.32
  202.5 0.0 all-reduce.3.cloned.1.call-done
  202.5 5.6 %convolution_bitcast_fusion = f32[512,1536]{1,0:T(8,128)} fusion(bf16[2,336,1536]{2,1,0:T(8,128)(2,1)} %param.21, f32[2,512,336]{1,2,0:T(8,128)} %get-tuple-element.2, f32[2,512,336]{1,2,0:T(8,128)} %get-tuple-element.3, f32[2,512]{1,0:T(2,128)S(1)} %copy.32), kind=kOutput, calls=%fused_computation.1 | convolution fusion | flops 1059373056 | bytes 7966720 | tf_op jit(solution)/shard_map/erf,efd->rd/dot_general | solution.py:85
  208.0 0.0 reduce-scatter.2.cloned.1.call-update
  208.1 57.1 %reduce-scatter.2.cloned.1.call-done = f32[32,1536]{1,0:T(8,128)} async-done(((f32[512,1536]{1,0:T(8,128)}), f32[32,1536]{1,0:T(8,128)}) %reduce-scatter.2.cloned.1.call-update) | async-done | bytes 196624 | tf_op jit(solution)/shard_map/reduce_scatter | solution.py:84
  265.2 9.1 %all_to_all.5 = f32[4,8,1536]{2,1,0:T(8,128)S(1)} all-to-all(f32[4,8,1536]{2,1,0:T(8,128)} %bitcast.46), channel_id=1, replica_groups=mesh['attn'=16,'egrp'=4,'etp'=4] {'egrp'}, dimensions={0} | all-to-all | bytes 393216 | tf_op jit(solution)/shard_map/all_to_all | solution.py:90
  274.3 0.6 reduce_sum.59
  (6 shorter events, 0.1 us)
Async XLA Ops:
  7.2 1.6 copy-start
  7.2 100.2 %all-gather.2.cloned.1.call-start = ((), (), s32[]{:S(2)}) async-start(), calls=%async_computation.2 | async-start | bytes 1597440 | tf_op jit(solution)/shard_map/all_gather | solution.py:72
  10.2 2.3 copy-start.2
  12.5 99.4 %copy-start.1 = (bf16[8,1536]{1,0:T(8,128)(2,1)}, bf16[8,1536]{1,0:T(8,128)(2,1)S(1)}, u32[]{:S(2)}) copy-start(bf16[8,1536]{1,0:T(8,128)(2,1)S(1)} %add_convert_fusion) | copy-start | bytes 73732
  24.9 177.6 %all-reduce.3.cloned.1.call-start = ((), (), s32[]{:S(2)}) async-start(), calls=%async_computation.4 | async-start | bytes 5505024 | tf_op jit(solution)/shard_map/psum | solution.py:82
  107.4 4.6 %copy-start.5 = (bf16[2,1536,336]{1,2,0:T(8,128)(2,1)S(1)}, bf16[2,1536,336]{1,2,0:T(8,128)(2,1)}, u32[]{:S(2)}) copy-start(bf16[2,1536,336]{1,2,0:T(8,128)(2,1)} %param.19) | copy-start | bytes 6193156
  107.4 4.6 %copy-start.6 = (bf16[512,1536]{1,0:T(8,128)(2,1)S(1)}, bf16[512,1536]{1,0:T(8,128)(2,1)}, u32[]{:S(2)}) copy-start(bf16[512,1536]{1,0:T(8,128)(2,1)} %all-gather.2.cloned.1.call-done) | copy-start | bytes 4718596
  114.3 0.7 copy-start.3
  114.3 0.7 copy-start.4
  114.3 150.9 %reduce-scatter.2.cloned.1.call-start = ((), (), s32[]{:S(2)}) async-start(), calls=%async_computation.3 | async-start | bytes 3342336 | tf_op jit(solution)/shard_map/reduce_scatter | solution.py:84
Sparse Core Ops, SparseCore 0:
  25.0 82.3 all-gather.1
  114.4 72.0 all-reduce.2
  208.2 56.9 reduce-scatter.1
where the time goes:
time: 285 us; the launch traced here: 281 us
  waiting for transfers between devices  140 us (49%)
  blocking collectives  107 us (38%)
  matrix products  15.9 us (6%)
  between operations  13.8 us (5%)
  other arithmetic  3.8 us (1%)
    all_gather x1, blocking collectives, per_device(): lax.all_gather(route, ('attn', 'egrp'), axis=0, tiled=True)  87.2 us
    all_gather x1, waiting for transfers between devices, per_device(): lax.all_gather(normed, ('attn', 'egrp'), axis=0, tiled=True)  82.4 us
    reduce_scatter x1, waiting for transfers between devices, per_device(): lax.psum_scatter(jnp.einsum('erf,efd->rd', hidden, w_down, preferred_elem...  57.1 us
    all_gather x1, blocking collectives, per_device(): lax.all_gather(stream, 'etp', axis=1, tiled=True).astype(jnp.float32)  10.5 us
    all_to_all x1, blocking collectives, per_device(): lax.all_to_all(reduced.reshape(lax.axis_size('egrp'), row_count, width_de...  9.09 us
  transfers between devices with their start and end apart: 3, of which 2 were waited for; matrix products, arithmetic and copies ran while one was open for 0% of the time, Pallas kernels for 0%

commit v1 on v0

v1 whole, which is shorter than its diff:
```python
import math

import jax
import jax.numpy as jnp
from jax import lax
from jax.sharding import PartitionSpec as P

HEAD_SIZE = 128
EXPERTS = 8

epsilon = 1e-05
f32, bf16 = jnp.float32, jnp.bfloat16


def attend(queries, cache_keys, stored_values, lengths):
    row_count = queries.shape[0]
    span = cache_keys.shape[1]
    kv_heads = cache_keys.shape[2] // HEAD_SIZE
    query_group = queries.shape[1] // (kv_heads * HEAD_SIZE)
    query_blocks = queries.reshape(row_count, kv_heads, query_group, HEAD_SIZE)
    key_blocks = cache_keys.reshape(row_count, span, kv_heads, HEAD_SIZE)
    value_blocks = stored_values.reshape(row_count, span, kv_heads, HEAD_SIZE)
    scores = jnp.einsum(
        "rhgd,rlhd->rhgl", query_blocks, key_blocks, preferred_element_type=f32
    ) * (1.0 / math.sqrt(HEAD_SIZE))
    position = lax.broadcasted_iota(jnp.int32, (1, 1, 1, span), 3)
    visible = position < lengths[:, None, None, None]
    scores = jnp.where(visible, scores, -1e30)
    peak = jnp.max(scores, axis=-1, keepdims=True)
    expd = jnp.exp(scores - peak)
    totals = jnp.sum(expd, axis=-1, keepdims=True)
    weights_bf = (expd / totals).astype(bf16)
    attended = jnp.einsum(
        "rhgl,rlhd->rhgd", weights_bf, value_blocks, preferred_element_type=f32
    )
    return attended.reshape(row_count, kv_heads * query_group * HEAD_SIZE).astype(bf16)


def shift(x, axis, step):
    n = lax.axis_size(axis)
    return lax.ppermute(x, axis, [(i, (i + step) % n) for i in range(n)])


def swap_core(x):
    return lax.ppermute(x, "attn", [(i, i ^ 1) for i in range(lax.axis_size("attn"))])


def per_device(
    queries,
    cache_keys,
    stored_values,
    lengths,
    residual_in,
    norm_gain,
    expert_ids,
    expert_scores,
    w_gate,
    w_up,
    w_down,
):
    z_size, x_size, y_size = lax.axis_size("attn") // 2, lax.axis_size("egrp"), lax.axis_size("etp")
    y, x = lax.axis_index("etp"), lax.axis_index("egrp")
    attended = attend(queries, cache_keys, stored_values, lengths)
    stream = (residual_in.astype(f32) + attended.astype(f32)).astype(bf16)
    rows, width = stream.shape
    shares = expert_scores / jnp.sum(expert_scores, axis=1, keepdims=True)
    expert_iota = lax.broadcasted_iota(jnp.int32, (1, 1, EXPERTS), 2)
    route = jnp.sum(
        jnp.where(expert_ids[:, :, None] == expert_iota, shares[:, :, None], 0.0), axis=1
    ).astype(bf16)

    held = jnp.concatenate([stream, jnp.pad(route, ((0, 0), (0, 128 - EXPERTS)))], axis=1)
    held = jnp.concatenate([held] + [shift(held, "attn", -2 * k) for k in range(1, z_size)], axis=0)
    held = jnp.concatenate([held] + [shift(held, "egrp", -k) for k in range(1, x_size)], axis=0)
    held = jnp.concatenate([held, swap_core(held)], axis=0)
    raw, routes = held[:, :width].astype(f32), held[:, width : width + EXPERTS]
    total = raw.shape[0]

    part_mean = jnp.mean(raw, axis=1)
    centred = raw - part_mean[:, None]
    part_dev = jnp.sum(jnp.square(centred), axis=1)
    stats = jnp.stack([part_mean, part_dev])
    all_stats = [stats] + [shift(stats, "etp", k) for k in range(1, y_size)]
    row_mean = sum(s[0] for s in all_stats) / y_size
    row_dev = sum(s[1] + width * jnp.square(s[0] - row_mean) for s in all_stats)
    row_scale = lax.rsqrt(row_dev / (width * y_size) + epsilon)

    gain = lax.dynamic_slice_in_dim(norm_gain, y * width, width, 0)
    scaled = (centred * gain.astype(f32)[None, :]).astype(bf16)
    gains = jnp.broadcast_to(gain[None, :], (8, width))

    def project(weight):
        part = jnp.einsum("edf,rd->efr", weight, scaled, preferred_element_type=f32)
        sums = jnp.einsum("edf,rd->efr", weight, gains, preferred_element_type=f32)[:, :, :1]
        return (part + sums * (part_mean - row_mean)[None, None, :]) * row_scale[None, None, :]

    both = jnp.stack([project(w_gate), project(w_up)])

    block = total // y_size

    def block_of(array, index):
        return lax.dynamic_slice_in_dim(array, lax.rem(index, y_size) * block, block, array.ndim - 1)

    mine = block_of(both, y)
    for k in range(1, y_size):
        mine = mine + shift(block_of(both, y + k).astype(bf16), "etp", k).astype(f32)
    experts_here = w_gate.shape[0]
    route_rows = lax.dynamic_slice(
        routes, (y * block, x * experts_here), (block, experts_here)
    ).astype(f32)
    hidden = (jax.nn.silu(mine[0]) * mine[1] * route_rows.T[:, None, :]).astype(bf16)
    turned = [hidden] + [shift(hidden, "etp", -k) for k in range(1, y_size)]
    whole = jnp.concatenate(turned + turned[:-1], axis=2)
    whole = lax.dynamic_slice_in_dim(whole, lax.rem(y_size - y, y_size) * block, total, 2)

    out = jnp.einsum("efr,efd->rd", whole, w_down, preferred_element_type=f32)
    half = total // 2
    out = out[:half] + swap_core(out[half:].astype(bf16)).astype(f32)
    for axis, size, stride in (("egrp", x_size, 1), ("attn", z_size, 2)):
        part = out.shape[0] // size
        summed = out[:part]
        for k in range(1, size):
            sent = out[k * part : (k + 1) * part].astype(bf16)
            summed = summed + shift(sent, axis, stride * k).astype(f32)
        out = summed
    return (stream, out.astype(bf16))


def solution(mesh):
    placed = (
        P(("attn", "egrp"), "etp"),
        P(("attn", "egrp"), None, "etp"),
        P(("attn", "egrp"), None, "etp"),
        P(("attn", "egrp")),
        P(("attn", "egrp"), "etp"),
        P(),
        P(("attn", "egrp"), None),
        P(("attn", "egrp"), None),
        P("egrp", "etp", "attn"),
        P("egrp", "etp", "attn"),
        P("egrp", "attn", "etp"),
    )
    return jax.shard_map(
        per_device,
        mesh=mesh,
        in_specs=placed,
        out_specs=(P(("attn", "egrp"), "etp"), P(("attn", "egrp"), "etp")),
        check_vma=False,
    )
```

time: 285 us -> 146 us (0.51)
  blocking collectives: 107 us -> 0 us
  waiting for transfers between devices: 140 us -> 48.9 us
  starting transfers between devices: 0.12 us -> 52.8 us
  between operations: 13.8 us -> 0.89 us
  local copies, waits for them, and re-layouts: 1.44 us -> 13.3 us
  other arithmetic: 3.8 us -> 12.6 us
    all_gather x2 -> x0, blocking collectives: 97.7 us -> none  [the longest x1 87.2 us: per_device(): lax.all_gather(route, ('attn', 'egrp'), axis=0, tiled=True)]
    all_gather x1 -> x0, waiting for transfers between devices: 82.4 us -> none  [per_device(): lax.all_gather(normed, ('attn', 'egrp'), axis=0, tiled=True)]
    reduce_scatter x1 -> x0, waiting for transfers between devices: 57.1 us -> none  [per_device(): lax.psum_scatter(jnp.einsum('erf,efd->rd', hidden, w_down, preferred_elem...]
    ppermute x0 -> x31, starting transfers between devices: none -> 52.8 us  [the longest x29 47.6 us: shift(): return lax.ppermute(x, axis, [(i, (i + step) % n) for i in range(n)])]
    ppermute x0 -> x31, waiting for transfers between devices: none -> 48.9 us  [the longest x29 47 us: shift(): return lax.ppermute(x, axis, [(i, (i + step) % n) for i in range(n)])]
    all_to_all x1 -> x0, blocking collectives: 9.09 us -> none  [per_device(): lax.all_to_all(reduced.reshape(lax.axis_size('egrp'), row_count, width_de...]
    unnamed x14 -> x32, local copies, waits for them, and re-layouts: 1.31 us -> 9.59 us
    dot_general x3 -> x5, matrix products: 12.5 us -> 11.8 us  [the longest x2 6.32 us: project(): part = jnp.einsum('edf,rd->efr', weight, scaled, preferred_element_type=f32)]
  transfers between devices with their start and end apart: 3 -> 31, of which waited for: 2 -> 19; matrix products, arithmetic and copies ran while one was open for 0% -> 8% of each run, Pallas kernels for 0% -> 0%
where the time goes in v1:
time: 146 us; the launch traced here: 144 us
  starting transfers between devices  52.8 us (36%)
  waiting for transfers between devices  48.9 us (33%)
  matrix products  15.2 us (10%)
  local copies, waits for them, and re-layouts  13.3 us (9%)
  other arithmetic  12.6 us (9%)
    ppermute x29, starting transfers between devices, shift(): return lax.ppermute(x, axis, [(i, (i + step) % n) for i in range(n)])  47.6 us
    ppermute x29, waiting for transfers between devices, shift(): return lax.ppermute(x, axis, [(i, (i + step) % n) for i in range(n)])  47 us
    unnamed x32, local copies, waits for them, and re-layouts  9.59 us
    dot_general x2, matrix products, project(): part = jnp.einsum('edf,rd->efr', weight, scaled, preferred_element_type=f32)  6.32 us
    ppermute x2, starting transfers between devices, swap_core(): lax.ppermute(x, 'attn', [(i, i ^ 1) for i in range(lax.axis_size('attn'))])  5.26 us
  transfers between devices with their start and end apart: 31, of which 19 were waited for; matrix products, arithmetic and copies ran while one was open for 8% of the time, Pallas kernels for 0%

profile of v1, /device:TPU:1, one launch (start us, length us, event | category | flops | bytes accessed | tf_op | source)
XLA Modules:
  0.0 143.7 jit_solution(8667561946678502315)
XLA Ops:
  0.6 0.8 reduce_sum.46
  2.9 1.4 fusion.17
  4.5 2.0 %fusion.23 = f32[8,2,6,128]{3,2,1,0:T(8,128)S(1)} fusion(f32[8,2,6]{2,1,0:T(2,128)S(1)} %fusion.69, f32[8,2,6,512]{3,2,1,0:T(8,128)S(1)} %fusion.17, bf16[8,512,256]{2,1,0:T(8,128)(2,1)} %param.13), kind=kOutput, calls=%fused_computation.34 | convolution fusion | flops 12755551 | bytes 2343296 | tf_op jit(solution)/shard_map/rhgl,rlhd->rhgd/dot_general | solution.py:33
  7.4 6.4 %collective-permute-start = (bf16[8,1664]{1,0:T(8,128)(2,1)S(1)}, bf16[8,1664]{1,0:T(8,128)(2,1)S(1)}, u32[]{:S(2)}, u32[]{:S(2)}) collective-permute-start(bf16[8,1664]{1,0:T(8,128)(2,1)S(1)} %get-tuple-element.52), channel_id=1, source_target_pairs={{0,224},{16,240},{32,0},{48,16},{64,32},{80,48},{96,64},{112,80},{... | collective-permute-start | bytes 79880 | tf_op jit(solution)/shard_map/ppermute | solution.py:41
  13.8 2.8 %collective-permute-start.4 = (bf16[8,1664]{1,0:T(8,128)(2,1)S(1)}, bf16[8,1664]{1,0:T(8,128)(2,1)S(1)}, u32[]{:S(2)}, u32[]{:S(2)}) collective-permute-start(bf16[8,1664]{1,0:T(8,128)(2,1)S(1)} %get-tuple-element.52), channel_id=1, source_target_pairs={{0,96},{16,112},{32,128},{48,144},{64,160},{80,176},{96,192},{112,... | collective-permute-start | bytes 79880 | tf_op jit(solution)/shard_map/ppermute | solution.py:41
  16.6 0.9 collective-permute-start.3
  17.5 4.0 %collective-permute-start.2 = (bf16[8,1664]{1,0:T(8,128)(2,1)S(1)}, bf16[8,1664]{1,0:T(8,128)(2,1)S(1)}, u32[]{:S(2)}, u32[]{:S(2)}) collective-permute-start(bf16[8,1664]{1,0:T(8,128)(2,1)S(1)} %get-tuple-element.52), channel_id=1, source_target_pairs={{0,160},{16,176},{32,192},{48,208},{64,224},{80,240},{96,0},{112,1... | collective-permute-start | bytes 79880 | tf_op jit(solution)/shard_map/ppermute | solution.py:41
  21.5 1.7 %collective-permute-start.1 = (bf16[8,1664]{1,0:T(8,128)(2,1)S(1)}, bf16[8,1664]{1,0:T(8,128)(2,1)S(1)}, u32[]{:S(2)}, u32[]{:S(2)}) collective-permute-start(bf16[8,1664]{1,0:T(8,128)(2,1)S(1)} %get-tuple-element.52), channel_id=1, source_target_pairs={{0,192},{16,208},{32,224},{48,240},{64,0},{80,16},{96,32},{112,48}... | collective-permute-start | bytes 79880 | tf_op jit(solution)/shard_map/ppermute | solution.py:41
  23.8 2.4 %collective-permute-done.1 = bf16[8,1664]{1,0:T(8,128)(2,1)S(1)} collective-permute-done((bf16[8,1664]{1,0:T(8,128)(2,1)S(1)}, bf16[8,1664]{1,0:T(8,128)(2,1)S(1)}, u32[]{:S(2)}, u32[]{:S(2)}) %collective-permute-start.1) | collective-permute-done | bytes 26656 | tf_op jit(solution)/shard_map/ppermute | solution.py:41
  30.8 2.5 %collective-permute-start.7 = (bf16[64,1664]{1,0:T(8,128)(2,1)S(1)}, bf16[64,1664]{1,0:T(8,128)(2,1)S(1)}, u32[]{:S(2)}, u32[]{:S(2)}) collective-permute-start(bf16[64,1664]{1,0:T(8,128)(2,1)S(1)} %get-tuple-element.31), channel_id=1, source_target_pairs={{0,12},{4,0},{8,4},{12,8},{1,13},{5,1},{9,5},{13,9},{2,14},{6,2},{... | collective-permute-start | bytes 638984 | tf_op jit(solution)/shard_map/ppermute | solution.py:41
  33.3 1.7 %collective-permute-start.8 = (bf16[64,1664]{1,0:T(8,128)(2,1)S(1)}, bf16[64,1664]{1,0:T(8,128)(2,1)S(1)}, u32[]{:S(2)}, u32[]{:S(2)}) collective-permute-start(bf16[64,1664]{1,0:T(8,128)(2,1)S(1)} %get-tuple-element.31), channel_id=1, source_target_pairs={{0,8},{4,12},{8,0},{12,4},{1,9},{5,13},{9,1},{13,5},{2,10},{6,14},... | collective-permute-start | bytes 638984 | tf_op jit(solution)/shard_map/ppermute | solution.py:41
  35.0 1.1 collective-permute-done.7
  36.9 4.1 %collective-permute-done.8 = bf16[64,1664]{1,0:T(8,128)(2,1)S(1)} collective-permute-done((bf16[64,1664]{1,0:T(8,128)(2,1)S(1)}, bf16[64,1664]{1,0:T(8,128)(2,1)S(1)}, u32[]{:S(2)}, u32[]{:S(2)}) %collective-permute-start.8) | collective-permute-done | bytes 213024 | tf_op jit(solution)/shard_map/ppermute | solution.py:41
  42.9 4.6 %collective-permute-start.10 = (bf16[256,1664]{1,0:T(8,128)(2,1)}, bf16[256,1664]{1,0:T(8,128)(2,1)S(1)}, u32[]{:S(2)}, u32[]{:S(2)}) collective-permute-start(bf16[256,1664]{1,0:T(8,128)(2,1)} %get-tuple-element.16), channel_id=1, source_target_pairs={{0,16},{16,0},{32,48},{48,32},{64,80},{80,64},{96,112},{112,96},{1... | collective-permute-start | bytes 2555912 | tf_op jit(solution)/shard_map/ppermute | solution.py:45
  48.3 2.2 %convolution_bitcast_fusion.4 = f32[2,336,8]{1,2,0:T(8,128)S(1)} fusion(bf16[2,1536,336]{1,2,0:T(8,128)(2,1)} %param.19, bf16[1536]{0:T(1024)(128)(2,1)S(1)} %get-tuple-element.9), kind=kOutput, calls=%fused_computation.36 | convolution fusion | flops 16515072 | bytes 2088960 | tf_op jit(solution)/shard_map/edf,rd->efr/dot_general | solution.py:94
  50.5 1.0 constant_dynamic-update-slice_fusion.19
  51.6 1.8 %convert_reduce_fusion = f32[512]{0:T(512)S(1)} fusion(bf16[512,1664]{1,0:T(8,128)(2,1)} %constant_dynamic-update-slice_fusion.19), kind=kLoop, calls=%fused_computation.10 | loop fusion | flops 1572352 | bytes 1574912 | tf_op jit(solution)/shard_map/reduce_sum | solution.py:79
  53.4 2.0 %fusion.4 = f32[512]{0:T(512)S(1)} fusion(f32[512]{0:T(512)S(1)} %broadcast_multiply_fusion, bf16[512,1664]{1,0:T(8,128)(2,1)} %constant_dynamic-update-slice_fusion.19), kind=kLoop, calls=%fused_computation.15 | loop fusion | flops 3145216 | bytes 1576960 | tf_op jit(solution)/shard_map/reduce_sum | solution.py:81
  55.4 2.8 %collective-permute-start.13 = (f32[2,512]{1,0:T(2,128)S(1)}, f32[2,512]{1,0:T(2,128)S(1)}, u32[]{:S(2)}, u32[]{:S(2)}) collective-permute-start(f32[2,512]{1,0:T(2,128)S(1)} %pad_maximum_fusion), channel_id=1, source_target_pairs={{0,3},{1,0},{2,1},{3,2},{4,7},{5,4},{6,5},{7,6},{8,11},{9,8},{10,9... | collective-permute-start | bytes 12296 | tf_op jit(solution)/shard_map/ppermute | solution.py:41
  60.1 2.9 %collective-permute-done.12 = f32[2,512]{1,0:T(2,128)S(1)} collective-permute-done((f32[2,512]{1,0:T(2,128)S(1)}, f32[2,512]{1,0:T(2,128)S(1)}, u32[]{:S(2)}, u32[]{:S(2)}) %collective-permute-start.12) | collective-permute-done | bytes 4128 | tf_op jit(solution)/shard_map/ppermute | solution.py:41
  63.1 3.5 %multiply_bitcast_fusion = f32[1,2,336,512]{3,2,1,0:T(8,128)S(1)} fusion(bf16[2,1536,336]{1,2,0:T(8,128)(2,1)} %param.20, f32[1536]{0:T(1024)S(1)} %get-tuple-element.8, f32[512]{0:T(512)S(1)} %broadcast_multiply_fusion, bf16[512,1664]{1,0:T(8,128)(2,1)} %constant_dynamic-update-slice_fusion.19, f32[2,336]{1,0:T(2,128)S(1)} %bitcast.92, ...), kind=kOutput, calls=%fused_computation.27 | convolution fusion | flops 1061142528 | bytes 5028480 | tf_op jit(solution)/shard_map/edf,rd->efr/dot_general | solution.py:93
  66.6 2.8 %multiply_bitcast_fusion.1 = f32[1,2,336,512]{3,2,1,0:T(8,128)S(1)} fusion(bf16[2,1536,336]{1,2,0:T(8,128)(2,1)S(1)} %copy-done.4, f32[1536]{0:T(1024)S(1)} %get-tuple-element.8, f32[512]{0:T(512)S(1)} %broadcast_multiply_fusion, bf16[512,1664]{1,0:T(8,128)(2,1)} %constant_dynamic-update-slice_fusion.19, f32[512]{0:T(512)S(1)} %get-tuple-element.55, ...), kind=kOutput, calls=%fused_computation.28 | convolution fusion | flops 1061142528 | bytes 5028480 | tf_op jit(solution)/shard_map/edf,rd->efr/dot_general | solution.py:93
  69.4 1.5 %fusion.35 = (bf16[2,2,336,128]{3,2,1,0:T(8,128)(2,1)}, bf16[2,2,336,128]{3,2,1,0:T(8,128)(2,1)}, bf16[2,2,336,128]{3,2,1,0:T(8,128)(2,1)}) fusion(s32[]{:T(128)S(6)} %select_n.36, f32[1,2,336,512]{3,2,1,0:T(8,128)S(1)} %multiply_bitcast_fusion.1, f32[1,2,336,512]{3,2,1,0:T(8,128)S(1)} %multiply_bitcast_fusion, s32[]{:T(128)S(6)} %select_n.37, s32[]{:T(128)S(6)} %select_n.38), kind=kLoop, calls=%fused_computation.44 | loop fusion | flops 2064384 | bytes 3784716 | tf_op jit(solution)/shard_map/convert_element_type | solution.py:106
  70.9 1.7 %collective-permute-start.15 = (bf16[2,2,336,128]{3,2,1,0:T(8,128)(2,1)}, bf16[2,2,336,128]{3,2,1,0:T(8,128)(2,1)}, u32[]{:S(2)}, u32[]{:S(2)}) collective-permute-start(bf16[2,2,336,128]{3,2,1,0:T(8,128)(2,1)} %get-tuple-element.11), channel_id=1, source_target_pairs={{0,2},{1,3},{2,0},{3,1},{4,6},{5,7},{6,4},{7,5},{8,10},{9,11},{10,... | collective-permute-start | bytes 1032200 | tf_op jit(solution)/shard_map/ppermute | solution.py:41
  72.7 1.7 %collective-permute-start.16 = (bf16[2,2,336,128]{3,2,1,0:T(8,128)(2,1)}, bf16[2,2,336,128]{3,2,1,0:T(8,128)(2,1)}, u32[]{:S(2)}, u32[]{:S(2)}) collective-permute-start(bf16[2,2,336,128]{3,2,1,0:T(8,128)(2,1)} %get-tuple-element.12), channel_id=1, source_target_pairs={{0,3},{1,0},{2,1},{3,2},{4,7},{5,4},{6,5},{7,6},{8,11},{9,8},{10,9... | collective-permute-start | bytes 1032200 | tf_op jit(solution)/shard_map/ppermute | solution.py:41
  74.4 0.9 slice.129
  75.5 5.3 %collective-permute-done.14 = bf16[2,2,336,128]{3,2,1,0:T(8,128)(2,1)} collective-permute-done((bf16[2,2,336,128]{3,2,1,0:T(8,128)(2,1)}, bf16[2,2,336,128]{3,2,1,0:T(8,128)(2,1)}, u32[]{:S(2)}, u32[]{:S(2)}) %collective-permute-start.14) | collective-permute-done | bytes 344096 | tf_op jit(solution)/shard_map/ppermute | solution.py:41
  80.8 6.4 %collective-permute-done.15 = bf16[2,2,336,128]{3,2,1,0:T(8,128)(2,1)} collective-permute-done((bf16[2,2,336,128]{3,2,1,0:T(8,128)(2,1)}, bf16[2,2,336,128]{3,2,1,0:T(8,128)(2,1)}, u32[]{:S(2)}, u32[]{:S(2)}) %collective-permute-start.15) | collective-permute-done | bytes 344096 | tf_op jit(solution)/shard_map/ppermute | solution.py:41
  87.2 2.2 %collective-permute-done.16 = bf16[2,2,336,128]{3,2,1,0:T(8,128)(2,1)} collective-permute-done((bf16[2,2,336,128]{3,2,1,0:T(8,128)(2,1)}, bf16[2,2,336,128]{3,2,1,0:T(8,128)(2,1)}, u32[]{:S(2)}, u32[]{:S(2)}) %collective-permute-start.16) | collective-permute-done | bytes 344096 | tf_op jit(solution)/shard_map/ppermute | solution.py:41
  89.4 1.4 fusion.33
  90.8 0.8 constant_dynamic-update-slice_fusion.37
  91.6 3.4 %collective-permute-start.17 = (bf16[2,336,128]{2,1,0:T(8,128)(2,1)S(1)}, bf16[2,336,128]{2,1,0:T(8,128)(2,1)S(1)}, u32[]{:S(2)}, u32[]{:S(2)}) collective-permute-start(bf16[2,336,128]{2,1,0:T(8,128)(2,1)S(1)} %get-tuple-element.7), channel_id=1, source_target_pairs={{0,3},{1,0},{2,1},{3,2},{4,7},{5,4},{6,5},{7,6},{8,11},{9,8},{10,9... | collective-permute-start | bytes 516104 | tf_op jit(solution)/shard_map/ppermute | solution.py:41
  95.6 6.5 %collective-permute-done.17 = bf16[2,336,128]{2,1,0:T(8,128)(2,1)S(1)} collective-permute-done((bf16[2,336,128]{2,1,0:T(8,128)(2,1)S(1)}, bf16[2,336,128]{2,1,0:T(8,128)(2,1)S(1)}, u32[]{:S(2)}, u32[]{:S(2)}) %collective-permute-start.17) | collective-permute-done | bytes 172064 | tf_op jit(solution)/shard_map/ppermute | solution.py:41
  103.6 2.7 %collective-permute-done.19 = bf16[2,336,128]{2,1,0:T(8,128)(2,1)S(1)} collective-permute-done((bf16[2,336,128]{2,1,0:T(8,128)(2,1)S(1)}, bf16[2,336,128]{2,1,0:T(8,128)(2,1)S(1)}, u32[]{:S(2)}, u32[]{:S(2)}) %collective-permute-start.19) | collective-permute-done | bytes 172064 | tf_op jit(solution)/shard_map/ppermute | solution.py:41
  109.1 2.5 %convolution_bitcast_fusion = f32[512,1536]{1,0:T(8,128)S(1)} fusion(bf16[2,336,1536]{2,1,0:T(8,128)(2,1)S(1)} %copy-done.2, bf16[2,336,896]{2,1,0:T(8,128)(2,1)} %constant_dynamic-update-slice_fusion.31, s32[]{:T(128)S(6)} %select_n.41), kind=kOutput, calls=%fused_computation.13 | convolution fusion | flops 1056964608 | bytes 5898244 | tf_op jit(solution)/shard_map/efr,efd->rd/dot_general | solution.py:116
  112.4 1.9 %collective-permute-done.20 = bf16[256,1536]{1,0:T(8,128)(2,1)S(1)} collective-permute-done((bf16[256,1536]{1,0:T(8,128)(2,1)S(1)}, bf16[256,1536]{1,0:T(8,128)(2,1)S(1)}, u32[]{:S(2)}, u32[]{:S(2)}) %collective-permute-start.20) | collective-permute-done | bytes 786464 | tf_op jit(solution)/shard_map/ppermute | solution.py:45
  114.8 2.8 %collective-permute-start.23 = (bf16[64,1536]{1,0:T(8,128)(2,1)S(1)}, bf16[64,1536]{1,0:T(8,128)(2,1)S(1)}, u32[]{:S(2)}, u32[]{:S(2)}) collective-permute-start(bf16[64,1536]{1,0:T(8,128)(2,1)S(1)} %get-tuple-element.14), channel_id=1, source_target_pairs={{0,12},{4,0},{8,4},{12,8},{1,13},{5,1},{9,5},{13,9},{2,14},{6,2},{... | collective-permute-start | bytes 589832 | tf_op jit(solution)/shard_map/ppermute | solution.py:41
  117.5 1.1 collective-permute-start.22
  118.6 3.5 %collective-permute-done.21 = bf16[64,1536]{1,0:T(8,128)(2,1)S(1)} collective-permute-done((bf16[64,1536]{1,0:T(8,128)(2,1)S(1)}, bf16[64,1536]{1,0:T(8,128)(2,1)S(1)}, u32[]{:S(2)}, u32[]{:S(2)}) %collective-permute-start.21) | collective-permute-done | bytes 196640 | tf_op jit(solution)/shard_map/ppermute | solution.py:41
  122.1 3.2 %collective-permute-done.23 = bf16[64,1536]{1,0:T(8,128)(2,1)S(1)} collective-permute-done((bf16[64,1536]{1,0:T(8,128)(2,1)S(1)}, bf16[64,1536]{1,0:T(8,128)(2,1)S(1)}, u32[]{:S(2)}, u32[]{:S(2)}) %collective-permute-start.23) | collective-permute-done | bytes 196640 | tf_op jit(solution)/shard_map/ppermute | solution.py:41
  125.3 2.2 %collective-permute-done.22 = bf16[64,1536]{1,0:T(8,128)(2,1)S(1)} collective-permute-done((bf16[64,1536]{1,0:T(8,128)(2,1)S(1)}, bf16[64,1536]{1,0:T(8,128)(2,1)S(1)}, u32[]{:S(2)}, u32[]{:S(2)}) %collective-permute-start.22) | collective-permute-done | bytes 196640 | tf_op jit(solution)/shard_map/ppermute | solution.py:41
  127.6 2.2 %collective-permute-start.24 = (bf16[8,1536]{1,0:T(8,128)(2,1)S(1)}, bf16[8,1536]{1,0:T(8,128)(2,1)S(1)}, u32[]{:S(2)}, u32[]{:S(2)}) collective-permute-start(bf16[8,1536]{1,0:T(8,128)(2,1)S(1)} %get-tuple-element.22), channel_id=1, source_target_pairs={{0,32},{16,48},{32,64},{48,80},{64,96},{80,112},{96,128},{112,144}... | collective-permute-start | bytes 73736 | tf_op jit(solution)/shard_map/ppermute | solution.py:41
  131.2 2.5 %collective-permute-start.28 = (bf16[8,1536]{1,0:T(8,128)(2,1)S(1)}, bf16[8,1536]{1,0:T(8,128)(2,1)S(1)}, u32[]{:S(2)}, u32[]{:S(2)}) collective-permute-start(bf16[8,1536]{1,0:T(8,128)(2,1)S(1)} %get-tuple-element.25), channel_id=1, source_target_pairs={{0,160},{16,176},{32,192},{48,208},{64,224},{80,240},{96,0},{112,1... | collective-permute-start | bytes 73736 | tf_op jit(solution)/shard_map/ppermute | solution.py:41
  133.7 2.3 %collective-permute-start.27 = (bf16[8,1536]{1,0:T(8,128)(2,1)S(1)}, bf16[8,1536]{1,0:T(8,128)(2,1)S(1)}, u32[]{:S(2)}, u32[]{:S(2)}) collective-permute-start(bf16[8,1536]{1,0:T(8,128)(2,1)S(1)} %get-tuple-element.26), channel_id=1, source_target_pairs={{0,128},{16,144},{32,160},{48,176},{64,192},{80,208},{96,224},{112... | collective-permute-start | bytes 73736 | tf_op jit(solution)/shard_map/ppermute | solution.py:41
  136.0 1.9 %collective-permute-start.26 = (bf16[8,1536]{1,0:T(8,128)(2,1)S(1)}, bf16[8,1536]{1,0:T(8,128)(2,1)S(1)}, u32[]{:S(2)}, u32[]{:S(2)}) collective-permute-start(bf16[8,1536]{1,0:T(8,128)(2,1)S(1)} %get-tuple-element.27), channel_id=1, source_target_pairs={{0,96},{16,112},{32,128},{48,144},{64,160},{80,176},{96,192},{112,... | collective-permute-start | bytes 73736 | tf_op jit(solution)/shard_map/ppermute | solution.py:41
  137.9 1.8 %collective-permute-start.25 = (bf16[8,1536]{1,0:T(8,128)(2,1)S(1)}, bf16[8,1536]{1,0:T(8,128)(2,1)S(1)}, u32[]{:S(2)}, u32[]{:S(2)}) collective-permute-start(bf16[8,1536]{1,0:T(8,128)(2,1)S(1)} %get-tuple-element.28), channel_id=1, source_target_pairs={{0,64},{16,80},{32,96},{48,112},{64,128},{80,144},{96,160},{112,17... | collective-permute-start | bytes 73736 | tf_op jit(solution)/shard_map/ppermute | solution.py:41
  140.3 1.6 %collective-permute-done.26 = bf16[8,1536]{1,0:T(8,128)(2,1)S(1)} collective-permute-done((bf16[8,1536]{1,0:T(8,128)(2,1)S(1)}, bf16[8,1536]{1,0:T(8,128)(2,1)S(1)}, u32[]{:S(2)}, u32[]{:S(2)}) %collective-permute-start.26) | collective-permute-done | bytes 24608 | tf_op jit(solution)/shard_map/ppermute | solution.py:41
  141.9 1.2 collective-permute-done.25
  (87 shorter events, 21.9 us)
Async XLA Ops:
  0.6 2.3 %copy-start = (bf16[8,512,256]{2,1,0:T(8,128)(2,1)S(1)}, bf16[8,512,256]{2,1,0:T(8,128)(2,1)}, u32[]{:S(2)}) copy-start(bf16[8,512,256]{2,1,0:T(8,128)(2,1)} %param.12) | copy-start | bytes 6291460
  4.5 2.1 %copy-start.7 = (s32[8,4]{0,1:T(4,128)S(1)}, s32[8,4]{0,1:T(4,128)}, u32[]{:S(2)}) copy-start(s32[8,4]{0,1:T(4,128)} %param.17) | copy-start | bytes 388
  4.5 2.2 %copy-start.6 = (bf16[8,1536]{1,0:T(8,128)(2,1)S(1)}, bf16[8,1536]{1,0:T(8,128)(2,1)}, u32[]{:S(2)}) copy-start(bf16[8,1536]{1,0:T(8,128)(2,1)} %param.15) | copy-start | bytes 73732
  6.7 29.3 %copy-start.5 = (bf16[8,1536]{1,0:T(8,128)(2,1)}, bf16[8,1536]{1,0:T(8,128)(2,1)S(1)}, u32[]{:S(2)}) copy-start(bf16[8,1536]{1,0:T(8,128)(2,1)S(1)} %add_convert_fusion) | copy-start | bytes 73732
  7.4 14.1 %collective-permute-start = (bf16[8,1664]{1,0:T(8,128)(2,1)S(1)}, bf16[8,1664]{1,0:T(8,128)(2,1)S(1)}, u32[]{:S(2)}, u32[]{:S(2)}) collective-permute-start(bf16[8,1664]{1,0:T(8,128)(2,1)S(1)} %get-tuple-element.52), channel_id=1, source_target_pairs={{0,224},{16,240},{32,0},{48,16},{64,32},{80,48},{96,64},{112,80},{... | collective-permute-start | bytes 79880 | tf_op jit(solution)/shard_map/ppermute | solution.py:41
  13.8 15.2 %collective-permute-start.5 = (bf16[8,1664]{1,0:T(8,128)(2,1)S(1)}, bf16[8,1664]{1,0:T(8,128)(2,1)S(1)}, u32[]{:S(2)}, u32[]{:S(2)}) collective-permute-start(bf16[8,1664]{1,0:T(8,128)(2,1)S(1)} %get-tuple-element.52), channel_id=1, source_target_pairs={{0,64},{16,80},{32,96},{48,112},{64,128},{80,144},{96,160},{112,17... | collective-permute-start | bytes 79880 | tf_op jit(solution)/shard_map/ppermute | solution.py:41
  13.8 14.5 %collective-permute-start.4 = (bf16[8,1664]{1,0:T(8,128)(2,1)S(1)}, bf16[8,1664]{1,0:T(8,128)(2,1)S(1)}, u32[]{:S(2)}, u32[]{:S(2)}) collective-permute-start(bf16[8,1664]{1,0:T(8,128)(2,1)S(1)} %get-tuple-element.52), channel_id=1, source_target_pairs={{0,96},{16,112},{32,128},{48,144},{64,160},{80,176},{96,192},{112,... | collective-permute-start | bytes 79880 | tf_op jit(solution)/shard_map/ppermute | solution.py:41
  16.6 11.1 %collective-permute-start.3 = (bf16[8,1664]{1,0:T(8,128)(2,1)S(1)}, bf16[8,1664]{1,0:T(8,128)(2,1)S(1)}, u32[]{:S(2)}, u32[]{:S(2)}) collective-permute-start(bf16[8,1664]{1,0:T(8,128)(2,1)S(1)} %get-tuple-element.52), channel_id=1, source_target_pairs={{0,128},{16,144},{32,160},{48,176},{64,192},{80,208},{96,224},{112... | collective-permute-start | bytes 79880 | tf_op jit(solution)/shard_map/ppermute | solution.py:41
  17.5 9.6 %collective-permute-start.2 = (bf16[8,1664]{1,0:T(8,128)(2,1)S(1)}, bf16[8,1664]{1,0:T(8,128)(2,1)S(1)}, u32[]{:S(2)}, u32[]{:S(2)}) collective-permute-start(bf16[8,1664]{1,0:T(8,128)(2,1)S(1)} %get-tuple-element.52), channel_id=1, source_target_pairs={{0,160},{16,176},{32,192},{48,208},{64,224},{80,240},{96,0},{112,1... | collective-permute-start | bytes 79880 | tf_op jit(solution)/shard_map/ppermute | solution.py:41
  21.5 4.7 %collective-permute-start.1 = (bf16[8,1664]{1,0:T(8,128)(2,1)S(1)}, bf16[8,1664]{1,0:T(8,128)(2,1)S(1)}, u32[]{:S(2)}, u32[]{:S(2)}) collective-permute-start(bf16[8,1664]{1,0:T(8,128)(2,1)S(1)} %get-tuple-element.52), channel_id=1, source_target_pairs={{0,192},{16,208},{32,224},{48,240},{64,0},{80,16},{96,32},{112,48}... | collective-permute-start | bytes 79880 | tf_op jit(solution)/shard_map/ppermute | solution.py:41
  26.3 3.9 %collective-permute-start.6 = (bf16[8,1664]{1,0:T(8,128)(2,1)S(1)}, bf16[8,1664]{1,0:T(8,128)(2,1)S(1)}, u32[]{:S(2)}, u32[]{:S(2)}) collective-permute-start(bf16[8,1664]{1,0:T(8,128)(2,1)S(1)} %get-tuple-element.52), channel_id=1, source_target_pairs={{0,32},{16,48},{32,64},{48,80},{64,96},{80,112},{96,128},{112,144}... | collective-permute-start | bytes 79880 | tf_op jit(solution)/shard_map/ppermute | solution.py:41
  30.8 5.3 %collective-permute-start.7 = (bf16[64,1664]{1,0:T(8,128)(2,1)S(1)}, bf16[64,1664]{1,0:T(8,128)(2,1)S(1)}, u32[]{:S(2)}, u32[]{:S(2)}) collective-permute-start(bf16[64,1664]{1,0:T(8,128)(2,1)S(1)} %get-tuple-element.31), channel_id=1, source_target_pairs={{0,12},{4,0},{8,4},{12,8},{1,13},{5,1},{9,5},{13,9},{2,14},{6,2},{... | collective-permute-start | bytes 638984 | tf_op jit(solution)/shard_map/ppermute | solution.py:41
  33.3 8.9 %collective-permute-start.9 = (bf16[64,1664]{1,0:T(8,128)(2,1)S(1)}, bf16[64,1664]{1,0:T(8,128)(2,1)S(1)}, u32[]{:S(2)}, u32[]{:S(2)}) collective-permute-start(bf16[64,1664]{1,0:T(8,128)(2,1)S(1)} %get-tuple-element.31), channel_id=1, source_target_pairs={{0,4},{4,8},{8,12},{12,0},{1,5},{5,9},{9,13},{13,1},{2,6},{6,10},{... | collective-permute-start | bytes 638984 | tf_op jit(solution)/shard_map/ppermute | solution.py:41
  33.3 7.7 %collective-permute-start.8 = (bf16[64,1664]{1,0:T(8,128)(2,1)S(1)}, bf16[64,1664]{1,0:T(8,128)(2,1)S(1)}, u32[]{:S(2)}, u32[]{:S(2)}) collective-permute-start(bf16[64,1664]{1,0:T(8,128)(2,1)S(1)} %get-tuple-element.31), channel_id=1, source_target_pairs={{0,8},{4,12},{8,0},{12,4},{1,9},{5,13},{9,1},{13,5},{2,10},{6,14},... | collective-permute-start | bytes 638984 | tf_op jit(solution)/shard_map/ppermute | solution.py:41
  42.9 7.6 %collective-permute-start.10 = (bf16[256,1664]{1,0:T(8,128)(2,1)}, bf16[256,1664]{1,0:T(8,128)(2,1)S(1)}, u32[]{:S(2)}, u32[]{:S(2)}) collective-permute-start(bf16[256,1664]{1,0:T(8,128)(2,1)} %get-tuple-element.16), channel_id=1, source_target_pairs={{0,16},{16,0},{32,48},{48,32},{64,80},{80,64},{96,112},{112,96},{1... | collective-permute-start | bytes 2555912 | tf_op jit(solution)/shard_map/ppermute | solution.py:45
  51.6 6.6 %copy-start.3 = (bf16[2,1536,336]{1,2,0:T(8,128)(2,1)S(1)}, bf16[2,1536,336]{1,2,0:T(8,128)(2,1)}, u32[]{:S(2)}) copy-start(bf16[2,1536,336]{1,2,0:T(8,128)(2,1)} %param.20) | copy-start | bytes 6193156
  55.4 4.7 %collective-permute-start.13 = (f32[2,512]{1,0:T(2,128)S(1)}, f32[2,512]{1,0:T(2,128)S(1)}, u32[]{:S(2)}, u32[]{:S(2)}) collective-permute-start(f32[2,512]{1,0:T(2,128)S(1)} %pad_maximum_fusion), channel_id=1, source_target_pairs={{0,3},{1,0},{2,1},{3,2},{4,7},{5,4},{6,5},{7,6},{8,11},{9,8},{10,9... | collective-permute-start | bytes 12296 | tf_op jit(solution)/shard_map/ppermute | solution.py:41
  58.9 4.0 %collective-permute-start.12 = (f32[2,512]{1,0:T(2,128)S(1)}, f32[2,512]{1,0:T(2,128)S(1)}, u32[]{:S(2)}, u32[]{:S(2)}) collective-permute-start(f32[2,512]{1,0:T(2,128)S(1)} %pad_maximum_fusion), channel_id=1, source_target_pairs={{0,2},{1,3},{2,0},{3,1},{4,6},{5,7},{6,4},{7,5},{8,10},{9,11},{10,... | collective-permute-start | bytes 12296 | tf_op jit(solution)/shard_map/ppermute | solution.py:41
  59.4 3.7 %collective-permute-start.11 = (f32[2,512]{1,0:T(2,128)S(1)}, f32[2,512]{1,0:T(2,128)S(1)}, u32[]{:S(2)}, u32[]{:S(2)}) collective-permute-start(f32[2,512]{1,0:T(2,128)S(1)} %pad_maximum_fusion), channel_id=1, source_target_pairs={{0,1},{1,2},{2,3},{3,0},{4,5},{5,6},{6,7},{7,4},{8,9},{9,10},{10,1... | collective-permute-start | bytes 12296 | tf_op jit(solution)/shard_map/ppermute | solution.py:41
  63.1 3.6 %copy-start.4 = (bf16[2,1536,336]{1,2,0:T(8,128)(2,1)S(1)}, bf16[2,1536,336]{1,2,0:T(8,128)(2,1)}, u32[]{:S(2)}) copy-start(bf16[2,1536,336]{1,2,0:T(8,128)(2,1)} %param.19) | copy-start | bytes 6193156
  69.4 1.5 %copy-start.1 = (f32[1,2,336,512]{3,2,1,0:T(8,128)}, f32[1,2,336,512]{3,2,1,0:T(8,128)S(1)}, u32[]{:S(2)}) copy-start(f32[1,2,336,512]{3,2,1,0:T(8,128)S(1)} %multiply_bitcast_fusion.1) | copy-start | bytes 4128772
  70.9 9.9 %collective-permute-start.14 = (bf16[2,2,336,128]{3,2,1,0:T(8,128)(2,1)}, bf16[2,2,336,128]{3,2,1,0:T(8,128)(2,1)}, u32[]{:S(2)}, u32[]{:S(2)}) collective-permute-start(bf16[2,2,336,128]{3,2,1,0:T(8,128)(2,1)} %get-tuple-element.10), channel_id=1, source_target_pairs={{0,1},{1,2},{2,3},{3,0},{4,5},{5,6},{6,7},{7,4},{8,9},{9,10},{10,1... | collective-permute-start | bytes 1032200 | tf_op jit(solution)/shard_map/ppermute | solution.py:41
  70.9 16.3 %collective-permute-start.15 = (bf16[2,2,336,128]{3,2,1,0:T(8,128)(2,1)}, bf16[2,2,336,128]{3,2,1,0:T(8,128)(2,1)}, u32[]{:S(2)}, u32[]{:S(2)}) collective-permute-start(bf16[2,2,336,128]{3,2,1,0:T(8,128)(2,1)} %get-tuple-element.11), channel_id=1, source_target_pairs={{0,2},{1,3},{2,0},{3,1},{4,6},{5,7},{6,4},{7,5},{8,10},{9,11},{10,... | collective-permute-start | bytes 1032200 | tf_op jit(solution)/shard_map/ppermute | solution.py:41
  72.7 16.7 %collective-permute-start.16 = (bf16[2,2,336,128]{3,2,1,0:T(8,128)(2,1)}, bf16[2,2,336,128]{3,2,1,0:T(8,128)(2,1)}, u32[]{:S(2)}, u32[]{:S(2)}) collective-permute-start(bf16[2,2,336,128]{3,2,1,0:T(8,128)(2,1)} %get-tuple-element.12), channel_id=1, source_target_pairs={{0,3},{1,0},{2,1},{3,2},{4,7},{5,4},{6,5},{7,6},{8,11},{9,8},{10,9... | collective-permute-start | bytes 1032200 | tf_op jit(solution)/shard_map/ppermute | solution.py:41
  91.6 10.5 %collective-permute-start.17 = (bf16[2,336,128]{2,1,0:T(8,128)(2,1)S(1)}, bf16[2,336,128]{2,1,0:T(8,128)(2,1)S(1)}, u32[]{:S(2)}, u32[]{:S(2)}) collective-permute-start(bf16[2,336,128]{2,1,0:T(8,128)(2,1)S(1)} %get-tuple-element.7), channel_id=1, source_target_pairs={{0,3},{1,0},{2,1},{3,2},{4,7},{5,4},{6,5},{7,6},{8,11},{9,8},{10,9... | collective-permute-start | bytes 516104 | tf_op jit(solution)/shard_map/ppermute | solution.py:41
  95.0 7.8 %collective-permute-start.18 = (bf16[2,336,128]{2,1,0:T(8,128)(2,1)S(1)}, bf16[2,336,128]{2,1,0:T(8,128)(2,1)S(1)}, u32[]{:S(2)}, u32[]{:S(2)}) collective-permute-start(bf16[2,336,128]{2,1,0:T(8,128)(2,1)S(1)} %get-tuple-element.7), channel_id=1, source_target_pairs={{0,2},{1,3},{2,0},{3,1},{4,6},{5,7},{6,4},{7,5},{8,10},{9,11},{10,... | collective-permute-start | bytes 516104 | tf_op jit(solution)/shard_map/ppermute | solution.py:41
  95.2 13.9 %copy-start.2 = (bf16[2,336,1536]{2,1,0:T(8,128)(2,1)S(1)}, bf16[2,336,1536]{2,1,0:T(8,128)(2,1)}, u32[]{:S(2)}) copy-start(bf16[2,336,1536]{2,1,0:T(8,128)(2,1)} %param.21) | copy-start | bytes 6193156
  95.2 11.1 %collective-permute-start.19 = (bf16[2,336,128]{2,1,0:T(8,128)(2,1)S(1)}, bf16[2,336,128]{2,1,0:T(8,128)(2,1)S(1)}, u32[]{:S(2)}, u32[]{:S(2)}) collective-permute-start(bf16[2,336,128]{2,1,0:T(8,128)(2,1)S(1)} %get-tuple-element.7), channel_id=1, source_target_pairs={{0,1},{1,2},{2,3},{3,0},{4,5},{5,6},{6,7},{7,4},{8,9},{9,10},{10,1... | collective-permute-start | bytes 516104 | tf_op jit(solution)/shard_map/ppermute | solution.py:41
  111.8 2.6 %collective-permute-start.20 = (bf16[256,1536]{1,0:T(8,128)(2,1)S(1)}, bf16[256,1536]{1,0:T(8,128)(2,1)S(1)}, u32[]{:S(2)}, u32[]{:S(2)}) collective-permute-start(bf16[256,1536]{1,0:T(8,128)(2,1)S(1)} %slice.181), channel_id=1, source_target_pairs={{0,16},{16,0},{32,48},{48,32},{64,80},{80,64},{96,112},{112,96},{1... | collective-permute-start | bytes 2359304 | tf_op jit(solution)/shard_map/ppermute | solution.py:45
  114.7 7.4 %collective-permute-start.21 = (bf16[64,1536]{1,0:T(8,128)(2,1)S(1)}, bf16[64,1536]{1,0:T(8,128)(2,1)S(1)}, u32[]{:S(2)}, u32[]{:S(2)}) collective-permute-start(bf16[64,1536]{1,0:T(8,128)(2,1)S(1)} %get-tuple-element.13), channel_id=1, source_target_pairs={{0,4},{4,8},{8,12},{12,0},{1,5},{5,9},{9,13},{13,1},{2,6},{6,10},{... | collective-permute-start | bytes 589832 | tf_op jit(solution)/shard_map/ppermute | solution.py:41
  114.8 10.5 %collective-permute-start.23 = (bf16[64,1536]{1,0:T(8,128)(2,1)S(1)}, bf16[64,1536]{1,0:T(8,128)(2,1)S(1)}, u32[]{:S(2)}, u32[]{:S(2)}) collective-permute-start(bf16[64,1536]{1,0:T(8,128)(2,1)S(1)} %get-tuple-element.14), channel_id=1, source_target_pairs={{0,12},{4,0},{8,4},{12,8},{1,13},{5,1},{9,5},{13,9},{2,14},{6,2},{... | collective-permute-start | bytes 589832 | tf_op jit(solution)/shard_map/ppermute | solution.py:41
  117.5 10.0 %collective-permute-start.22 = (bf16[64,1536]{1,0:T(8,128)(2,1)S(1)}, bf16[64,1536]{1,0:T(8,128)(2,1)S(1)}, u32[]{:S(2)}, u32[]{:S(2)}) collective-permute-start(bf16[64,1536]{1,0:T(8,128)(2,1)S(1)} %get-tuple-element.15), channel_id=1, source_target_pairs={{0,8},{4,12},{8,0},{12,4},{1,9},{5,13},{9,1},{13,5},{2,10},{6,14},... | collective-permute-start | bytes 589832 | tf_op jit(solution)/shard_map/ppermute | solution.py:41
  127.6 8.4 %collective-permute-start.24 = (bf16[8,1536]{1,0:T(8,128)(2,1)S(1)}, bf16[8,1536]{1,0:T(8,128)(2,1)S(1)}, u32[]{:S(2)}, u32[]{:S(2)}) collective-permute-start(bf16[8,1536]{1,0:T(8,128)(2,1)S(1)} %get-tuple-element.22), channel_id=1, source_target_pairs={{0,32},{16,48},{32,64},{48,80},{64,96},{80,112},{96,128},{112,144}... | collective-permute-start | bytes 73736 | tf_op jit(solution)/shard_map/ppermute | solution.py:41
  129.8 8.1 %collective-permute-start.30 = (bf16[8,1536]{1,0:T(8,128)(2,1)S(1)}, bf16[8,1536]{1,0:T(8,128)(2,1)S(1)}, u32[]{:S(2)}, u32[]{:S(2)}) collective-permute-start(bf16[8,1536]{1,0:T(8,128)(2,1)S(1)} %get-tuple-element.23), channel_id=1, source_target_pairs={{0,224},{16,240},{32,0},{48,16},{64,32},{80,48},{96,64},{112,80},{... | collective-permute-start | bytes 73736 | tf_op jit(solution)/shard_map/ppermute | solution.py:41
  130.4 9.3 %collective-permute-start.29 = (bf16[8,1536]{1,0:T(8,128)(2,1)S(1)}, bf16[8,1536]{1,0:T(8,128)(2,1)S(1)}, u32[]{:S(2)}, u32[]{:S(2)}) collective-permute-start(bf16[8,1536]{1,0:T(8,128)(2,1)S(1)} %get-tuple-element.24), channel_id=1, source_target_pairs={{0,192},{16,208},{32,224},{48,240},{64,0},{80,16},{96,32},{112,48}... | collective-permute-start | bytes 73736 | tf_op jit(solution)/shard_map/ppermute | solution.py:41
  131.2 8.5 %collective-permute-start.28 = (bf16[8,1536]{1,0:T(8,128)(2,1)S(1)}, bf16[8,1536]{1,0:T(8,128)(2,1)S(1)}, u32[]{:S(2)}, u32[]{:S(2)}) collective-permute-start(bf16[8,1536]{1,0:T(8,128)(2,1)S(1)} %get-tuple-element.25), channel_id=1, source_target_pairs={{0,160},{16,176},{32,192},{48,208},{64,224},{80,240},{96,0},{112,1... | collective-permute-start | bytes 73736 | tf_op jit(solution)/shard_map/ppermute | solution.py:41
  133.7 6.6 %collective-permute-start.27 = (bf16[8,1536]{1,0:T(8,128)(2,1)S(1)}, bf16[8,1536]{1,0:T(8,128)(2,1)S(1)}, u32[]{:S(2)}, u32[]{:S(2)}) collective-permute-start(bf16[8,1536]{1,0:T(8,128)(2,1)S(1)} %get-tuple-element.26), channel_id=1, source_target_pairs={{0,128},{16,144},{32,160},{48,176},{64,192},{80,208},{96,224},{112... | collective-permute-start | bytes 73736 | tf_op jit(solution)/shard_map/ppermute | solution.py:41
  136.0 5.8 %collective-permute-start.26 = (bf16[8,1536]{1,0:T(8,128)(2,1)S(1)}, bf16[8,1536]{1,0:T(8,128)(2,1)S(1)}, u32[]{:S(2)}, u32[]{:S(2)}) collective-permute-start(bf16[8,1536]{1,0:T(8,128)(2,1)S(1)} %get-tuple-element.27), channel_id=1, source_target_pairs={{0,96},{16,112},{32,128},{48,144},{64,160},{80,176},{96,192},{112,... | collective-permute-start | bytes 73736 | tf_op jit(solution)/shard_map/ppermute | solution.py:41
  137.9 5.2 %collective-permute-start.25 = (bf16[8,1536]{1,0:T(8,128)(2,1)S(1)}, bf16[8,1536]{1,0:T(8,128)(2,1)S(1)}, u32[]{:S(2)}, u32[]{:S(2)}) collective-permute-start(bf16[8,1536]{1,0:T(8,128)(2,1)S(1)} %get-tuple-element.28), channel_id=1, source_target_pairs={{0,64},{16,80},{32,96},{48,112},{64,128},{80,144},{96,160},{112,17... | collective-permute-start | bytes 73736 | tf_op jit(solution)/shard_map/ppermute | solution.py:41

commit v2 on v0

v2 whole, which is shorter than its diff:
```python
import math

import jax
import jax.numpy as jnp
from jax import lax
from jax.experimental import pallas as pl
from jax.experimental.pallas import tpu as pltpu
from jax.sharding import PartitionSpec as P

HEAD_SIZE = 128
EXPERTS = 8

epsilon = 1e-05
f32, bf16 = jnp.float32, jnp.bfloat16


def attend(queries, cache_keys, stored_values, lengths):
    row_count = queries.shape[0]
    span = cache_keys.shape[1]
    kv_heads = cache_keys.shape[2] // HEAD_SIZE
    query_group = queries.shape[1] // (kv_heads * HEAD_SIZE)
    query_blocks = queries.reshape(row_count, kv_heads, query_group, HEAD_SIZE)
    key_blocks = cache_keys.reshape(row_count, span, kv_heads, HEAD_SIZE)
    value_blocks = stored_values.reshape(row_count, span, kv_heads, HEAD_SIZE)
    scores = jnp.einsum(
        "rhgd,rlhd->rhgl", query_blocks, key_blocks, preferred_element_type=f32
    ) * (1.0 / math.sqrt(HEAD_SIZE))
    position = lax.broadcasted_iota(jnp.int32, (1, 1, 1, span), 3)
    visible = position < lengths[:, None, None, None]
    scores = jnp.where(visible, scores, -1e30)
    peak = jnp.max(scores, axis=-1, keepdims=True)
    expd = jnp.exp(scores - peak)
    totals = jnp.sum(expd, axis=-1, keepdims=True)
    weights_bf = (expd / totals).astype(bf16)
    attended = jnp.einsum(
        "rhgl,rlhd->rhgd", weights_bf, value_blocks, preferred_element_type=f32
    )
    return attended.reshape(row_count, kv_heads * query_group * HEAD_SIZE).astype(bf16)


def send(x, axes, target):
    sizes = [lax.axis_size(axis) for axis in axes]
    pairs = []
    for index in range(math.prod(sizes)):
        place, rest = [], index
        for size in reversed(sizes):
            place.insert(0, rest % size)
            rest //= size
        other = 0
        for coordinate, size in zip(target(*place), sizes):
            other = other * size + coordinate % size
        pairs.append((index, other))
    return lax.ppermute(x, axes, pairs)


def swap_core(x):
    return send(x, ("attn",), lambda a: (a ^ 1,))


def along_z(x, step, back=False):
    sign = 1 if back else -1
    return send(x, ("attn",), lambda a: (a + sign * 2 * (step if a % 2 == 0 else -step),))


def along_x(x, step):
    return send(x, ("attn", "egrp"), lambda a, i: (a, i ^ (2 if step == 2 else 1 if a % 2 == step else 3)))


def to_y(x, step):
    return send(x, ("etp",), lambda i: (i + step,))


VMEM, SMEM, ANY = pltpu.VMEM, pltpu.SMEM, pl.ANY
NT = (((1,), (1,)), ((), ()))
CAPACITY_OF_512 = 384


def chosen(ranks, slots):
    slot = lax.broadcasted_iota(jnp.int32, (slots, ranks.shape[1]), 0)
    return (slot.astype(f32) == ranks).astype(bf16)


def pack_kernel(place, own, other, gate_own, gate_other, up_own, up_other, *outs):
    *outs, share, ranks = outs
    y, first = place[0], place[1]
    experts, fan, n = gate_own.shape
    units, slots = outs[0].shape[1], outs[0].shape[2]
    rows, extra = 2 * n, own.shape[1]
    route = jnp.concatenate([own[...], other[...]], axis=0)
    named = (route.astype(f32) > 0.0).astype(bf16)
    before = lax.broadcasted_iota(jnp.int32, (rows, rows), 1) <= lax.broadcasted_iota(
        jnp.int32, (rows, rows), 0
    )
    counts = jnp.dot(before.astype(bf16), named, preferred_element_type=f32)
    placed = jnp.where(named > 0, counts - 1.0, -1.0)
    column = lax.broadcasted_iota(jnp.int32, (rows, extra), 1)
    slot = lax.broadcasted_iota(jnp.int32, (rows, slots), 1).astype(f32)
    ranks[...] = jnp.transpose(placed)
    for e in range(experts):
        here = column == first + e
        rank = jnp.sum(jnp.where(here, placed, 0.0), axis=1, keepdims=True)
        onehot = (slot == rank).astype(bf16)

        @pl.when(y // (len(outs) // experts) == e)
        def _():
            values = jnp.sum(jnp.where(here, route.astype(f32), 0.0), axis=1, keepdims=True)
            values = jnp.sum(onehot.astype(f32) * values, axis=0, keepdims=True)
            share[...] = jnp.broadcast_to(values, share.shape)

        for g, (part_own, part_other) in enumerate(((gate_own, gate_other), (up_own, up_other))):
            packed = jnp.dot(part_own[e], onehot[:n], preferred_element_type=f32)
            packed = packed + jnp.dot(part_other[e], onehot[n:], preferred_element_type=f32)
            for h in range(fan // units):
                part = packed[h * units : (h + 1) * units].astype(bf16)
                step = lax.rem(e * (fan // units) + h + len(outs) - y, len(outs))
                for k, out in enumerate(outs):

                    @pl.when(step == k)
                    def _(out=out, g=g, part=part):
                        out[g] = part


def pack(place, own, other, sums):
    experts, fan, n = sums[0].shape
    rows, extra = 2 * n, own.shape[1]
    parts, slots = 4, rows * CAPACITY_OF_512 // 512
    whole = pl.BlockSpec(memory_space=VMEM)
    return pl.pallas_call(
        pack_kernel,
        out_shape=[jax.ShapeDtypeStruct((2, experts * fan // parts, slots), bf16)] * parts
        + [jax.ShapeDtypeStruct((8, slots), f32), jax.ShapeDtypeStruct((extra, rows), f32)],
        in_specs=[pl.BlockSpec(memory_space=SMEM)] + [whole] * 6,
        out_specs=[whole] * (parts + 2),
        compiler_params=pltpu.CompilerParams(vmem_limit_bytes=16 << 20),
        cost_estimate=pl.CostEstimate(flops=1 << 29, bytes_accessed=2 << 20, transcendentals=0),
    )(place, own, other, *sums)


def split_kernel(*refs):
    *pieces, rows, features, routes = refs
    width, at = features.shape[1], 0
    for piece in pieces:
        count = piece.shape[0]
        if rows is not None:
            rows[at : at + count] = piece[...]
        features[at : at + count] = piece[:, :width]
        routes[at : at + count] = piece[:, width:]
        at += count


def split(pieces, width, joined):
    count, columns = sum(p.shape[0] for p in pieces), pieces[0].shape[1]
    whole = pl.BlockSpec(memory_space=VMEM)
    widths = [columns] * joined + [width, columns - width]

    def kernel(*refs):
        outs = refs[len(pieces) :]
        split_kernel(*refs[: len(pieces)], outs[0] if joined else None, *outs[-2:])

    return pl.pallas_call(
        kernel,
        out_shape=[jax.ShapeDtypeStruct((count, w), pieces[0].dtype) for w in widths],
        in_specs=[whole] * len(pieces),
        out_specs=[whole] * len(widths),
        compiler_params=pltpu.CompilerParams(vmem_limit_bytes=8 << 20),
        cost_estimate=pl.CostEstimate(flops=1, bytes_accessed=1 << 20, transcendentals=0),
    )(*pieces)


def scatter_kernel(place, hidden0, hidden1, hidden2, hidden3, ranks, out):
    parts, slots = out.shape[0], hidden0.shape[1]
    for k, hidden in enumerate((hidden0, hidden1, hidden2, hidden3)):
        at = lax.rem(place[0] + k, parts)
        onehot = chosen(ranks[pl.ds(place[1] + at // 2, 1), :], slots)
        out[at] = jnp.dot(hidden[...], onehot, preferred_element_type=f32).astype(bf16)


def scatter(place, hidden, ranks):
    whole = pl.BlockSpec(memory_space=VMEM)
    return pl.pallas_call(
        scatter_kernel,
        out_shape=jax.ShapeDtypeStruct((4, hidden[0].shape[0], ranks.shape[1]), bf16),
        in_specs=[pl.BlockSpec(memory_space=SMEM)] + [whole] * 5,
        out_specs=whole,
        compiler_params=pltpu.CompilerParams(vmem_limit_bytes=16 << 20),
        cost_estimate=pl.CostEstimate(flops=1 << 28, bytes_accessed=1 << 20, transcendentals=0),
    )(place, *hidden, ranks)


def per_device(
    queries,
    cache_keys,
    stored_values,
    lengths,
    residual_in,
    norm_gain,
    expert_ids,
    expert_scores,
    w_gate,
    w_up,
    w_down,
):
    y, x = lax.axis_index("etp"), lax.axis_index("egrp")
    y_size = lax.axis_size("etp")
    attended = attend(queries, cache_keys, stored_values, lengths)
    stream = (residual_in.astype(f32) + attended.astype(f32)).astype(bf16)
    rows, width = stream.shape
    shares = expert_scores / jnp.sum(expert_scores, axis=1, keepdims=True)
    expert_iota = lax.broadcasted_iota(jnp.int32, (1, 1, EXPERTS), 2)
    route = jnp.sum(
        jnp.where(expert_ids[:, :, None] == expert_iota, shares[:, :, None], 0.0), axis=1
    ).astype(bf16)

    raw = stream.astype(f32)
    part_mean = jnp.mean(raw, axis=1, keepdims=True)
    part_dev = jnp.sum(jnp.square(raw - part_mean), axis=1, keepdims=True)
    stats = jnp.concatenate([part_mean, part_dev], axis=1)
    stats = [stats] + [to_y(stats, k) for k in range(1, y_size)]
    mean = sum(s[:, :1] for s in stats) / y_size
    dev = sum(s[:, 1:] + width * jnp.square(s[:, :1] - mean) for s in stats)
    gain = lax.dynamic_slice_in_dim(norm_gain, y * width, width, 0).astype(f32)
    normed = (raw - mean) * lax.rsqrt(dev / (width * y_size) + epsilon) * gain[None, :]
    held = jnp.concatenate(
        [normed.astype(bf16), jnp.pad(route, ((0, 0), (0, 128 - EXPERTS)))], axis=1
    )

    place = jnp.stack([y, x * w_gate.shape[0]]).astype(jnp.int32)
    down = w_down.reshape(-1, width)

    def project(weight, tokens):
        return jnp.einsum("edf,rd->efr", weight, tokens, preferred_element_type=f32).astype(bf16)

    across = along_z(held, 4)
    chip = jnp.concatenate([held, swap_core(held)], axis=0)
    held = jnp.concatenate([held, across] + [along_z(chip, k) for k in (1, 2, 3)], axis=0)
    own, own_rows, own_routes = split([held] + [along_x(held, k) for k in range(3)], width, True)
    other_rows, other_routes = split([swap_core(own)], width, False)
    sums = [project(w, t) for w in (w_gate, w_up) for t in (own_rows, other_rows)]
    *parts, share, ranks = pack(place, own_routes, other_routes, sums)
    sums = parts[0].astype(f32) + sum(
        to_y(part, k).astype(f32) for k, part in enumerate(parts) if k > 0
    )
    hidden = (jax.nn.silu(sums[0]) * sums[1] * share[:1]).astype(bf16)
    hidden = scatter(place, [hidden] + [to_y(hidden, -k) for k in range(1, y_size)], ranks)
    hidden = hidden.reshape(down.shape[0], -1)
    n = own.shape[0]

    def back_down(at):
        return jnp.einsum("fr,fd->rd", hidden[:, at : at + n], down, preferred_element_type=f32)

    other = swap_core(back_down(n).astype(bf16))
    total = back_down(0) + other.astype(f32)
    n = n // 4
    total = total[:n] + sum(
        along_x(total[(k + 1) * n : (k + 2) * n].astype(bf16), k).astype(f32) for k in range(3)
    )
    mine, across, n = total[:rows], total[rows : 2 * rows].astype(bf16), 2 * rows
    chip = sum(
        along_z(total[k * n : (k + 1) * n].astype(bf16), k, True).astype(f32) for k in (1, 2, 3)
    )
    mine = mine + along_z(across, 4, True).astype(f32) + chip[:rows]
    mine = mine + swap_core(chip[rows:].astype(bf16)).astype(f32)
    return (stream, mine.astype(bf16))


def solution(mesh):
    placed = (
        P(("attn", "egrp"), "etp"),
        P(("attn", "egrp"), None, "etp"),
        P(("attn", "egrp"), None, "etp"),
        P(("attn", "egrp")),
        P(("attn", "egrp"), "etp"),
        P(),
        P(("attn", "egrp"), None),
        P(("attn", "egrp"), None),
        P("egrp", "etp", "attn"),
        P("egrp", "etp", "attn"),
        P("egrp", "attn", "etp"),
    )
    return jax.shard_map(
        per_device,
        mesh=mesh,
        in_specs=placed,
        out_specs=(P(("attn", "egrp"), "etp"), P(("attn", "egrp"), "etp")),
        check_vma=False,
    )
```

time: 285 us -> 115 us (0.40); the launches traced: 281 us -> 114 us
  blocking collectives: 107 us -> 0 us
  waiting for transfers between devices: 140 us -> 46.2 us
  starting transfers between devices: 0.12 us -> 46.1 us
  between operations: 13.8 us -> 0.91 us
  matrix products: 15.9 us -> 9.88 us
  Pallas kernels: 0 us -> 5.28 us
    all_gather x2 -> x0, blocking collectives: 97.7 us -> none  [the longest x1 87.2 us: per_device(): lax.all_gather(route, ('attn', 'egrp'), axis=0, tiled=True)]
    all_gather x1 -> x0, waiting for transfers between devices: 82.4 us -> none  [per_device(): lax.all_gather(normed, ('attn', 'egrp'), axis=0, tiled=True)]
    reduce_scatter x1 -> x0, waiting for transfers between devices: 57.1 us -> none  [per_device(): lax.psum_scatter(jnp.einsum('erf,efd->rd', hidden, w_down, preferred_elem...]
    ppermute x0 -> x27, waiting for transfers between devices: none -> 46.2 us  [send(): return lax.ppermute(x, axes, pairs)]
    ppermute x0 -> x27, starting transfers between devices: none -> 46.1 us  [send(): return lax.ppermute(x, axes, pairs)]
    all_to_all x1 -> x0, blocking collectives: 9.09 us -> none  [per_device(): lax.all_to_all(reduced.reshape(lax.axis_size('egrp'), row_count, width_de...]
    dot_general x3 -> x6, matrix products: 12.5 us -> 6.46 us  [the longest x4 4.88 us: project(): jnp.einsum('edf,rd->efr', weight, tokens, preferred_element_type=f32)]
    pallas_call x0 -> x4, Pallas kernels: none -> 5.28 us  [the longest x1 3.09 us: pack(): pl.pallas_call(pack_kernel, out_shape=[jax.ShapeDtypeStruct((2, experts *...]
  transfers between devices with their start and end apart: 3 -> 27, of which waited for: 2 -> 16; matrix products, arithmetic and copies ran while one was open for 0% -> 4% of each run, Pallas kernels for 0% -> 0%
where the time goes in v2:
time: 115 us; the launch traced here: 114 us
  waiting for transfers between devices  46.2 us (40%)
  starting transfers between devices  46.1 us (40%)
  matrix products  9.88 us (9%)
  Pallas kernels  5.28 us (5%)
  other arithmetic  3.46 us (3%)
  local copies, waits for them, and re-layouts  2.61 us (2%)
    ppermute x27, waiting for transfers between devices, send(): return lax.ppermute(x, axes, pairs)  46.2 us
    ppermute x27, starting transfers between devices, send(): return lax.ppermute(x, axes, pairs)  46.1 us
    dot_general x4, matrix products, project(): jnp.einsum('edf,rd->efr', weight, tokens, preferred_element_type=f32)  4.88 us
    pallas_call x1, Pallas kernels, pack(): pl.pallas_call(pack_kernel, out_shape=[jax.ShapeDtypeStruct((2, experts *...  3.09 us
    unnamed x23, local copies, waits for them, and re-layouts  2.48 us
  transfers between devices with their start and end apart: 27, of which 16 were waited for; matrix products, arithmetic and copies ran while one was open for 4% of the time, Pallas kernels for 0%

profile of v2, /device:TPU:1, one launch (start us, length us, event | category | flops | bytes accessed | tf_op | source)
XLA Modules:
  0.0 114.5 jit_solution(1764703307652119912)
XLA Ops:
  0.6 0.9 iota_compare_fusion.1
  1.5 0.7 copy-done
  2.2 1.4 %fusion.16 = f32[8,2,6,512]{3,2,1,0:T(8,128)S(1)} fusion(pred[8,512]{1,0:T(8,128)(4,1)S(1)} %iota_compare_fusion.1, bf16[8,2,6,128]{3,0,2,1:T(8,128)(2,1)} %bitcast.79, bf16[8,512,256]{2,1,0:T(8,128)(2,1)S(1)} %copy-done), kind=kOutput, calls=%fused_computation.20 | convolution fusion | flops 12681216 | bytes 2322432 | tf_op jit(solution)/shard_map/rhgd,rlhd->rhgl/dot_general | solution.py:25
  3.9 2.0 %fusion.22 = f32[8,2,6,128]{3,2,1,0:T(8,128)S(1)} fusion(f32[8,2,6]{2,1,0:T(2,128)S(1)} %fusion.47, f32[8,2,6,512]{3,2,1,0:T(8,128)S(1)} %fusion.16, bf16[8,512,256]{2,1,0:T(8,128)(2,1)} %param.13), kind=kOutput, calls=%fused_computation.22 | convolution fusion | flops 12755551 | bytes 2343296 | tf_op jit(solution)/shard_map/rhgl,rlhd->rhgd/dot_general | solution.py:35
  6.3 3.6 %collective-permute-start.2 = (f32[8,2]{0,1:T(2,128)S(1)}, f32[8,2]{0,1:T(2,128)S(1)}, u32[]{:S(2)}, u32[]{:S(2)}) collective-permute-start(f32[8,2]{0,1:T(2,128)S(1)} %pad_maximum_fusion.2), channel_id=1, source_target_pairs={{0,3},{1,0},{2,1},{3,2},{4,7},{5,4},{6,5},{7,6},{8,11},{9,8},{10,9... | collective-permute-start | bytes 200 | tf_op jit(solution)/shard_map/ppermute | solution.py:53
  10.3 0.7 collective-permute-start
  11.1 0.8 dynamic-slice_convert_fusion
  11.9 2.0 %collective-permute-done.1 = f32[8,2]{0,1:T(2,128)S(1)} collective-permute-done((f32[8,2]{0,1:T(2,128)S(1)}, f32[8,2]{0,1:T(2,128)S(1)}, u32[]{:S(2)}, u32[]{:S(2)}) %collective-permute-start.1) | collective-permute-done | bytes 96 | tf_op jit(solution)/shard_map/ppermute | solution.py:53
  14.0 2.5 %collective-permute-start.4 = (bf16[8,1664]{1,0:T(8,128)(2,1)S(1)}, bf16[8,1664]{1,0:T(8,128)(2,1)S(1)}, u32[]{:S(2)}, u32[]{:S(2)}) collective-permute-start(bf16[8,1664]{1,0:T(8,128)(2,1)S(1)} %get-tuple-element.36), channel_id=1, source_target_pairs={{0,16},{16,0},{32,48},{48,32},{64,80},{80,64},{96,112},{112,96},{1... | collective-permute-start | bytes 79880 | tf_op jit(solution)/shard_map/ppermute | solution.py:53
  16.5 6.9 %collective-permute-start.3 = (bf16[8,1664]{1,0:T(8,128)(2,1)S(1)}, bf16[8,1664]{1,0:T(8,128)(2,1)S(1)}, u32[]{:S(2)}, u32[]{:S(2)}) collective-permute-start(bf16[8,1664]{1,0:T(8,128)(2,1)S(1)} %get-tuple-element.36), channel_id=1, source_target_pairs={{0,128},{16,144},{32,160},{48,176},{64,192},{80,208},{96,224},{112... | collective-permute-start | bytes 79880 | tf_op jit(solution)/shard_map/ppermute | solution.py:53
  23.4 1.7 %collective-permute-start.7 = (bf16[16,1664]{1,0:T(8,128)(2,1)S(1)}, bf16[16,1664]{1,0:T(8,128)(2,1)S(1)}, u32[]{:S(2)}, u32[]{:S(2)}) collective-permute-start(bf16[16,1664]{1,0:T(8,128)(2,1)S(1)} %pad_maximum_fusion), channel_id=1, source_target_pairs={{0,160},{16,112},{32,192},{48,144},{64,224},{80,176},{96,0},{112,2... | collective-permute-start | bytes 159752 | tf_op jit(solution)/shard_map/ppermute | solution.py:53
  25.8 5.7 %collective-permute-done.5 = bf16[16,1664]{1,0:T(8,128)(2,1)S(1)} collective-permute-done((bf16[16,1664]{1,0:T(8,128)(2,1)S(1)}, bf16[16,1664]{1,0:T(8,128)(2,1)S(1)}, u32[]{:S(2)}, u32[]{:S(2)}) %collective-permute-start.5) | collective-permute-done | bytes 53280 | tf_op jit(solution)/shard_map/ppermute | solution.py:53
  31.5 2.8 %collective-permute-start.10 = (bf16[64,1664]{1,0:T(8,128)(2,1)S(1)}, bf16[64,1664]{1,0:T(8,128)(2,1)S(1)}, u32[]{:S(2)}, u32[]{:S(2)}) collective-permute-start(bf16[64,1664]{1,0:T(8,128)(2,1)S(1)} %constant_dynamic-update-slice_fusion.refs_0_), channel_id=1, source_target_pairs={{0,8},{4,12},{8,0},{12,4},{16,24},{20,28},{24,16},{28,20},{32,40},... | collective-permute-start | bytes 638984 | tf_op jit(solution)/shard_map/ppermute | solution.py:53
  35.2 3.5 %collective-permute-done.10.refs_3_ = bf16[64,1664]{1,0:T(8,128)(2,1)S(1)} collective-permute-done((bf16[64,1664]{1,0:T(8,128)(2,1)S(1)}, bf16[64,1664]{1,0:T(8,128)(2,1)S(1)}, u32[]{:S(2)}, u32[]{:S(2)}) %collective-permute-start.10) | collective-permute-done | bytes 213024 | tf_op jit(solution)/shard_map/ppermute | solution.py:53
  38.7 4.7 %collective-permute-done.9.refs_2_ = bf16[64,1664]{1,0:T(8,128)(2,1)S(1)} collective-permute-done((bf16[64,1664]{1,0:T(8,128)(2,1)S(1)}, bf16[64,1664]{1,0:T(8,128)(2,1)S(1)}, u32[]{:S(2)}, u32[]{:S(2)}) %collective-permute-start.9) | collective-permute-done | bytes 213024 | tf_op jit(solution)/shard_map/ppermute | solution.py:53
  43.4 0.8 collective-permute-done.8.refs_1_
  44.2 1.0 shard_map.122
  45.2 0.9 copy-done.1
  46.1 1.3 %collective-permute-start.11 = (bf16[256,1664]{1,0:T(8,128)(2,1)}, bf16[256,1664]{1,0:T(8,128)(2,1)S(1)}, u32[]{:S(2)}, u32[]{:S(2)}) collective-permute-start(bf16[256,1664]{1,0:T(8,128)(2,1)} %get-tuple-element.14), channel_id=1, source_target_pairs={{0,16},{16,0},{32,48},{48,32},{64,80},{80,64},{96,112},{112,96},{1... | collective-permute-start | bytes 2555912 | tf_op jit(solution)/shard_map/ppermute | solution.py:53
  47.5 2.7 %fusion.10.up_own = bf16[2,336,256]{2,1,0:T(8,128)(2,1)S(1)} fusion(bf16[2,1536,336]{1,2,0:T(8,128)(2,1)} %param.20, bf16[256,1536]{1,0:T(8,128)(2,1)} %copy-done.1), kind=kOutput, calls=%fused_computation.16 | convolution fusion | flops 528654336 | bytes 3194880 | tf_op jit(solution)/shard_map/edf,rd->efr/dot_general | solution.py:231
  50.3 0.7 fusion.8.gate_own
  51.1 0.8 copy-done.8
  51.8 0.7 fusion.11.up_other
  52.6 0.7 fusion.9.gate_other
  53.3 3.1 %shard_map.124 = (bf16[2,168,384]{2,1,0:T(8,128)(2,1)S(1)}, bf16[2,168,384]{2,1,0:T(8,128)(2,1)S(1)}, bf16[2,168,384]{2,1,0:T(8,128)(2,1)S(1)}, bf16[2,168,384]{...) custom-call(s32[2]{0:T(128)S(1)} %pad_add_fusion.place, ...), custom_call_target="tpu_custom_call" | custom-call | flops 536870912 | bytes 2097152 | tf_op jit(solution)/shard_map/pallas_call | solution.py:128
  56.5 1.5 %collective-permute-start.13 = (bf16[2,168,384]{2,1,0:T(8,128)(2,1)S(1)}, bf16[2,168,384]{2,1,0:T(8,128)(2,1)S(1)}, u32[]{:S(2)}, u32[]{:S(2)}) collective-permute-start(bf16[2,168,384]{2,1,0:T(8,128)(2,1)S(1)} %get-tuple-element.20), channel_id=1, source_target_pairs={{0,2},{1,3},{2,0},{3,1},{4,6},{5,7},{6,4},{7,5},{8,10},{9,11},{10,... | collective-permute-start | bytes 774152 | tf_op jit(solution)/shard_map/ppermute | solution.py:53
  58.0 2.0 %collective-permute-start.14 = (bf16[2,168,384]{2,1,0:T(8,128)(2,1)S(1)}, bf16[2,168,384]{2,1,0:T(8,128)(2,1)S(1)}, u32[]{:S(2)}, u32[]{:S(2)}) collective-permute-start(bf16[2,168,384]{2,1,0:T(8,128)(2,1)S(1)} %get-tuple-element.21), channel_id=1, source_target_pairs={{0,3},{1,0},{2,1},{3,2},{4,7},{5,4},{6,5},{7,6},{8,11},{9,8},{10,9... | collective-permute-start | bytes 774152 | tf_op jit(solution)/shard_map/ppermute | solution.py:53
  60.0 11.1 %collective-permute-done.12 = bf16[2,168,384]{2,1,0:T(8,128)(2,1)S(1)} collective-permute-done((bf16[2,168,384]{2,1,0:T(8,128)(2,1)S(1)}, bf16[2,168,384]{2,1,0:T(8,128)(2,1)S(1)}, u32[]{:S(2)}, u32[]{:S(2)}) %collective-permute-start.12) | collective-permute-done | bytes 258080 | tf_op jit(solution)/shard_map/ppermute | solution.py:53
  71.6 1.4 %collective-permute-start.17 = (bf16[168,384]{1,0:T(8,128)(2,1)S(1)}, bf16[168,384]{1,0:T(8,128)(2,1)S(1)}, u32[]{:S(2)}, u32[]{:S(2)}) collective-permute-start(bf16[168,384]{1,0:T(8,128)(2,1)S(1)} %fusion.33.hidden0), channel_id=1, source_target_pairs={{0,1},{1,2},{2,3},{3,0},{4,5},{5,6},{6,7},{7,4},{8,9},{9,10},{10,1... | collective-permute-start | bytes 387080 | tf_op jit(solution)/shard_map/ppermute | solution.py:53
  73.1 2.8 %collective-permute-start.16 = (bf16[168,384]{1,0:T(8,128)(2,1)S(1)}, bf16[168,384]{1,0:T(8,128)(2,1)S(1)}, u32[]{:S(2)}, u32[]{:S(2)}) collective-permute-start(bf16[168,384]{1,0:T(8,128)(2,1)S(1)} %fusion.33.hidden0), channel_id=1, source_target_pairs={{0,2},{1,3},{2,0},{3,1},{4,6},{5,7},{6,4},{7,5},{8,10},{9,11},{10,... | collective-permute-start | bytes 387080 | tf_op jit(solution)/shard_map/ppermute | solution.py:53
  75.8 1.5 %collective-permute-done.17.hidden3 = bf16[168,384]{1,0:T(8,128)(2,1)S(1)} collective-permute-done((bf16[168,384]{1,0:T(8,128)(2,1)S(1)}, bf16[168,384]{1,0:T(8,128)(2,1)S(1)}, u32[]{:S(2)}, u32[]{:S(2)}) %collective-permute-start.17) | collective-permute-done | bytes 129056 | tf_op jit(solution)/shard_map/ppermute | solution.py:53
  77.4 4.3 %collective-permute-done.16.hidden2 = bf16[168,384]{1,0:T(8,128)(2,1)S(1)} collective-permute-done((bf16[168,384]{1,0:T(8,128)(2,1)S(1)}, bf16[168,384]{1,0:T(8,128)(2,1)S(1)}, u32[]{:S(2)}, u32[]{:S(2)}) %collective-permute-start.16) | collective-permute-done | bytes 129056 | tf_op jit(solution)/shard_map/ppermute | solution.py:53
  81.7 1.1 shard_map.125
  82.8 0.8 convolution_convert_fusion
  83.6 1.4 %collective-permute-start.18 = (bf16[256,1536]{1,0:T(8,128)(2,1)S(1)}, bf16[256,1536]{1,0:T(8,128)(2,1)S(1)}, u32[]{:S(2)}, u32[]{:S(2)}) collective-permute-start(bf16[256,1536]{1,0:T(8,128)(2,1)S(1)} %convolution_convert_fusion), channel_id=1, source_target_pairs={{0,16},{16,0},{32,48},{48,32},{64,80},{80,64},{96,112},{112,96},{1... | collective-permute-start | bytes 2359304 | tf_op jit(solution)/shard_map/ppermute | solution.py:53
  85.0 1.9 %collective-permute-done.18 = bf16[256,1536]{1,0:T(8,128)(2,1)S(1)} collective-permute-done((bf16[256,1536]{1,0:T(8,128)(2,1)S(1)}, bf16[256,1536]{1,0:T(8,128)(2,1)S(1)}, u32[]{:S(2)}, u32[]{:S(2)}) %collective-permute-start.18) | collective-permute-done | bytes 786464 | tf_op jit(solution)/shard_map/ppermute | solution.py:53
  86.9 0.8 fusion.48
  87.8 2.5 %collective-permute-start.19 = (bf16[64,1536]{1,0:T(8,128)(2,1)S(1)}, bf16[64,1536]{1,0:T(8,128)(2,1)S(1)}, u32[]{:S(2)}, u32[]{:S(2)}) collective-permute-start(bf16[64,1536]{1,0:T(8,128)(2,1)S(1)} %get-tuple-element.30), channel_id=1, source_target_pairs={{0,4},{4,0},{8,12},{12,8},{16,28},{20,24},{24,20},{28,16},{32,36},... | collective-permute-start | bytes 589832 | tf_op jit(solution)/shard_map/ppermute | solution.py:53
  91.1 5.2 %collective-permute-done.19 = bf16[64,1536]{1,0:T(8,128)(2,1)S(1)} collective-permute-done((bf16[64,1536]{1,0:T(8,128)(2,1)S(1)}, bf16[64,1536]{1,0:T(8,128)(2,1)S(1)}, u32[]{:S(2)}, u32[]{:S(2)}) %collective-permute-start.19) | collective-permute-done | bytes 196640 | tf_op jit(solution)/shard_map/ppermute | solution.py:53
  96.3 2.4 %collective-permute-done.21 = bf16[64,1536]{1,0:T(8,128)(2,1)S(1)} collective-permute-done((bf16[64,1536]{1,0:T(8,128)(2,1)S(1)}, bf16[64,1536]{1,0:T(8,128)(2,1)S(1)}, u32[]{:S(2)}, u32[]{:S(2)}) %collective-permute-start.21) | collective-permute-done | bytes 196640 | tf_op jit(solution)/shard_map/ppermute | solution.py:53
  98.7 1.1 %collective-permute-done.20 = bf16[64,1536]{1,0:T(8,128)(2,1)S(1)} collective-permute-done((bf16[64,1536]{1,0:T(8,128)(2,1)S(1)}, bf16[64,1536]{1,0:T(8,128)(2,1)S(1)}, u32[]{:S(2)}, u32[]{:S(2)}) %collective-permute-start.20) | collective-permute-done | bytes 196640 | tf_op jit(solution)/shard_map/ppermute | solution.py:53
  100.0 0.9 collective-permute-start.23
  100.9 2.2 %collective-permute-start.25 = (bf16[16,1536]{1,0:T(8,128)(2,1)S(1)}, bf16[16,1536]{1,0:T(8,128)(2,1)S(1)}, u32[]{:S(2)}, u32[]{:S(2)}) collective-permute-start(bf16[16,1536]{1,0:T(8,128)(2,1)S(1)} %get-tuple-element.34), channel_id=1, source_target_pairs={{0,96},{16,176},{32,128},{48,208},{64,160},{80,240},{96,192},{112,... | collective-permute-start | bytes 147464 | tf_op jit(solution)/shard_map/ppermute | solution.py:53
  103.1 1.4 %collective-permute-start.24 = (bf16[16,1536]{1,0:T(8,128)(2,1)S(1)}, bf16[16,1536]{1,0:T(8,128)(2,1)S(1)}, u32[]{:S(2)}, u32[]{:S(2)}) collective-permute-start(bf16[16,1536]{1,0:T(8,128)(2,1)S(1)} %get-tuple-element.35), channel_id=1, source_target_pairs={{0,64},{16,208},{32,96},{48,240},{64,128},{80,16},{96,160},{112,48... | collective-permute-start | bytes 147464 | tf_op jit(solution)/shard_map/ppermute | solution.py:53
  104.5 2.6 %collective-permute-start.22 = (bf16[8,1536]{1,0:T(8,128)(2,1)S(1)}, bf16[8,1536]{1,0:T(8,128)(2,1)S(1)}, u32[]{:S(2)}, u32[]{:S(2)}) collective-permute-start(bf16[8,1536]{1,0:T(8,128)(2,1)S(1)} %slice.108), channel_id=1, source_target_pairs={{0,128},{16,144},{32,160},{48,176},{64,192},{80,208},{96,224},{112... | collective-permute-start | bytes 73736 | tf_op jit(solution)/shard_map/ppermute | solution.py:53
  107.1 0.8 collective-permute-done.24
  108.0 5.0 %collective-permute-start.26 = (bf16[8,1536]{1,0:T(8,128)(2,1)S(1)}, bf16[8,1536]{1,0:T(8,128)(2,1)S(1)}, u32[]{:S(2)}, u32[]{:S(2)}) collective-permute-start(bf16[8,1536]{1,0:T(8,128)(2,1)S(1)} %slice.148), channel_id=1, source_target_pairs={{0,16},{16,0},{32,48},{48,32},{64,80},{80,64},{96,112},{112,96},{1... | collective-permute-start | bytes 73736 | tf_op jit(solution)/shard_map/ppermute | solution.py:53
  113.0 0.8 collective-permute-done.26
  (69 shorter events, 5.2 us)
Async XLA Ops:
  0.6 1.6 %copy-start = (bf16[8,512,256]{2,1,0:T(8,128)(2,1)S(1)}, bf16[8,512,256]{2,1,0:T(8,128)(2,1)}, u32[]{:S(2)}) copy-start(bf16[8,512,256]{2,1,0:T(8,128)(2,1)} %param.12) | copy-start | bytes 6291460
  3.6 2.3 %copy-start.5 = (bf16[8,1536]{1,0:T(8,128)(2,1)S(1)}, bf16[8,1536]{1,0:T(8,128)(2,1)}, u32[]{:S(2)}) copy-start(bf16[8,1536]{1,0:T(8,128)(2,1)} %param.15) | copy-start | bytes 73732
  3.6 7.4 %copy-start.6 = (f32[8,4]{0,1:T(4,128)S(1)}, f32[8,4]{0,1:T(4,128)}, u32[]{:S(2)}) copy-start(f32[8,4]{0,1:T(4,128)} %param.18) | copy-start | bytes 388
  3.6 7.4 %copy-start.7 = (s32[8,4]{0,1:T(4,128)S(1)}, s32[8,4]{0,1:T(4,128)}, u32[]{:S(2)}) copy-start(s32[8,4]{0,1:T(4,128)} %param.17) | copy-start | bytes 388
  6.1 44.1 %copy-start.4 = (bf16[8,1536]{1,0:T(8,128)(2,1)}, bf16[8,1536]{1,0:T(8,128)(2,1)S(1)}, u32[]{:S(2)}) copy-start(bf16[8,1536]{1,0:T(8,128)(2,1)S(1)} %get-tuple-element.29) | copy-start | bytes 73732
  6.3 5.6 %collective-permute-start.2 = (f32[8,2]{0,1:T(2,128)S(1)}, f32[8,2]{0,1:T(2,128)S(1)}, u32[]{:S(2)}, u32[]{:S(2)}) collective-permute-start(f32[8,2]{0,1:T(2,128)S(1)} %pad_maximum_fusion.2), channel_id=1, source_target_pairs={{0,3},{1,0},{2,1},{3,2},{4,7},{5,4},{6,5},{7,6},{8,11},{9,8},{10,9... | collective-permute-start | bytes 200 | tf_op jit(solution)/shard_map/ppermute | solution.py:53
  9.9 3.9 %collective-permute-start.1 = (f32[8,2]{0,1:T(2,128)S(1)}, f32[8,2]{0,1:T(2,128)S(1)}, u32[]{:S(2)}, u32[]{:S(2)}) collective-permute-start(f32[8,2]{0,1:T(2,128)S(1)} %pad_maximum_fusion.2), channel_id=1, source_target_pairs={{0,2},{1,3},{2,0},{3,1},{4,6},{5,7},{6,4},{7,5},{8,10},{9,11},{10,... | collective-permute-start | bytes 200 | tf_op jit(solution)/shard_map/ppermute | solution.py:53
  10.3 3.6 %collective-permute-start = (f32[8,2]{0,1:T(2,128)S(1)}, f32[8,2]{0,1:T(2,128)S(1)}, u32[]{:S(2)}, u32[]{:S(2)}) collective-permute-start(f32[8,2]{0,1:T(2,128)S(1)} %pad_maximum_fusion.2), channel_id=1, source_target_pairs={{0,1},{1,2},{2,3},{3,0},{4,5},{5,6},{6,7},{7,4},{8,9},{9,10},{10,1... | collective-permute-start | bytes 200 | tf_op jit(solution)/shard_map/ppermute | solution.py:53
  14.0 9.4 %collective-permute-start.4 = (bf16[8,1664]{1,0:T(8,128)(2,1)S(1)}, bf16[8,1664]{1,0:T(8,128)(2,1)S(1)}, u32[]{:S(2)}, u32[]{:S(2)}) collective-permute-start(bf16[8,1664]{1,0:T(8,128)(2,1)S(1)} %get-tuple-element.36), channel_id=1, source_target_pairs={{0,16},{16,0},{32,48},{48,32},{64,80},{80,64},{96,112},{112,96},{1... | collective-permute-start | bytes 79880 | tf_op jit(solution)/shard_map/ppermute | solution.py:53
  16.5 9.2 %collective-permute-start.3 = (bf16[8,1664]{1,0:T(8,128)(2,1)S(1)}, bf16[8,1664]{1,0:T(8,128)(2,1)S(1)}, u32[]{:S(2)}, u32[]{:S(2)}) collective-permute-start(bf16[8,1664]{1,0:T(8,128)(2,1)S(1)} %get-tuple-element.36), channel_id=1, source_target_pairs={{0,128},{16,144},{32,160},{48,176},{64,192},{80,208},{96,224},{112... | collective-permute-start | bytes 79880 | tf_op jit(solution)/shard_map/ppermute | solution.py:53
  23.4 8.1 %collective-permute-start.7 = (bf16[16,1664]{1,0:T(8,128)(2,1)S(1)}, bf16[16,1664]{1,0:T(8,128)(2,1)S(1)}, u32[]{:S(2)}, u32[]{:S(2)}) collective-permute-start(bf16[16,1664]{1,0:T(8,128)(2,1)S(1)} %pad_maximum_fusion), channel_id=1, source_target_pairs={{0,160},{16,112},{32,192},{48,144},{64,224},{80,176},{96,0},{112,2... | collective-permute-start | bytes 159752 | tf_op jit(solution)/shard_map/ppermute | solution.py:53
  25.2 6.3 %collective-permute-start.6 = (bf16[16,1664]{1,0:T(8,128)(2,1)S(1)}, bf16[16,1664]{1,0:T(8,128)(2,1)S(1)}, u32[]{:S(2)}, u32[]{:S(2)}) collective-permute-start(bf16[16,1664]{1,0:T(8,128)(2,1)S(1)} %pad_maximum_fusion), channel_id=1, source_target_pairs={{0,192},{16,80},{32,224},{48,112},{64,0},{80,144},{96,32},{112,176... | collective-permute-start | bytes 159752 | tf_op jit(solution)/shard_map/ppermute | solution.py:53
  25.2 6.3 %collective-permute-start.5 = (bf16[16,1664]{1,0:T(8,128)(2,1)S(1)}, bf16[16,1664]{1,0:T(8,128)(2,1)S(1)}, u32[]{:S(2)}, u32[]{:S(2)}) collective-permute-start(bf16[16,1664]{1,0:T(8,128)(2,1)S(1)} %pad_maximum_fusion), channel_id=1, source_target_pairs={{0,224},{16,48},{32,0},{48,80},{64,32},{80,112},{96,64},{112,144},... | collective-permute-start | bytes 159752 | tf_op jit(solution)/shard_map/ppermute | solution.py:53
  31.5 7.2 %collective-permute-start.10 = (bf16[64,1664]{1,0:T(8,128)(2,1)S(1)}, bf16[64,1664]{1,0:T(8,128)(2,1)S(1)}, u32[]{:S(2)}, u32[]{:S(2)}) collective-permute-start(bf16[64,1664]{1,0:T(8,128)(2,1)S(1)} %constant_dynamic-update-slice_fusion.refs_0_), channel_id=1, source_target_pairs={{0,8},{4,12},{8,0},{12,4},{16,24},{20,28},{24,16},{28,20},{32,40},... | collective-permute-start | bytes 638984 | tf_op jit(solution)/shard_map/ppermute | solution.py:53
  34.4 9.1 %collective-permute-start.9 = (bf16[64,1664]{1,0:T(8,128)(2,1)S(1)}, bf16[64,1664]{1,0:T(8,128)(2,1)S(1)}, u32[]{:S(2)}, u32[]{:S(2)}) collective-permute-start(bf16[64,1664]{1,0:T(8,128)(2,1)S(1)} %constant_dynamic-update-slice_fusion.refs_0_), channel_id=1, source_target_pairs={{0,12},{4,8},{8,4},{12,0},{16,20},{20,16},{24,28},{28,24},{32,44},... | collective-permute-start | bytes 638984 | tf_op jit(solution)/shard_map/ppermute | solution.py:53
  34.7 9.5 %collective-permute-start.8 = (bf16[64,1664]{1,0:T(8,128)(2,1)S(1)}, bf16[64,1664]{1,0:T(8,128)(2,1)S(1)}, u32[]{:S(2)}, u32[]{:S(2)}) collective-permute-start(bf16[64,1664]{1,0:T(8,128)(2,1)S(1)} %constant_dynamic-update-slice_fusion.refs_0_), channel_id=1, source_target_pairs={{0,4},{4,0},{8,12},{12,8},{16,28},{20,24},{24,20},{28,16},{32,36},... | collective-permute-start | bytes 638984 | tf_op jit(solution)/shard_map/ppermute | solution.py:53
  45.2 0.9 copy-start.1
  46.1 4.9 %collective-permute-start.11 = (bf16[256,1664]{1,0:T(8,128)(2,1)}, bf16[256,1664]{1,0:T(8,128)(2,1)S(1)}, u32[]{:S(2)}, u32[]{:S(2)}) collective-permute-start(bf16[256,1664]{1,0:T(8,128)(2,1)} %get-tuple-element.14), channel_id=1, source_target_pairs={{0,16},{16,0},{32,48},{48,32},{64,80},{80,64},{96,112},{112,96},{1... | collective-permute-start | bytes 2555912 | tf_op jit(solution)/shard_map/ppermute | solution.py:53
  47.4 2.8 %copy-start.2 = (bf16[256,1536]{1,0:T(8,128)(2,1)S(1)}, bf16[256,1536]{1,0:T(8,128)(2,1)}, u32[]{:S(2)}) copy-start(bf16[256,1536]{1,0:T(8,128)(2,1)} %copy-done.1) | copy-start | bytes 2359300
  47.4 2.8 %copy-start.9 = (bf16[2,1536,336]{1,2,0:T(8,128)(2,1)S(1)}, bf16[2,1536,336]{1,2,0:T(8,128)(2,1)}, u32[]{:S(2)}) copy-start(bf16[2,1536,336]{1,2,0:T(8,128)(2,1)} %param.19) | copy-start | bytes 6193156
  50.3 1.6 %copy-start.8 = (bf16[2,1536,336]{1,2,0:T(8,128)(2,1)S(1)}, bf16[2,1536,336]{1,2,0:T(8,128)(2,1)}, u32[]{:S(2)}) copy-start(bf16[2,1536,336]{1,2,0:T(8,128)(2,1)} %param.20) | copy-start | bytes 6193156
  56.4 26.4 %copy-start.3 = (bf16[2,336,1536]{2,1,0:T(8,128)(2,1)S(1)}, bf16[2,336,1536]{2,1,0:T(8,128)(2,1)}, u32[]{:S(2)}) copy-start(bf16[2,336,1536]{2,1,0:T(8,128)(2,1)} %param.21) | copy-start | bytes 6193156
  56.4 14.7 %collective-permute-start.12 = (bf16[2,168,384]{2,1,0:T(8,128)(2,1)S(1)}, bf16[2,168,384]{2,1,0:T(8,128)(2,1)S(1)}, u32[]{:S(2)}, u32[]{:S(2)}) collective-permute-start(bf16[2,168,384]{2,1,0:T(8,128)(2,1)S(1)} %get-tuple-element.19), channel_id=1, source_target_pairs={{0,1},{1,2},{2,3},{3,0},{4,5},{5,6},{6,7},{7,4},{8,9},{9,10},{10,1... | collective-permute-start | bytes 774152 | tf_op jit(solution)/shard_map/ppermute | solution.py:53
  56.5 14.6 %collective-permute-start.13 = (bf16[2,168,384]{2,1,0:T(8,128)(2,1)S(1)}, bf16[2,168,384]{2,1,0:T(8,128)(2,1)S(1)}, u32[]{:S(2)}, u32[]{:S(2)}) collective-permute-start(bf16[2,168,384]{2,1,0:T(8,128)(2,1)S(1)} %get-tuple-element.20), channel_id=1, source_target_pairs={{0,2},{1,3},{2,0},{3,1},{4,6},{5,7},{6,4},{7,5},{8,10},{9,11},{10,... | collective-permute-start | bytes 774152 | tf_op jit(solution)/shard_map/ppermute | solution.py:53
  58.0 13.4 %collective-permute-start.14 = (bf16[2,168,384]{2,1,0:T(8,128)(2,1)S(1)}, bf16[2,168,384]{2,1,0:T(8,128)(2,1)S(1)}, u32[]{:S(2)}, u32[]{:S(2)}) collective-permute-start(bf16[2,168,384]{2,1,0:T(8,128)(2,1)S(1)} %get-tuple-element.21), channel_id=1, source_target_pairs={{0,3},{1,0},{2,1},{3,2},{4,7},{5,4},{6,5},{7,6},{8,11},{9,8},{10,9... | collective-permute-start | bytes 774152 | tf_op jit(solution)/shard_map/ppermute | solution.py:53
  71.6 5.7 %collective-permute-start.17 = (bf16[168,384]{1,0:T(8,128)(2,1)S(1)}, bf16[168,384]{1,0:T(8,128)(2,1)S(1)}, u32[]{:S(2)}, u32[]{:S(2)}) collective-permute-start(bf16[168,384]{1,0:T(8,128)(2,1)S(1)} %fusion.33.hidden0), channel_id=1, source_target_pairs={{0,1},{1,2},{2,3},{3,0},{4,5},{5,6},{6,7},{7,4},{8,9},{9,10},{10,1... | collective-permute-start | bytes 387080 | tf_op jit(solution)/shard_map/ppermute | solution.py:53
  73.1 8.6 %collective-permute-start.16 = (bf16[168,384]{1,0:T(8,128)(2,1)S(1)}, bf16[168,384]{1,0:T(8,128)(2,1)S(1)}, u32[]{:S(2)}, u32[]{:S(2)}) collective-permute-start(bf16[168,384]{1,0:T(8,128)(2,1)S(1)} %fusion.33.hidden0), channel_id=1, source_target_pairs={{0,2},{1,3},{2,0},{3,1},{4,6},{5,7},{6,4},{7,5},{8,10},{9,11},{10,... | collective-permute-start | bytes 387080 | tf_op jit(solution)/shard_map/ppermute | solution.py:53
  75.8 5.8 %collective-permute-start.15 = (bf16[168,384]{1,0:T(8,128)(2,1)S(1)}, bf16[168,384]{1,0:T(8,128)(2,1)S(1)}, u32[]{:S(2)}, u32[]{:S(2)}) collective-permute-start(bf16[168,384]{1,0:T(8,128)(2,1)S(1)} %fusion.33.hidden0), channel_id=1, source_target_pairs={{0,3},{1,0},{2,1},{3,2},{4,7},{5,4},{6,5},{7,6},{8,11},{9,8},{10,9... | collective-permute-start | bytes 387080 | tf_op jit(solution)/shard_map/ppermute | solution.py:53
  83.6 3.3 %collective-permute-start.18 = (bf16[256,1536]{1,0:T(8,128)(2,1)S(1)}, bf16[256,1536]{1,0:T(8,128)(2,1)S(1)}, u32[]{:S(2)}, u32[]{:S(2)}) collective-permute-start(bf16[256,1536]{1,0:T(8,128)(2,1)S(1)} %convolution_convert_fusion), channel_id=1, source_target_pairs={{0,16},{16,0},{32,48},{48,32},{64,80},{80,64},{96,112},{112,96},{1... | collective-permute-start | bytes 2359304 | tf_op jit(solution)/shard_map/ppermute | solution.py:53
  87.8 8.6 %collective-permute-start.19 = (bf16[64,1536]{1,0:T(8,128)(2,1)S(1)}, bf16[64,1536]{1,0:T(8,128)(2,1)S(1)}, u32[]{:S(2)}, u32[]{:S(2)}) collective-permute-start(bf16[64,1536]{1,0:T(8,128)(2,1)S(1)} %get-tuple-element.30), channel_id=1, source_target_pairs={{0,4},{4,0},{8,12},{12,8},{16,28},{20,24},{24,20},{28,16},{32,36},... | collective-permute-start | bytes 589832 | tf_op jit(solution)/shard_map/ppermute | solution.py:53
  90.2 8.5 %collective-permute-start.21 = (bf16[64,1536]{1,0:T(8,128)(2,1)S(1)}, bf16[64,1536]{1,0:T(8,128)(2,1)S(1)}, u32[]{:S(2)}, u32[]{:S(2)}) collective-permute-start(bf16[64,1536]{1,0:T(8,128)(2,1)S(1)} %get-tuple-element.31), channel_id=1, source_target_pairs={{0,8},{4,12},{8,0},{12,4},{16,24},{20,28},{24,16},{28,20},{32,40},... | collective-permute-start | bytes 589832 | tf_op jit(solution)/shard_map/ppermute | solution.py:53
  90.8 9.0 %collective-permute-start.20 = (bf16[64,1536]{1,0:T(8,128)(2,1)S(1)}, bf16[64,1536]{1,0:T(8,128)(2,1)S(1)}, u32[]{:S(2)}, u32[]{:S(2)}) collective-permute-start(bf16[64,1536]{1,0:T(8,128)(2,1)S(1)} %get-tuple-element.32), channel_id=1, source_target_pairs={{0,12},{4,8},{8,4},{12,0},{16,20},{20,16},{24,28},{28,24},{32,44},... | collective-permute-start | bytes 589832 | tf_op jit(solution)/shard_map/ppermute | solution.py:53
  100.0 7.2 %collective-permute-start.23 = (bf16[16,1536]{1,0:T(8,128)(2,1)S(1)}, bf16[16,1536]{1,0:T(8,128)(2,1)S(1)}, u32[]{:S(2)}, u32[]{:S(2)}) collective-permute-start(bf16[16,1536]{1,0:T(8,128)(2,1)S(1)} %get-tuple-element.33), channel_id=1, source_target_pairs={{0,32},{16,240},{32,64},{48,16},{64,96},{80,48},{96,128},{112,80},... | collective-permute-start | bytes 147464 | tf_op jit(solution)/shard_map/ppermute | solution.py:53
  100.9 6.2 %collective-permute-start.25 = (bf16[16,1536]{1,0:T(8,128)(2,1)S(1)}, bf16[16,1536]{1,0:T(8,128)(2,1)S(1)}, u32[]{:S(2)}, u32[]{:S(2)}) collective-permute-start(bf16[16,1536]{1,0:T(8,128)(2,1)S(1)} %get-tuple-element.34), channel_id=1, source_target_pairs={{0,96},{16,176},{32,128},{48,208},{64,160},{80,240},{96,192},{112,... | collective-permute-start | bytes 147464 | tf_op jit(solution)/shard_map/ppermute | solution.py:53
  103.1 4.9 %collective-permute-start.24 = (bf16[16,1536]{1,0:T(8,128)(2,1)S(1)}, bf16[16,1536]{1,0:T(8,128)(2,1)S(1)}, u32[]{:S(2)}, u32[]{:S(2)}) collective-permute-start(bf16[16,1536]{1,0:T(8,128)(2,1)S(1)} %get-tuple-element.35), channel_id=1, source_target_pairs={{0,64},{16,208},{32,96},{48,240},{64,128},{80,16},{96,160},{112,48... | collective-permute-start | bytes 147464 | tf_op jit(solution)/shard_map/ppermute | solution.py:53
  104.5 8.5 %collective-permute-start.22 = (bf16[8,1536]{1,0:T(8,128)(2,1)S(1)}, bf16[8,1536]{1,0:T(8,128)(2,1)S(1)}, u32[]{:S(2)}, u32[]{:S(2)}) collective-permute-start(bf16[8,1536]{1,0:T(8,128)(2,1)S(1)} %slice.108), channel_id=1, source_target_pairs={{0,128},{16,144},{32,160},{48,176},{64,192},{80,208},{96,224},{112... | collective-permute-start | bytes 73736 | tf_op jit(solution)/shard_map/ppermute | solution.py:53
  108.0 5.9 %collective-permute-start.26 = (bf16[8,1536]{1,0:T(8,128)(2,1)S(1)}, bf16[8,1536]{1,0:T(8,128)(2,1)S(1)}, u32[]{:S(2)}, u32[]{:S(2)}) collective-permute-start(bf16[8,1536]{1,0:T(8,128)(2,1)S(1)} %slice.148), channel_id=1, source_target_pairs={{0,16},{16,0},{32,48},{48,32},{64,80},{80,64},{96,112},{112,96},{1... | collective-permute-start | bytes 73736 | tf_op jit(solution)/shard_map/ppermute | solution.py:53

commit v3 on v2

--- a/solution.py
+++ b/solution.py
@@ -11,6 +11,7 @@
 EXPERTS = 8
 
 epsilon = 1e-05
+PART_WIDTH = 1536
 f32, bf16 = jnp.float32, jnp.bfloat16
 
 
@@ -35,7 +36,7 @@
     attended = jnp.einsum(
         "rhgl,rlhd->rhgd", weights_bf, value_blocks, preferred_element_type=f32
     )
-    return attended.reshape(row_count, kv_heads * query_group * HEAD_SIZE).astype(bf16)
+    return attended.reshape(row_count, kv_heads * query_group * HEAD_SIZE)
 
 
 def send(x, axes, target):
@@ -75,6 +76,48 @@
 CAPACITY_OF_512 = 384
 
 
+def finish_kernel(place, attended, residual, gain, ids, scores, stream, held):
+    rows, width = attended.shape
+    column = lax.broadcasted_iota(jnp.int32, (rows, held.shape[1] - width), 1)
+    share = scores[...] / jnp.sum(scores[...], axis=0, keepdims=True)
+    share, named = jnp.transpose(share), jnp.transpose(ids[...].astype(f32))
+    notes = jnp.zeros(column.shape, f32)
+    for k in range(named.shape[1]):
+        here = column.astype(f32) == named[:, k : k + 1]
+        notes = notes + jnp.where(here, share[:, k : k + 1], 0.0)
+    summed = residual[...].astype(f32) + attended[...].astype(bf16).astype(f32)
+    stream[...] = summed.astype(bf16)
+    raw = summed.astype(bf16).astype(f32)
+    mean = jnp.sum(raw, axis=1, keepdims=True) / width
+    centred = raw - mean
+    dev = jnp.sum(jnp.square(centred), axis=1, keepdims=True)
+    at = EXPERTS
+    for rest in (mean, dev):
+        for _ in range(3):
+            term = rest.astype(bf16).astype(f32)
+            notes = jnp.where(column == at, term, notes)
+            rest, at = rest - term, at + 1
+    own = gain[pl.ds(pl.multiple_of(place[0] * width, width), width)]
+    held[:, :width] = (centred * own.astype(f32).reshape(1, width)).astype(bf16)
+    held[:, width:] = notes.astype(bf16)
+
+
+def finish(place, attended, residual, gain, ids, scores):
+    whole = pl.BlockSpec(memory_space=VMEM)
+    rows, width = attended.shape
+    return pl.pallas_call(
+        finish_kernel,
+        out_shape=[
+            jax.ShapeDtypeStruct((rows, width), bf16),
+            jax.ShapeDtypeStruct((rows, width + 128), bf16),
+        ],
+        in_specs=[pl.BlockSpec(memory_space=SMEM)] + [whole] * 5,
+        out_specs=[whole] * 2,
+        compiler_params=pltpu.CompilerParams(vmem_limit_bytes=4 << 20),
+        cost_estimate=pl.CostEstimate(flops=1 << 16, bytes_accessed=1 << 16, transcendentals=0),
+    )(place, attended, residual, gain, ids, scores)
+
+
 def chosen(ranks, slots):
     slot = lax.broadcasted_iota(jnp.int32, (slots, ranks.shape[1]), 0)
     return (slot.astype(f32) == ranks).astype(bf16)
@@ -84,34 +127,39 @@
     *outs, share, ranks = outs
     y, first = place[0], place[1]
     experts, fan, n = gate_own.shape
-    units, slots = outs[0].shape[1], outs[0].shape[2]
+    slots, units = outs[0].shape[2], experts * fan // len(outs)
     rows, extra = 2 * n, own.shape[1]
-    route = jnp.concatenate([own[...], other[...]], axis=0)
-    named = (route.astype(f32) > 0.0).astype(bf16)
+    notes = jnp.concatenate([own[...], other[...]], axis=0).astype(f32)
+    named = notes > 0.0
     before = lax.broadcasted_iota(jnp.int32, (rows, rows), 1) <= lax.broadcasted_iota(
         jnp.int32, (rows, rows), 0
     )
-    counts = jnp.dot(before.astype(bf16), named, preferred_element_type=f32)
-    placed = jnp.where(named > 0, counts - 1.0, -1.0)
+    counts = jnp.dot(
+        before.astype(bf16), jnp.where(named, 1.0, 0.0).astype(bf16), preferred_element_type=f32
+    )
+    placed = jnp.where(named, counts - 1.0, -1.0)
     column = lax.broadcasted_iota(jnp.int32, (rows, extra), 1)
     slot = lax.broadcasted_iota(jnp.int32, (rows, slots), 1).astype(f32)
     ranks[...] = jnp.transpose(placed)
+    turned = jnp.transpose(notes)[: 2 * EXPERTS].astype(bf16)
+    line = lax.broadcasted_iota(jnp.int32, (2 * EXPERTS, slots), 0)
     for e in range(experts):
-        here = column == first + e
-        rank = jnp.sum(jnp.where(here, placed, 0.0), axis=1, keepdims=True)
+        rank = jnp.sum(jnp.where(column == first + e, placed, 0.0), axis=1, keepdims=True)
         onehot = (slot == rank).astype(bf16)
+        listed = jnp.dot(turned, onehot, preferred_element_type=f32)
+        stats = listed[EXPERTS:]
 
         @pl.when(y // (len(outs) // experts) == e)
         def _():
-            values = jnp.sum(jnp.where(here, route.astype(f32), 0.0), axis=1, keepdims=True)
-            values = jnp.sum(onehot.astype(f32) * values, axis=0, keepdims=True)
+            values = jnp.sum(jnp.where(line == first + e, listed, 0.0), axis=0, keepdims=True)
             share[...] = jnp.broadcast_to(values, share.shape)
 
         for g, (part_own, part_other) in enumerate(((gate_own, gate_other), (up_own, up_other))):
             packed = jnp.dot(part_own[e], onehot[:n], preferred_element_type=f32)
             packed = packed + jnp.dot(part_other[e], onehot[n:], preferred_element_type=f32)
             for h in range(fan // units):
-                part = packed[h * units : (h + 1) * units].astype(bf16)
+                part = jnp.concatenate([packed[h * units : (h + 1) * units], stats], axis=0)
+                part = part.astype(bf16)
                 step = lax.rem(e * (fan // units) + h + len(outs) - y, len(outs))
                 for k, out in enumerate(outs):
 
@@ -127,7 +175,7 @@
     whole = pl.BlockSpec(memory_space=VMEM)
     return pl.pallas_call(
         pack_kernel,
-        out_shape=[jax.ShapeDtypeStruct((2, experts * fan // parts, slots), bf16)] * parts
+        out_shape=[jax.ShapeDtypeStruct((2, experts * fan // parts + EXPERTS, slots), bf16)] * parts
         + [jax.ShapeDtypeStruct((8, slots), f32), jax.ShapeDtypeStruct((extra, rows), f32)],
         in_specs=[pl.BlockSpec(memory_space=SMEM)] + [whole] * 6,
         out_specs=[whole] * (parts + 2),
@@ -165,6 +213,44 @@
         compiler_params=pltpu.CompilerParams(vmem_limit_bytes=8 << 20),
         cost_estimate=pl.CostEstimate(flops=1, bytes_accessed=1 << 20, transcendentals=0),
     )(*pieces)
+
+
+def activate_kernel(part0, part1, part2, part3, gains, share, hidden):
+    parts = [[p[g].astype(f32) for g in range(2)] for p in (part0, part1, part2, part3)]
+    units, slots = hidden.shape
+    count = len(parts)
+    means, devs = [], []
+    for part in parts:
+        stats = part[0][units:]
+        means.append(stats[0:1] + stats[1:2] + stats[2:3])
+        devs.append(stats[3:4] + stats[4:5] + stats[5:6])
+    mean = sum(means) / count
+    var = sum(devs) / (count * PART_WIDTH)
+    var = var + sum(jnp.square(m - mean) for m in means) / count
+    scale = lax.rsqrt(var + epsilon)
+    columns = jnp.transpose(gains[...])
+
+    def total(g):
+        result = sum(part[g][:units] for part in parts)
+        for k in range(count):
+            result = result + columns[:, 2 * k + g : 2 * k + g + 1] * (means[k] - mean)
+        return result * scale
+
+    gate = total(0)
+    hidden[...] = (gate * jax.nn.sigmoid(gate) * total(1) * share[0:1]).astype(bf16)
+
+
+def activate(parts, gains, share):
+    whole = pl.BlockSpec(memory_space=VMEM)
+    units, slots = parts[0].shape[1] - EXPERTS, parts[0].shape[2]
+    return pl.pallas_call(
+        activate_kernel,
+        out_shape=jax.ShapeDtypeStruct((units, slots), bf16),
+        in_specs=[whole] * 6,
+        out_specs=whole,
+        compiler_params=pltpu.CompilerParams(vmem_limit_bytes=8 << 20),
+        cost_estimate=pl.CostEstimate(flops=1, bytes_accessed=1 << 20, transcendentals=1),
+    )(*parts, gains, share)
 
 
 def scatter_kernel(place, hidden0, hidden1, hidden2, hidden3, ranks, out):
@@ -203,28 +289,11 @@
     y, x = lax.axis_index("etp"), lax.axis_index("egrp")
     y_size = lax.axis_size("etp")
     attended = attend(queries, cache_keys, stored_values, lengths)
-    stream = (residual_in.astype(f32) + attended.astype(f32)).astype(bf16)
+    place = jnp.stack([y, x * w_gate.shape[0]]).astype(jnp.int32)
+    stream, held = finish(place, attended, residual_in, norm_gain, expert_ids.T, expert_scores.T)
     rows, width = stream.shape
-    shares = expert_scores / jnp.sum(expert_scores, axis=1, keepdims=True)
-    expert_iota = lax.broadcasted_iota(jnp.int32, (1, 1, EXPERTS), 2)
-    route = jnp.sum(
-        jnp.where(expert_ids[:, :, None] == expert_iota, shares[:, :, None], 0.0), axis=1
-    ).astype(bf16)
-
-    raw = stream.astype(f32)
-    part_mean = jnp.mean(raw, axis=1, keepdims=True)
-    part_dev = jnp.sum(jnp.square(raw - part_mean), axis=1, keepdims=True)
-    stats = jnp.concatenate([part_mean, part_dev], axis=1)
-    stats = [stats] + [to_y(stats, k) for k in range(1, y_size)]
-    mean = sum(s[:, :1] for s in stats) / y_size
-    dev = sum(s[:, 1:] + width * jnp.square(s[:, :1] - mean) for s in stats)
     gain = lax.dynamic_slice_in_dim(norm_gain, y * width, width, 0).astype(f32)
-    normed = (raw - mean) * lax.rsqrt(dev / (width * y_size) + epsilon) * gain[None, :]
-    held = jnp.concatenate(
-        [normed.astype(bf16), jnp.pad(route, ((0, 0), (0, 128 - EXPERTS)))], axis=1
-    )
-
-    place = jnp.stack([y, x * w_gate.shape[0]]).astype(jnp.int32)
+
     down = w_down.reshape(-1, width)
 
     def project(weight, tokens):
@@ -233,14 +302,23 @@
     across = along_z(held, 4)
     chip = jnp.concatenate([held, swap_core(held)], axis=0)
     held = jnp.concatenate([held, across] + [along_z(chip, k) for k in (1, 2, 3)], axis=0)
-    own, own_rows, own_routes = split([held] + [along_x(held, k) for k in range(3)], width, True)
-    other_rows, other_routes = split([swap_core(own)], width, False)
+    gain, held = lax.optimization_barrier((gain, held))
+    gains = jnp.stack(
+        [jnp.einsum("edf,d->ef", w.astype(f32), gain).reshape(y_size, -1) for w in (w_gate, w_up)]
+    )
+
+    def gain_block(k):
+        return lax.dynamic_index_in_dim(gains, lax.rem(y + k, y_size), 1, False)
+
+    gains = [gain_block(0)] + [to_y(gain_block(k), k) for k in range(1, y_size)]
+    pieces = [along_x(held, k) for k in range(3)]
+    pieces, gains = lax.optimization_barrier((pieces, jnp.concatenate(gains, axis=0)))
+    own, own_rows, own_notes = split([held] + pieces, width, True)
+    other_rows, other_notes = split([swap_core(own)], width, False)
     sums = [project(w, t) for w in (w_gate, w_up) for t in (own_rows, other_rows)]
-    *parts, share, ranks = pack(place, own_routes, other_routes, sums)
-    sums = parts[0].astype(f32) + sum(
-        to_y(part, k).astype(f32) for k, part in enumerate(parts) if k > 0
-    )
-    hidden = (jax.nn.silu(sums[0]) * sums[1] * share[:1]).astype(bf16)
+    *parts, share, ranks = pack(place, own_notes, other_notes, sums)
+    parts = [parts[0]] + [to_y(part, k) for k, part in enumerate(parts) if k > 0]
+    hidden = activate(parts, gains, share)
     hidden = scatter(place, [hidden] + [to_y(hidden, -k) for k in range(1, y_size)], ranks)
     hidden = hidden.reshape(down.shape[0], -1)
     n = own.shape[0]

time: 115 us -> 108 us (0.939)
  waiting for transfers between devices: 46.2 us -> 36.9 us
  matrix products: 9.88 us -> 12.4 us
  other arithmetic: 3.46 us -> 1.93 us
  starting transfers between devices: 46.1 us -> 47.5 us
    ppermute x27, waiting for transfers between devices: 46.2 us -> 36.9 us  [send(): return lax.ppermute(x, axes, pairs)]
    dot_general x0 -> x2, matrix products: none -> 2.96 us  [per_device(): jnp.einsum('edf,d->ef', w.astype(f32), gain).reshape(y_size, -1)]
    pallas_call x0 -> x2, Pallas kernels: none -> 1.72 us  [the longest x1 1.27 us: finish(): pl.pallas_call(finish_kernel, out_shape=[jax.ShapeDtypeStruct((rows, widt...]
    ppermute x27, starting transfers between devices: 46.1 us -> 47.5 us  [send(): return lax.ppermute(x, axes, pairs)]
    unnamed x23 -> x22, local copies, waits for them, and re-layouts: 2.48 us -> 1.57 us
  transfers between devices with their start and end apart: 27 -> 27, of which waited for: 16 -> 12; matrix products, arithmetic and copies ran while one was open for 4% -> 6% of each run, Pallas kernels for 0% -> 0%
where the time goes in v3:
time: 108 us
  starting transfers between devices  47.5 us (44%)
  waiting for transfers between devices  36.9 us (34%)
  matrix products  12.4 us (11%)
  Pallas kernels  5.99 us (6%)
  local copies, waits for them, and re-layouts  1.97 us (2%)
  other arithmetic  1.93 us (2%)
    ppermute x27, starting transfers between devices, send(): return lax.ppermute(x, axes, pairs)  47.5 us
    ppermute x27, waiting for transfers between devices, send(): return lax.ppermute(x, axes, pairs)  36.9 us
    dot_general x4, matrix products, project(): jnp.einsum('edf,rd->efr', weight, tokens, preferred_element_type=f32)  4.48 us
    pallas_call x1, Pallas kernels, pack(): pl.pallas_call(pack_kernel, out_shape=[jax.ShapeDtypeStruct((2, experts *...  2.98 us
    dot_general x2, matrix products, per_device(): jnp.einsum('edf,d->ef', w.astype(f32), gain).reshape(y_size, -1)  2.96 us
  transfers between devices with their start and end apart: 27, of which 12 were waited for; matrix products, arithmetic and copies ran while one was open for 6% of the time, Pallas kernels for 0%

profile of v3, /device:TPU:1, one launch (start us, length us, event | category | flops | bytes accessed | tf_op | source)
XLA Modules:
  0.0 107.7 jit_solution(128603507765926651)
XLA Ops:
  0.7 0.9 iota_compare_fusion
  1.5 0.7 copy-done
  2.2 1.4 %fusion.16 = f32[8,2,6,512]{3,2,1,0:T(8,128)S(1)} fusion(pred[8,512]{1,0:T(8,128)(4,1)S(1)} %iota_compare_fusion, bf16[8,2,6,128]{3,0,2,1:T(8,128)(2,1)} %bitcast.75, bf16[8,512,256]{2,1,0:T(8,128)(2,1)S(1)} %copy-done), kind=kOutput, calls=%fused_computation.20 | convolution fusion | flops 12681216 | bytes 2322432 | tf_op jit(solution)/shard_map/rhgd,rlhd->rhgl/dot_general | solution.py:26
  3.9 2.0 %fusion.1 = f32[8,2,6,128]{3,2,1,0:T(8,128)S(1)} fusion(f32[8,2,6]{2,1,0:T(2,128)S(1)} %fusion.40, f32[8,2,6,512]{3,2,1,0:T(8,128)S(1)} %fusion.16, bf16[8,512,256]{2,1,0:T(8,128)(2,1)} %param.13), kind=kOutput, calls=%fused_computation.3 | convolution fusion | flops 12730975 | bytes 2343296 | tf_op jit(solution)/shard_map/rhgl,rlhd->rhgd/dot_general | solution.py:36
  6.0 1.3 %shard_map.122 = (bf16[8,1536]{1,0:T(8,128)(2,1)}, bf16[8,1664]{1,0:T(8,128)(2,1)S(1)}) custom-call(s32[2]{0:T(128)S(1)} %pad_add_fusion.place, f32[8,1536]{1,0:T(8,128)S(1)} %reshape.48.attended, bf16[8,1536]{1,0:T(8,128)(2,1)S(1)} %copy-done.1, bf16[6144]{0:T(1024)(128)(2,1)S(1)} %copy-done.2, s32[4,8]{1,0:T(4,128)S(1)} %bitcast.71, f32[4,8]{1,0:T(4,128)S(1)} %bitcast.72), custom_call_target="tpu_custom_call" | custom-call | flops 65536 | bytes 65536 | tf_op jit(solution)/shard_map/pallas_call | solution.py:108
  7.3 3.2 %collective-permute-start.1 = (bf16[8,1664]{1,0:T(8,128)(2,1)S(1)}, bf16[8,1664]{1,0:T(8,128)(2,1)S(1)}, u32[]{:S(2)}, u32[]{:S(2)}) collective-permute-start(bf16[8,1664]{1,0:T(8,128)(2,1)S(1)} %get-tuple-element.22), channel_id=1, source_target_pairs={{0,16},{16,0},{32,48},{48,32},{64,80},{80,64},{96,112},{112,96},{1... | collective-permute-start | bytes 79880 | tf_op jit(solution)/shard_map/ppermute | solution.py:54
  10.6 5.2 %collective-permute-start = (bf16[8,1664]{1,0:T(8,128)(2,1)S(1)}, bf16[8,1664]{1,0:T(8,128)(2,1)S(1)}, u32[]{:S(2)}, u32[]{:S(2)}) collective-permute-start(bf16[8,1664]{1,0:T(8,128)(2,1)S(1)} %get-tuple-element.22), channel_id=1, source_target_pairs={{0,128},{16,144},{32,160},{48,176},{64,192},{80,208},{96,224},{112... | collective-permute-start | bytes 79880 | tf_op jit(solution)/shard_map/ppermute | solution.py:54
  15.8 1.7 %collective-permute-start.4 = (bf16[16,1664]{1,0:T(8,128)(2,1)S(1)}, bf16[16,1664]{1,0:T(8,128)(2,1)S(1)}, u32[]{:S(2)}, u32[]{:S(2)}) collective-permute-start(bf16[16,1664]{1,0:T(8,128)(2,1)S(1)} %constant_dynamic-update-slice_fusion), channel_id=1, source_target_pairs={{0,160},{16,112},{32,192},{48,144},{64,224},{80,176},{96,0},{112,2... | collective-permute-start | bytes 159752 | tf_op jit(solution)/shard_map/ppermute | solution.py:54
  18.1 5.8 %collective-permute-done.2 = bf16[16,1664]{1,0:T(8,128)(2,1)S(1)} collective-permute-done((bf16[16,1664]{1,0:T(8,128)(2,1)S(1)}, bf16[16,1664]{1,0:T(8,128)(2,1)S(1)}, u32[]{:S(2)}, u32[]{:S(2)}) %collective-permute-start.2) | collective-permute-done | bytes 53280 | tf_op jit(solution)/shard_map/ppermute | solution.py:54
  23.9 2.8 %collective-permute-start.7 = (bf16[64,1664]{1,0:T(8,128)(2,1)S(1)}, bf16[64,1664]{1,0:T(8,128)(2,1)S(1)}, u32[]{:S(2)}, u32[]{:S(2)}) collective-permute-start(bf16[64,1664]{1,0:T(8,128)(2,1)S(1)} %constant_dynamic-update-slice_fusion.2.refs_0_), channel_id=1, source_target_pairs={{0,8},{4,12},{8,0},{12,4},{16,24},{20,28},{24,16},{28,20},{32,40},... | collective-permute-start | bytes 638984 | tf_op jit(solution)/shard_map/ppermute | solution.py:54
  27.1 0.6 collective-permute-start.5
  27.6 2.2 %fusion.43 = f32[1,2,336]{2,0,1:T(1,128)S(1)} fusion(bf16[1536,1,1]{0,1,2:T(2,128)(2,1)S(1)} %reshape.51, bf16[2,1536,336]{1,2,0:T(8,128)(2,1)} %param.20), kind=kOutput, calls=%fused_computation.72 | convolution fusion | flops 2064384 | bytes 2070144 | tf_op jit(solution)/shard_map/edf,d->ef/dot_general | solution.py:307
  29.9 0.7 fusion.42
  30.8 1.4 %collective-permute-start.8 = (f32[2,168]{1,0:T(2,128)S(1)}, f32[2,168]{1,0:T(2,128)S(1)}, u32[]{:S(2)}, u32[]{:S(2)}) collective-permute-start(f32[2,168]{1,0:T(2,128)S(1)} %get-tuple-element.51), channel_id=1, source_target_pairs={{0,1},{1,2},{2,3},{3,0},{4,5},{5,6},{6,7},{7,4},{8,9},{9,10},{10,1... | collective-permute-start | bytes 4040 | tf_op jit(solution)/shard_map/ppermute | solution.py:54
  32.2 2.6 %collective-permute-start.9 = (f32[2,168]{1,0:T(2,128)S(1)}, f32[2,168]{1,0:T(2,128)S(1)}, u32[]{:S(2)}, u32[]{:S(2)}) collective-permute-start(f32[2,168]{1,0:T(2,128)S(1)} %get-tuple-element.52), channel_id=1, source_target_pairs={{0,2},{1,3},{2,0},{3,1},{4,6},{5,7},{6,4},{7,5},{8,10},{9,11},{10,... | collective-permute-start | bytes 4040 | tf_op jit(solution)/shard_map/ppermute | solution.py:54
  34.9 1.5 %collective-permute-start.10 = (f32[2,168]{1,0:T(2,128)S(1)}, f32[2,168]{1,0:T(2,128)S(1)}, u32[]{:S(2)}, u32[]{:S(2)}) collective-permute-start(f32[2,168]{1,0:T(2,128)S(1)} %get-tuple-element.53), channel_id=1, source_target_pairs={{0,3},{1,0},{2,1},{3,2},{4,7},{5,4},{6,5},{7,6},{8,11},{9,8},{10,9... | collective-permute-start | bytes 4040 | tf_op jit(solution)/shard_map/ppermute | solution.py:54
  36.4 1.1 %collective-permute-done.10 = f32[2,168]{1,0:T(2,128)S(1)} collective-permute-done((f32[2,168]{1,0:T(2,128)S(1)}, f32[2,168]{1,0:T(2,128)S(1)}, u32[]{:S(2)}, u32[]{:S(2)}) %collective-permute-start.10) | collective-permute-done | bytes 1376 | tf_op jit(solution)/shard_map/ppermute | solution.py:54
  37.7 3.5 %collective-permute-start.11 = (bf16[256,1664]{1,0:T(8,128)(2,1)S(1)}, bf16[256,1664]{1,0:T(8,128)(2,1)S(1)}, u32[]{:S(2)}, u32[]{:S(2)}) collective-permute-start(bf16[256,1664]{1,0:T(8,128)(2,1)S(1)} %get-tuple-element.29), channel_id=1, source_target_pairs={{0,16},{16,0},{32,48},{48,32},{64,80},{80,64},{96,112},{112,96},{1... | collective-permute-start | bytes 2555912 | tf_op jit(solution)/shard_map/ppermute | solution.py:54
  41.2 2.3 %fusion.10.up_own = bf16[2,336,256]{2,1,0:T(8,128)(2,1)S(1)} fusion(bf16[2,1536,336]{1,2,0:T(8,128)(2,1)} %param.20, bf16[256,1536]{1,0:T(8,128)(2,1)S(1)} %get-tuple-element.31), kind=kOutput, calls=%fused_computation.16 | convolution fusion | flops 528654336 | bytes 3194880 | tf_op jit(solution)/shard_map/edf,rd->efr/dot_general | solution.py:300
  43.5 0.7 fusion.8.gate_own
  44.3 0.8 copy-done.6
  45.1 0.7 fusion.11.up_other
  45.8 0.7 fusion.9.gate_other
  46.6 3.0 %shard_map.125 = (bf16[2,176,384]{2,1,0:T(8,128)(2,1)S(1)}, bf16[2,176,384]{2,1,0:T(8,128)(2,1)S(1)}, bf16[2,176,384]{2,1,0:T(8,128)(2,1)S(1)}, bf16[2,176,384]{...) custom-call(s32[2]{0:T(128)S(1)} %pad_add_fusion.place, ...), custom_call_target="tpu_custom_call" | custom-call | flops 536870912 | bytes 2097152 | tf_op jit(solution)/shard_map/pallas_call | solution.py:176
  49.7 3.8 %collective-permute-start.13 = (bf16[2,176,384]{2,1,0:T(8,128)(2,1)S(1)}, bf16[2,176,384]{2,1,0:T(8,128)(2,1)S(1)}, u32[]{:S(2)}, u32[]{:S(2)}) collective-permute-start(bf16[2,176,384]{2,1,0:T(8,128)(2,1)S(1)} %get-tuple-element.35), channel_id=1, source_target_pairs={{0,2},{1,3},{2,0},{3,1},{4,6},{5,7},{6,4},{7,5},{8,10},{9,11},{10,... | collective-permute-start | bytes 811016 | tf_op jit(solution)/shard_map/ppermute | solution.py:54
  53.5 5.4 %collective-permute-done.12.part1 = bf16[2,176,384]{2,1,0:T(8,128)(2,1)S(1)} collective-permute-done((bf16[2,176,384]{2,1,0:T(8,128)(2,1)S(1)}, bf16[2,176,384]{2,1,0:T(8,128)(2,1)S(1)}, u32[]{:S(2)}, u32[]{:S(2)}) %collective-permute-start.12) | collective-permute-done | bytes 270368 | tf_op jit(solution)/shard_map/ppermute | solution.py:54
  58.9 6.9 %collective-permute-done.13.part2 = bf16[2,176,384]{2,1,0:T(8,128)(2,1)S(1)} collective-permute-done((bf16[2,176,384]{2,1,0:T(8,128)(2,1)S(1)}, bf16[2,176,384]{2,1,0:T(8,128)(2,1)S(1)}, u32[]{:S(2)}, u32[]{:S(2)}) %collective-permute-start.13) | collective-permute-done | bytes 270368 | tf_op jit(solution)/shard_map/ppermute | solution.py:54
  66.3 1.0 collective-permute-start.17
  67.2 2.6 %collective-permute-start.16 = (bf16[168,384]{1,0:T(8,128)(2,1)S(1)}, bf16[168,384]{1,0:T(8,128)(2,1)S(1)}, u32[]{:S(2)}, u32[]{:S(2)}) collective-permute-start(bf16[168,384]{1,0:T(8,128)(2,1)S(1)} %shard_map.126.hidden0), channel_id=1, source_target_pairs={{0,2},{1,3},{2,0},{3,1},{4,6},{5,7},{6,4},{7,5},{8,10},{9,11},{10,... | collective-permute-start | bytes 387080 | tf_op jit(solution)/shard_map/ppermute | solution.py:54
  69.9 1.5 %collective-permute-done.17.hidden3 = bf16[168,384]{1,0:T(8,128)(2,1)S(1)} collective-permute-done((bf16[168,384]{1,0:T(8,128)(2,1)S(1)}, bf16[168,384]{1,0:T(8,128)(2,1)S(1)}, u32[]{:S(2)}, u32[]{:S(2)}) %collective-permute-start.17) | collective-permute-done | bytes 129056 | tf_op jit(solution)/shard_map/ppermute | solution.py:54
  71.3 4.4 %collective-permute-done.16.hidden2 = bf16[168,384]{1,0:T(8,128)(2,1)S(1)} collective-permute-done((bf16[168,384]{1,0:T(8,128)(2,1)S(1)}, bf16[168,384]{1,0:T(8,128)(2,1)S(1)}, u32[]{:S(2)}, u32[]{:S(2)}) %collective-permute-start.16) | collective-permute-done | bytes 129056 | tf_op jit(solution)/shard_map/ppermute | solution.py:54
  75.7 1.1 %shard_map.127 = bf16[4,168,512]{2,1,0:T(8,128)(2,1)S(1)} custom-call(s32[2]{0:T(128)S(1)} %pad_add_fusion.place, bf16[168,384]{1,0:T(8,128)(2,1)S(1)} %shard_map.126.hidden0, bf16[168,384]{1,0:T(8,128)(2,1)S(1)} %collective-permute-done.15.hidden1, bf16[168,384]{1,0:T(8,128)(2,1)S(1)} %collective-permute-done.16.hidden2, ...), custom_call_target="tpu_custom_call" | custom-call | flops 268435456 | bytes 1048576 | tf_op jit(solution)/shard_map/pallas_call | solution.py:266
  76.8 0.8 convolution_convert_fusion
  77.6 1.5 %collective-permute-start.18 = (bf16[256,1536]{1,0:T(8,128)(2,1)S(1)}, bf16[256,1536]{1,0:T(8,128)(2,1)S(1)}, u32[]{:S(2)}, u32[]{:S(2)}) collective-permute-start(bf16[256,1536]{1,0:T(8,128)(2,1)S(1)} %convolution_convert_fusion), channel_id=1, source_target_pairs={{0,16},{16,0},{32,48},{48,32},{64,80},{80,64},{96,112},{112,96},{1... | collective-permute-start | bytes 2359304 | tf_op jit(solution)/shard_map/ppermute | solution.py:54
  79.1 1.9 %collective-permute-done.18 = bf16[256,1536]{1,0:T(8,128)(2,1)S(1)} collective-permute-done((bf16[256,1536]{1,0:T(8,128)(2,1)S(1)}, bf16[256,1536]{1,0:T(8,128)(2,1)S(1)}, u32[]{:S(2)}, u32[]{:S(2)}) %collective-permute-start.18) | collective-permute-done | bytes 786464 | tf_op jit(solution)/shard_map/ppermute | solution.py:54
  81.0 0.8 fusion.41
  81.8 1.9 %collective-permute-start.19 = (bf16[64,1536]{1,0:T(8,128)(2,1)S(1)}, bf16[64,1536]{1,0:T(8,128)(2,1)S(1)}, u32[]{:S(2)}, u32[]{:S(2)}) collective-permute-start(bf16[64,1536]{1,0:T(8,128)(2,1)S(1)} %get-tuple-element.42), channel_id=1, source_target_pairs={{0,4},{4,0},{8,12},{12,8},{16,28},{20,24},{24,20},{28,16},{32,36},... | collective-permute-start | bytes 589832 | tf_op jit(solution)/shard_map/ppermute | solution.py:54
  83.7 1.7 %collective-permute-start.21 = (bf16[64,1536]{1,0:T(8,128)(2,1)S(1)}, bf16[64,1536]{1,0:T(8,128)(2,1)S(1)}, u32[]{:S(2)}, u32[]{:S(2)}) collective-permute-start(bf16[64,1536]{1,0:T(8,128)(2,1)S(1)} %get-tuple-element.43), channel_id=1, source_target_pairs={{0,8},{4,12},{8,0},{12,4},{16,24},{20,28},{24,16},{28,20},{32,40},... | collective-permute-start | bytes 589832 | tf_op jit(solution)/shard_map/ppermute | solution.py:54
  85.5 2.2 %collective-permute-done.19 = bf16[64,1536]{1,0:T(8,128)(2,1)S(1)} collective-permute-done((bf16[64,1536]{1,0:T(8,128)(2,1)S(1)}, bf16[64,1536]{1,0:T(8,128)(2,1)S(1)}, u32[]{:S(2)}, u32[]{:S(2)}) %collective-permute-start.19) | collective-permute-done | bytes 196640 | tf_op jit(solution)/shard_map/ppermute | solution.py:54
  87.7 4.5 %collective-permute-done.21 = bf16[64,1536]{1,0:T(8,128)(2,1)S(1)} collective-permute-done((bf16[64,1536]{1,0:T(8,128)(2,1)S(1)}, bf16[64,1536]{1,0:T(8,128)(2,1)S(1)}, u32[]{:S(2)}, u32[]{:S(2)}) %collective-permute-start.21) | collective-permute-done | bytes 196640 | tf_op jit(solution)/shard_map/ppermute | solution.py:54
  92.2 1.7 %collective-permute-done.20 = bf16[64,1536]{1,0:T(8,128)(2,1)S(1)} collective-permute-done((bf16[64,1536]{1,0:T(8,128)(2,1)S(1)}, bf16[64,1536]{1,0:T(8,128)(2,1)S(1)}, u32[]{:S(2)}, u32[]{:S(2)}) %collective-permute-start.20) | collective-permute-done | bytes 196640 | tf_op jit(solution)/shard_map/ppermute | solution.py:54
  94.0 2.0 %collective-permute-start.23 = (bf16[16,1536]{1,0:T(8,128)(2,1)S(1)}, bf16[16,1536]{1,0:T(8,128)(2,1)S(1)}, u32[]{:S(2)}, u32[]{:S(2)}) collective-permute-start(bf16[16,1536]{1,0:T(8,128)(2,1)S(1)} %get-tuple-element.45), channel_id=1, source_target_pairs={{0,32},{16,240},{32,64},{48,16},{64,96},{80,48},{96,128},{112,80},... | collective-permute-start | bytes 147464 | tf_op jit(solution)/shard_map/ppermute | solution.py:54
  96.0 0.7 collective-permute-start.25
  96.8 2.3 %collective-permute-start.24 = (bf16[16,1536]{1,0:T(8,128)(2,1)S(1)}, bf16[16,1536]{1,0:T(8,128)(2,1)S(1)}, u32[]{:S(2)}, u32[]{:S(2)}) collective-permute-start(bf16[16,1536]{1,0:T(8,128)(2,1)S(1)} %get-tuple-element.47), channel_id=1, source_target_pairs={{0,64},{16,208},{32,96},{48,240},{64,128},{80,16},{96,160},{112,48... | collective-permute-start | bytes 147464 | tf_op jit(solution)/shard_map/ppermute | solution.py:54
  99.1 2.5 %collective-permute-start.22 = (bf16[8,1536]{1,0:T(8,128)(2,1)S(1)}, bf16[8,1536]{1,0:T(8,128)(2,1)S(1)}, u32[]{:S(2)}, u32[]{:S(2)}) collective-permute-start(bf16[8,1536]{1,0:T(8,128)(2,1)S(1)} %slice.67), channel_id=1, source_target_pairs={{0,128},{16,144},{32,160},{48,176},{64,192},{80,208},{96,224},{112... | collective-permute-start | bytes 73736 | tf_op jit(solution)/shard_map/ppermute | solution.py:54
  101.6 4.0 %collective-permute-start.26 = (bf16[8,1536]{1,0:T(8,128)(2,1)S(1)}, bf16[8,1536]{1,0:T(8,128)(2,1)S(1)}, u32[]{:S(2)}, u32[]{:S(2)}) collective-permute-start(bf16[8,1536]{1,0:T(8,128)(2,1)S(1)} %slice.87), channel_id=1, source_target_pairs={{0,16},{16,0},{32,48},{48,32},{64,80},{80,64},{96,112},{112,96},{1... | collective-permute-start | bytes 73736 | tf_op jit(solution)/shard_map/ppermute | solution.py:54
  105.6 1.4 %collective-permute-done.22 = bf16[8,1536]{1,0:T(8,128)(2,1)S(1)} collective-permute-done((bf16[8,1536]{1,0:T(8,128)(2,1)S(1)}, bf16[8,1536]{1,0:T(8,128)(2,1)S(1)}, u32[]{:S(2)}, u32[]{:S(2)}) %collective-permute-start.22) | collective-permute-done | bytes 24608 | tf_op jit(solution)/shard_map/ppermute | solution.py:54
  107.0 0.6 fusion.27
  (65 shorter events, 2.7 us)
Async XLA Ops:
  0.6 1.6 %copy-start = (bf16[8,512,256]{2,1,0:T(8,128)(2,1)S(1)}, bf16[8,512,256]{2,1,0:T(8,128)(2,1)}, u32[]{:S(2)}) copy-start(bf16[8,512,256]{2,1,0:T(8,128)(2,1)} %param.12) | copy-start | bytes 6291460
  3.6 2.4 %copy-start.1 = (bf16[8,1536]{1,0:T(8,128)(2,1)S(1)}, bf16[8,1536]{1,0:T(8,128)(2,1)}, u32[]{:S(2)}) copy-start(bf16[8,1536]{1,0:T(8,128)(2,1)} %residual.1) | copy-start | bytes 73732
  3.6 2.4 %copy-start.2 = (bf16[6144]{0:T(1024)(128)(2,1)S(1)}, bf16[6144]{0:T(1024)(128)(2,1)}, u32[]{:S(2)}) copy-start(bf16[6144]{0:T(1024)(128)(2,1)} %gain.1) | copy-start | bytes 36868
  3.6 2.4 %copy-start.3 = (s32[8,4]{0,1:T(4,128)S(1)}, s32[8,4]{0,1:T(4,128)}, u32[]{:S(2)}) copy-start(s32[8,4]{0,1:T(4,128)} %param.17) | copy-start | bytes 388
  3.6 2.4 %copy-start.4 = (f32[8,4]{0,1:T(4,128)S(1)}, f32[8,4]{0,1:T(4,128)}, u32[]{:S(2)}) copy-start(f32[8,4]{0,1:T(4,128)} %param.18) | copy-start | bytes 388
  7.3 8.5 %collective-permute-start.1 = (bf16[8,1664]{1,0:T(8,128)(2,1)S(1)}, bf16[8,1664]{1,0:T(8,128)(2,1)S(1)}, u32[]{:S(2)}, u32[]{:S(2)}) collective-permute-start(bf16[8,1664]{1,0:T(8,128)(2,1)S(1)} %get-tuple-element.22), channel_id=1, source_target_pairs={{0,16},{16,0},{32,48},{48,32},{64,80},{80,64},{96,112},{112,96},{1... | collective-permute-start | bytes 79880 | tf_op jit(solution)/shard_map/ppermute | solution.py:54
  10.6 7.5 %collective-permute-start = (bf16[8,1664]{1,0:T(8,128)(2,1)S(1)}, bf16[8,1664]{1,0:T(8,128)(2,1)S(1)}, u32[]{:S(2)}, u32[]{:S(2)}) collective-permute-start(bf16[8,1664]{1,0:T(8,128)(2,1)S(1)} %get-tuple-element.22), channel_id=1, source_target_pairs={{0,128},{16,144},{32,160},{48,176},{64,192},{80,208},{96,224},{112... | collective-permute-start | bytes 79880 | tf_op jit(solution)/shard_map/ppermute | solution.py:54
  15.8 14.1 %copy-start.7 = (bf16[2,1536,336]{1,2,0:T(8,128)(2,1)S(1)}, bf16[2,1536,336]{1,2,0:T(8,128)(2,1)}, u32[]{:S(2)}) copy-start(bf16[2,1536,336]{1,2,0:T(8,128)(2,1)} %param.19) | copy-start | bytes 6193156
  15.8 8.1 %collective-permute-start.4 = (bf16[16,1664]{1,0:T(8,128)(2,1)S(1)}, bf16[16,1664]{1,0:T(8,128)(2,1)S(1)}, u32[]{:S(2)}, u32[]{:S(2)}) collective-permute-start(bf16[16,1664]{1,0:T(8,128)(2,1)S(1)} %constant_dynamic-update-slice_fusion), channel_id=1, source_target_pairs={{0,160},{16,112},{32,192},{48,144},{64,224},{80,176},{96,0},{112,2... | collective-permute-start | bytes 159752 | tf_op jit(solution)/shard_map/ppermute | solution.py:54
  17.6 6.3 %collective-permute-start.3 = (bf16[16,1664]{1,0:T(8,128)(2,1)S(1)}, bf16[16,1664]{1,0:T(8,128)(2,1)S(1)}, u32[]{:S(2)}, u32[]{:S(2)}) collective-permute-start(bf16[16,1664]{1,0:T(8,128)(2,1)S(1)} %constant_dynamic-update-slice_fusion), channel_id=1, source_target_pairs={{0,192},{16,80},{32,224},{48,112},{64,0},{80,144},{96,32},{112,176... | collective-permute-start | bytes 159752 | tf_op jit(solution)/shard_map/ppermute | solution.py:54
  17.6 6.3 %collective-permute-start.2 = (bf16[16,1664]{1,0:T(8,128)(2,1)S(1)}, bf16[16,1664]{1,0:T(8,128)(2,1)S(1)}, u32[]{:S(2)}, u32[]{:S(2)}) collective-permute-start(bf16[16,1664]{1,0:T(8,128)(2,1)S(1)} %constant_dynamic-update-slice_fusion), channel_id=1, source_target_pairs={{0,224},{16,48},{32,0},{48,80},{64,32},{80,112},{96,64},{112,144},... | collective-permute-start | bytes 159752 | tf_op jit(solution)/shard_map/ppermute | solution.py:54
  23.9 13.6 %collective-permute-start.7 = (bf16[64,1664]{1,0:T(8,128)(2,1)S(1)}, bf16[64,1664]{1,0:T(8,128)(2,1)S(1)}, u32[]{:S(2)}, u32[]{:S(2)}) collective-permute-start(bf16[64,1664]{1,0:T(8,128)(2,1)S(1)} %constant_dynamic-update-slice_fusion.2.refs_0_), channel_id=1, source_target_pairs={{0,8},{4,12},{8,0},{12,4},{16,24},{20,28},{24,16},{28,20},{32,40},... | collective-permute-start | bytes 638984 | tf_op jit(solution)/shard_map/ppermute | solution.py:54
  26.8 10.8 %collective-permute-start.6 = (bf16[64,1664]{1,0:T(8,128)(2,1)S(1)}, bf16[64,1664]{1,0:T(8,128)(2,1)S(1)}, u32[]{:S(2)}, u32[]{:S(2)}) collective-permute-start(bf16[64,1664]{1,0:T(8,128)(2,1)S(1)} %constant_dynamic-update-slice_fusion.2.refs_0_), channel_id=1, source_target_pairs={{0,12},{4,8},{8,4},{12,0},{16,20},{20,16},{24,28},{28,24},{32,44},... | collective-permute-start | bytes 638984 | tf_op jit(solution)/shard_map/ppermute | solution.py:54
  27.1 10.5 %collective-permute-start.5 = (bf16[64,1664]{1,0:T(8,128)(2,1)S(1)}, bf16[64,1664]{1,0:T(8,128)(2,1)S(1)}, u32[]{:S(2)}, u32[]{:S(2)}) collective-permute-start(bf16[64,1664]{1,0:T(8,128)(2,1)S(1)} %constant_dynamic-update-slice_fusion.2.refs_0_), channel_id=1, source_target_pairs={{0,4},{4,0},{8,12},{12,8},{16,28},{20,24},{24,20},{28,16},{32,36},... | collective-permute-start | bytes 638984 | tf_op jit(solution)/shard_map/ppermute | solution.py:54
  30.8 4.1 %collective-permute-start.8 = (f32[2,168]{1,0:T(2,128)S(1)}, f32[2,168]{1,0:T(2,128)S(1)}, u32[]{:S(2)}, u32[]{:S(2)}) collective-permute-start(f32[2,168]{1,0:T(2,128)S(1)} %get-tuple-element.51), channel_id=1, source_target_pairs={{0,1},{1,2},{2,3},{3,0},{4,5},{5,6},{6,7},{7,4},{8,9},{9,10},{10,1... | collective-permute-start | bytes 4040 | tf_op jit(solution)/shard_map/ppermute | solution.py:54
  32.2 4.2 %collective-permute-start.9 = (f32[2,168]{1,0:T(2,128)S(1)}, f32[2,168]{1,0:T(2,128)S(1)}, u32[]{:S(2)}, u32[]{:S(2)}) collective-permute-start(f32[2,168]{1,0:T(2,128)S(1)} %get-tuple-element.52), channel_id=1, source_target_pairs={{0,2},{1,3},{2,0},{3,1},{4,6},{5,7},{6,4},{7,5},{8,10},{9,11},{10,... | collective-permute-start | bytes 4040 | tf_op jit(solution)/shard_map/ppermute | solution.py:54
  34.9 2.6 %collective-permute-start.10 = (f32[2,168]{1,0:T(2,128)S(1)}, f32[2,168]{1,0:T(2,128)S(1)}, u32[]{:S(2)}, u32[]{:S(2)}) collective-permute-start(f32[2,168]{1,0:T(2,128)S(1)} %get-tuple-element.53), channel_id=1, source_target_pairs={{0,3},{1,0},{2,1},{3,2},{4,7},{5,4},{6,5},{7,6},{8,11},{9,8},{10,9... | collective-permute-start | bytes 4040 | tf_op jit(solution)/shard_map/ppermute | solution.py:54
  37.5 6.0 %copy-start.8 = (bf16[2,1536,336]{1,2,0:T(8,128)(2,1)S(1)}, bf16[2,1536,336]{1,2,0:T(8,128)(2,1)}, u32[]{:S(2)}) copy-start(bf16[2,1536,336]{1,2,0:T(8,128)(2,1)} %param.19) | copy-start | bytes 6193156
  37.7 6.6 %collective-permute-start.11 = (bf16[256,1664]{1,0:T(8,128)(2,1)S(1)}, bf16[256,1664]{1,0:T(8,128)(2,1)S(1)}, u32[]{:S(2)}, u32[]{:S(2)}) collective-permute-start(bf16[256,1664]{1,0:T(8,128)(2,1)S(1)} %get-tuple-element.29), channel_id=1, source_target_pairs={{0,16},{16,0},{32,48},{48,32},{64,80},{80,64},{96,112},{112,96},{1... | collective-permute-start | bytes 2555912 | tf_op jit(solution)/shard_map/ppermute | solution.py:54
  43.5 1.6 %copy-start.6 = (bf16[2,1536,336]{1,2,0:T(8,128)(2,1)S(1)}, bf16[2,1536,336]{1,2,0:T(8,128)(2,1)}, u32[]{:S(2)}) copy-start(bf16[2,1536,336]{1,2,0:T(8,128)(2,1)} %param.20) | copy-start | bytes 6193156
  46.5 30.3 %copy-start.5 = (bf16[2,336,1536]{2,1,0:T(8,128)(2,1)S(1)}, bf16[2,336,1536]{2,1,0:T(8,128)(2,1)}, u32[]{:S(2)}) copy-start(bf16[2,336,1536]{2,1,0:T(8,128)(2,1)} %param.21) | copy-start | bytes 6193156
  49.5 9.3 %collective-permute-start.12 = (bf16[2,176,384]{2,1,0:T(8,128)(2,1)S(1)}, bf16[2,176,384]{2,1,0:T(8,128)(2,1)S(1)}, u32[]{:S(2)}, u32[]{:S(2)}) collective-permute-start(bf16[2,176,384]{2,1,0:T(8,128)(2,1)S(1)} %get-tuple-element.34), channel_id=1, source_target_pairs={{0,1},{1,2},{2,3},{3,0},{4,5},{5,6},{6,7},{7,4},{8,9},{9,10},{10,1... | collective-permute-start | bytes 811016 | tf_op jit(solution)/shard_map/ppermute | solution.py:54
  49.7 16.1 %collective-permute-start.13 = (bf16[2,176,384]{2,1,0:T(8,128)(2,1)S(1)}, bf16[2,176,384]{2,1,0:T(8,128)(2,1)S(1)}, u32[]{:S(2)}, u32[]{:S(2)}) collective-permute-start(bf16[2,176,384]{2,1,0:T(8,128)(2,1)S(1)} %get-tuple-element.35), channel_id=1, source_target_pairs={{0,2},{1,3},{2,0},{3,1},{4,6},{5,7},{6,4},{7,5},{8,10},{9,11},{10,... | collective-permute-start | bytes 811016 | tf_op jit(solution)/shard_map/ppermute | solution.py:54
  53.5 12.3 %collective-permute-start.14 = (bf16[2,176,384]{2,1,0:T(8,128)(2,1)S(1)}, bf16[2,176,384]{2,1,0:T(8,128)(2,1)S(1)}, u32[]{:S(2)}, u32[]{:S(2)}) collective-permute-start(bf16[2,176,384]{2,1,0:T(8,128)(2,1)S(1)} %get-tuple-element.36), channel_id=1, source_target_pairs={{0,3},{1,0},{2,1},{3,2},{4,7},{5,4},{6,5},{7,6},{8,11},{9,8},{10,9... | collective-permute-start | bytes 811016 | tf_op jit(solution)/shard_map/ppermute | solution.py:54
  66.3 5.1 %collective-permute-start.17 = (bf16[168,384]{1,0:T(8,128)(2,1)S(1)}, bf16[168,384]{1,0:T(8,128)(2,1)S(1)}, u32[]{:S(2)}, u32[]{:S(2)}) collective-permute-start(bf16[168,384]{1,0:T(8,128)(2,1)S(1)} %shard_map.126.hidden0), channel_id=1, source_target_pairs={{0,1},{1,2},{2,3},{3,0},{4,5},{5,6},{6,7},{7,4},{8,9},{9,10},{10,1... | collective-permute-start | bytes 387080 | tf_op jit(solution)/shard_map/ppermute | solution.py:54
  67.2 8.5 %collective-permute-start.16 = (bf16[168,384]{1,0:T(8,128)(2,1)S(1)}, bf16[168,384]{1,0:T(8,128)(2,1)S(1)}, u32[]{:S(2)}, u32[]{:S(2)}) collective-permute-start(bf16[168,384]{1,0:T(8,128)(2,1)S(1)} %shard_map.126.hidden0), channel_id=1, source_target_pairs={{0,2},{1,3},{2,0},{3,1},{4,6},{5,7},{6,4},{7,5},{8,10},{9,11},{10,... | collective-permute-start | bytes 387080 | tf_op jit(solution)/shard_map/ppermute | solution.py:54
  69.9 5.8 %collective-permute-start.15 = (bf16[168,384]{1,0:T(8,128)(2,1)S(1)}, bf16[168,384]{1,0:T(8,128)(2,1)S(1)}, u32[]{:S(2)}, u32[]{:S(2)}) collective-permute-start(bf16[168,384]{1,0:T(8,128)(2,1)S(1)} %shard_map.126.hidden0), channel_id=1, source_target_pairs={{0,3},{1,0},{2,1},{3,2},{4,7},{5,4},{6,5},{7,6},{8,11},{9,8},{10,9... | collective-permute-start | bytes 387080 | tf_op jit(solution)/shard_map/ppermute | solution.py:54
  77.6 3.4 %collective-permute-start.18 = (bf16[256,1536]{1,0:T(8,128)(2,1)S(1)}, bf16[256,1536]{1,0:T(8,128)(2,1)S(1)}, u32[]{:S(2)}, u32[]{:S(2)}) collective-permute-start(bf16[256,1536]{1,0:T(8,128)(2,1)S(1)} %convolution_convert_fusion), channel_id=1, source_target_pairs={{0,16},{16,0},{32,48},{48,32},{64,80},{80,64},{96,112},{112,96},{1... | collective-permute-start | bytes 2359304 | tf_op jit(solution)/shard_map/ppermute | solution.py:54
  81.8 5.8 %collective-permute-start.19 = (bf16[64,1536]{1,0:T(8,128)(2,1)S(1)}, bf16[64,1536]{1,0:T(8,128)(2,1)S(1)}, u32[]{:S(2)}, u32[]{:S(2)}) collective-permute-start(bf16[64,1536]{1,0:T(8,128)(2,1)S(1)} %get-tuple-element.42), channel_id=1, source_target_pairs={{0,4},{4,0},{8,12},{12,8},{16,28},{20,24},{24,20},{28,16},{32,36},... | collective-permute-start | bytes 589832 | tf_op jit(solution)/shard_map/ppermute | solution.py:54
  83.7 8.4 %collective-permute-start.21 = (bf16[64,1536]{1,0:T(8,128)(2,1)S(1)}, bf16[64,1536]{1,0:T(8,128)(2,1)S(1)}, u32[]{:S(2)}, u32[]{:S(2)}) collective-permute-start(bf16[64,1536]{1,0:T(8,128)(2,1)S(1)} %get-tuple-element.43), channel_id=1, source_target_pairs={{0,8},{4,12},{8,0},{12,4},{16,24},{20,28},{24,16},{28,20},{32,40},... | collective-permute-start | bytes 589832 | tf_op jit(solution)/shard_map/ppermute | solution.py:54
  85.5 8.4 %collective-permute-start.20 = (bf16[64,1536]{1,0:T(8,128)(2,1)S(1)}, bf16[64,1536]{1,0:T(8,128)(2,1)S(1)}, u32[]{:S(2)}, u32[]{:S(2)}) collective-permute-start(bf16[64,1536]{1,0:T(8,128)(2,1)S(1)} %get-tuple-element.44), channel_id=1, source_target_pairs={{0,12},{4,8},{8,4},{12,0},{16,20},{20,16},{24,28},{28,24},{32,44},... | collective-permute-start | bytes 589832 | tf_op jit(solution)/shard_map/ppermute | solution.py:54
  94.0 7.5 %collective-permute-start.23 = (bf16[16,1536]{1,0:T(8,128)(2,1)S(1)}, bf16[16,1536]{1,0:T(8,128)(2,1)S(1)}, u32[]{:S(2)}, u32[]{:S(2)}) collective-permute-start(bf16[16,1536]{1,0:T(8,128)(2,1)S(1)} %get-tuple-element.45), channel_id=1, source_target_pairs={{0,32},{16,240},{32,64},{48,16},{64,96},{80,48},{96,128},{112,80},... | collective-permute-start | bytes 147464 | tf_op jit(solution)/shard_map/ppermute | solution.py:54
  96.0 5.5 %collective-permute-start.25 = (bf16[16,1536]{1,0:T(8,128)(2,1)S(1)}, bf16[16,1536]{1,0:T(8,128)(2,1)S(1)}, u32[]{:S(2)}, u32[]{:S(2)}) collective-permute-start(bf16[16,1536]{1,0:T(8,128)(2,1)S(1)} %get-tuple-element.46), channel_id=1, source_target_pairs={{0,96},{16,176},{32,128},{48,208},{64,160},{80,240},{96,192},{112,... | collective-permute-start | bytes 147464 | tf_op jit(solution)/shard_map/ppermute | solution.py:54
  96.8 4.8 %collective-permute-start.24 = (bf16[16,1536]{1,0:T(8,128)(2,1)S(1)}, bf16[16,1536]{1,0:T(8,128)(2,1)S(1)}, u32[]{:S(2)}, u32[]{:S(2)}) collective-permute-start(bf16[16,1536]{1,0:T(8,128)(2,1)S(1)} %get-tuple-element.47), channel_id=1, source_target_pairs={{0,64},{16,208},{32,96},{48,240},{64,128},{80,16},{96,160},{112,48... | collective-permute-start | bytes 147464 | tf_op jit(solution)/shard_map/ppermute | solution.py:54
  99.1 8.0 %collective-permute-start.22 = (bf16[8,1536]{1,0:T(8,128)(2,1)S(1)}, bf16[8,1536]{1,0:T(8,128)(2,1)S(1)}, u32[]{:S(2)}, u32[]{:S(2)}) collective-permute-start(bf16[8,1536]{1,0:T(8,128)(2,1)S(1)} %slice.67), channel_id=1, source_target_pairs={{0,128},{16,144},{32,160},{48,176},{64,192},{80,208},{96,224},{112... | collective-permute-start | bytes 73736 | tf_op jit(solution)/shard_map/ppermute | solution.py:54
  101.6 5.4 %collective-permute-start.26 = (bf16[8,1536]{1,0:T(8,128)(2,1)S(1)}, bf16[8,1536]{1,0:T(8,128)(2,1)S(1)}, u32[]{:S(2)}, u32[]{:S(2)}) collective-permute-start(bf16[8,1536]{1,0:T(8,128)(2,1)S(1)} %slice.87), channel_id=1, source_target_pairs={{0,16},{16,0},{32,48},{48,32},{64,80},{80,64},{96,112},{112,96},{1... | collective-permute-start | bytes 73736 | tf_op jit(solution)/shard_map/ppermute | solution.py:54

commit v4 on v3

--- a/solution.py
+++ b/solution.py
@@ -26,8 +26,8 @@
     scores = jnp.einsum(
         "rhgd,rlhd->rhgl", query_blocks, key_blocks, preferred_element_type=f32
     ) * (1.0 / math.sqrt(HEAD_SIZE))
-    position = lax.broadcasted_iota(jnp.int32, (1, 1, 1, span), 3)
-    visible = position < lengths[:, None, None, None]
+    position = lax.broadcasted_iota(jnp.int32, scores.shape, 3)
+    visible = position < jnp.broadcast_to(lengths[:, None, None, None], scores.shape)
     scores = jnp.where(visible, scores, -1e30)
     peak = jnp.max(scores, axis=-1, keepdims=True)
     expd = jnp.exp(scores - peak)
@@ -123,12 +123,10 @@
     return (slot.astype(f32) == ranks).astype(bf16)
 
 
-def pack_kernel(place, own, other, gate_own, gate_other, up_own, up_other, *outs):
-    *outs, share, ranks = outs
+def list_kernel(place, own, other, onehots, stats, share, ranks):
     y, first = place[0], place[1]
-    experts, fan, n = gate_own.shape
-    slots, units = outs[0].shape[2], experts * fan // len(outs)
-    rows, extra = 2 * n, own.shape[1]
+    experts, rows, slots = onehots.shape
+    parts, extra = stats.shape[0], own.shape[1]
     notes = jnp.concatenate([own[...], other[...]], axis=0).astype(f32)
     named = notes > 0.0
     before = lax.broadcasted_iota(jnp.int32, (rows, rows), 1) <= lax.broadcasted_iota(
@@ -146,42 +144,66 @@
     for e in range(experts):
         rank = jnp.sum(jnp.where(column == first + e, placed, 0.0), axis=1, keepdims=True)
         onehot = (slot == rank).astype(bf16)
+        onehots[e] = onehot
         listed = jnp.dot(turned, onehot, preferred_element_type=f32)
-        stats = listed[EXPERTS:]
-
-        @pl.when(y // (len(outs) // experts) == e)
+        for h in range(parts // experts):
+            stats[e * (parts // experts) + h] = listed[EXPERTS:]
+
+        @pl.when(y // (parts // experts) == e)
         def _():
             values = jnp.sum(jnp.where(line == first + e, listed, 0.0), axis=0, keepdims=True)
             share[...] = jnp.broadcast_to(values, share.shape)
 
-        for g, (part_own, part_other) in enumerate(((gate_own, gate_other), (up_own, up_other))):
-            packed = jnp.dot(part_own[e], onehot[:n], preferred_element_type=f32)
-            packed = packed + jnp.dot(part_other[e], onehot[n:], preferred_element_type=f32)
-            for h in range(fan // units):
-                part = jnp.concatenate([packed[h * units : (h + 1) * units], stats], axis=0)
-                part = part.astype(bf16)
-                step = lax.rem(e * (fan // units) + h + len(outs) - y, len(outs))
-                for k, out in enumerate(outs):
-
-                    @pl.when(step == k)
-                    def _(out=out, g=g, part=part):
-                        out[g] = part
-
-
-def pack(place, own, other, sums):
-    experts, fan, n = sums[0].shape
-    rows, extra = 2 * n, own.shape[1]
-    parts, slots = 4, rows * CAPACITY_OF_512 // 512
+
+def list_rows(place, own, other, experts, parts):
+    rows, extra = 2 * own.shape[0], own.shape[1]
+    slots = rows * CAPACITY_OF_512 // 512
+    whole = pl.BlockSpec(memory_space=VMEM)
+    return pl.pallas_call(
+        list_kernel,
+        out_shape=[
+            jax.ShapeDtypeStruct((experts, rows, slots), bf16),
+            jax.ShapeDtypeStruct((parts, EXPERTS, slots), f32),
+            jax.ShapeDtypeStruct((EXPERTS, slots), f32),
+            jax.ShapeDtypeStruct((extra, rows), f32),
+        ],
+        in_specs=[pl.BlockSpec(memory_space=SMEM)] + [whole] * 2,
+        out_specs=[whole] * 4,
+        compiler_params=pltpu.CompilerParams(vmem_limit_bytes=12 << 20),
+        cost_estimate=pl.CostEstimate(flops=1 << 27, bytes_accessed=1 << 20, transcendentals=0),
+    )(place, own, other)
+
+
+def pack_kernel(place, own, other, onehots, below, *outs):
+    experts, fan, _ = own.shape
+    units = outs[0].shape[0] - below.shape[1]
+    for e in range(experts):
+        packed = jnp.concatenate([own[e], other[e]], axis=1)
+        packed = jnp.dot(packed, onehots[e], preferred_element_type=f32)
+        for h in range(fan // units):
+            q = e * (fan // units) + h
+            part = jnp.concatenate([packed[h * units : (h + 1) * units], below[q]], axis=0)
+            part = part.astype(bf16)
+            step = lax.rem(q + len(outs) - place[0], len(outs))
+            for k, out in enumerate(outs):
+
+                @pl.when(step == k)
+                def _(out=out, part=part):
+                    out[...] = part
+
+
+def pack(place, own, other, onehots, below):
+    experts, fan, _ = own.shape
+    parts, lines, slots = below.shape
     whole = pl.BlockSpec(memory_space=VMEM)
     return pl.pallas_call(
         pack_kernel,
-        out_shape=[jax.ShapeDtypeStruct((2, experts * fan // parts + EXPERTS, slots), bf16)] * parts
-        + [jax.ShapeDtypeStruct((8, slots), f32), jax.ShapeDtypeStruct((extra, rows), f32)],
-        in_specs=[pl.BlockSpec(memory_space=SMEM)] + [whole] * 6,
-        out_specs=[whole] * (parts + 2),
-        compiler_params=pltpu.CompilerParams(vmem_limit_bytes=16 << 20),
-        cost_estimate=pl.CostEstimate(flops=1 << 29, bytes_accessed=2 << 20, transcendentals=0),
-    )(place, own, other, *sums)
+        out_shape=[jax.ShapeDtypeStruct((experts * fan // parts + lines, slots), bf16)] * parts,
+        in_specs=[pl.BlockSpec(memory_space=SMEM)] + [whole] * 4,
+        out_specs=[whole] * parts,
+        compiler_params=pltpu.CompilerParams(vmem_limit_bytes=12 << 20),
+        cost_estimate=pl.CostEstimate(flops=1 << 28, bytes_accessed=2 << 20, transcendentals=0),
+    )(place, own, other, onehots, below)
 
 
 def split_kernel(*refs):
@@ -215,8 +237,10 @@
     )(*pieces)
 
 
-def activate_kernel(part0, part1, part2, part3, gains, share, hidden):
-    parts = [[p[g].astype(f32) for g in range(2)] for p in (part0, part1, part2, part3)]
+def activate_kernel(*refs):
+    *parts, share, hidden = refs
+    half = len(parts) // 2
+    parts = [[p[...].astype(f32) for p in pair] for pair in zip(parts[:half], parts[half:])]
     units, slots = hidden.shape
     count = len(parts)
     means, devs = [], []
@@ -228,7 +252,11 @@
     var = sum(devs) / (count * PART_WIDTH)
     var = var + sum(jnp.square(m - mean) for m in means) / count
     scale = lax.rsqrt(var + epsilon)
-    columns = jnp.transpose(gains[...])
+    gains = []
+    for part in parts:
+        terms = part[1][units:]
+        gains += [terms[0:1] + terms[1:2] + terms[2:3], terms[3:4] + terms[4:5] + terms[5:6]]
+    columns = jnp.transpose(jnp.concatenate(gains, axis=0)[:, :256])[:units]
 
     def total(g):
         result = sum(part[g][:units] for part in parts)
@@ -240,17 +268,17 @@
     hidden[...] = (gate * jax.nn.sigmoid(gate) * total(1) * share[0:1]).astype(bf16)
 
 
-def activate(parts, gains, share):
-    whole = pl.BlockSpec(memory_space=VMEM)
-    units, slots = parts[0].shape[1] - EXPERTS, parts[0].shape[2]
+def activate(parts, share):
+    whole = pl.BlockSpec(memory_space=VMEM)
+    units, slots = parts[0].shape[0] - EXPERTS, parts[0].shape[1]
     return pl.pallas_call(
         activate_kernel,
         out_shape=jax.ShapeDtypeStruct((units, slots), bf16),
-        in_specs=[whole] * 6,
+        in_specs=[whole] * (len(parts) + 1),
         out_specs=whole,
         compiler_params=pltpu.CompilerParams(vmem_limit_bytes=8 << 20),
         cost_estimate=pl.CostEstimate(flops=1, bytes_accessed=1 << 20, transcendentals=1),
-    )(*parts, gains, share)
+    )(*parts, share)
 
 
 def scatter_kernel(place, hidden0, hidden1, hidden2, hidden3, ranks, out):
@@ -294,6 +322,7 @@
     rows, width = stream.shape
     gain = lax.dynamic_slice_in_dim(norm_gain, y * width, width, 0).astype(f32)
 
+    units = w_gate.shape[0] * w_gate.shape[2] // y_size
     down = w_down.reshape(-1, width)
 
     def project(weight, tokens):
@@ -307,19 +336,30 @@
         [jnp.einsum("edf,d->ef", w.astype(f32), gain).reshape(y_size, -1) for w in (w_gate, w_up)]
     )
 
-    def gain_block(k):
-        return lax.dynamic_index_in_dim(gains, lax.rem(y + k, y_size), 1, False)
-
-    gains = [gain_block(0)] + [to_y(gain_block(k), k) for k in range(1, y_size)]
+    terms, rest = [], gains
+    for _ in range(3):
+        terms.append(lax.reduce_precision(rest, 8, 7))
+        rest = rest - terms[-1]
+    gains = jnp.stack(terms, axis=1).reshape(2 * len(terms), y_size, units).swapaxes(0, 1)
+    slots = 4 * held.shape[0] * 2 * CAPACITY_OF_512 // 512
+    gains = jnp.pad(gains, ((0, 0), (0, EXPERTS - gains.shape[1]), (0, slots - units)))
     pieces = [along_x(held, k) for k in range(3)]
-    pieces, gains = lax.optimization_barrier((pieces, jnp.concatenate(gains, axis=0)))
+    pieces, gains = lax.optimization_barrier((pieces, gains))
     own, own_rows, own_notes = split([held] + pieces, width, True)
     other_rows, other_notes = split([swap_core(own)], width, False)
-    sums = [project(w, t) for w in (w_gate, w_up) for t in (own_rows, other_rows)]
-    *parts, share, ranks = pack(place, own_notes, other_notes, sums)
-    parts = [parts[0]] + [to_y(part, k) for k, part in enumerate(parts) if k > 0]
-    hidden = activate(parts, gains, share)
-    hidden = scatter(place, [hidden] + [to_y(hidden, -k) for k in range(1, y_size)], ranks)
+    onehots, stats, share, ranks = list_rows(
+        place, own_notes, other_notes, w_gate.shape[0], y_size
+    )
+    gate_sums, up_sums = project(w_gate, own_rows), project(w_up, own_rows)
+    gate_parts = pack(place, gate_sums, project(w_gate, other_rows), onehots, stats)
+    other_rows, gate_parts = lax.optimization_barrier((other_rows, gate_parts))
+    up_parts = pack(place, up_sums, project(w_up, other_rows), onehots, gains)
+    parts = []
+    for packed in (gate_parts, up_parts):
+        parts += [packed[0]] + [to_y(packed[k], k) for k in range(1, y_size)]
+    hidden = activate(parts, share)
+    got = {k: to_y(hidden, -k) for k in (1, 3, 2)}
+    hidden = scatter(place, [hidden] + [got[k] for k in range(1, y_size)], ranks)
     hidden = hidden.reshape(down.shape[0], -1)
     n = own.shape[0]
 
@@ -327,15 +367,18 @@
         return jnp.einsum("fr,fd->rd", hidden[:, at : at + n], down, preferred_element_type=f32)
 
     other = swap_core(back_down(n).astype(bf16))
-    total = back_down(0) + other.astype(f32)
+    total = lax.optimization_barrier(back_down(0)) + other.astype(f32)
     n = n // 4
-    total = total[:n] + sum(
-        along_x(total[(k + 1) * n : (k + 2) * n].astype(bf16), k).astype(f32) for k in range(3)
-    )
-    mine, across, n = total[:rows], total[rows : 2 * rows].astype(bf16), 2 * rows
-    chip = sum(
-        along_z(total[k * n : (k + 1) * n].astype(bf16), k, True).astype(f32) for k in (1, 2, 3)
-    )
+    total, sent = lax.optimization_barrier(
+        (total[:n], [total[k * n : (k + 1) * n].astype(bf16) for k in range(1, 4)])
+    )
+    total = total + sum(along_x(sent[k], k).astype(f32) for k in range(3))
+    n = 2 * rows
+    mine, across, *chip = lax.optimization_barrier(
+        (total[:rows], total[rows:n].astype(bf16))
+        + tuple(total[k * n : (k + 1) * n].astype(bf16) for k in (1, 2, 3))
+    )
+    chip = sum(along_z(part, k + 1, True).astype(f32) for k, part in enumerate(chip))
     mine = mine + along_z(across, 4, True).astype(f32) + chip[:rows]
     mine = mine + swap_core(chip[rows:].astype(bf16)).astype(f32)
     return (stream, mine.astype(bf16))

time: 108 us -> 103 us (0.954)
  starting transfers between devices: 47.5 us -> 43.4 us
  waiting for transfers between devices: 36.9 us -> 35.3 us
    ppermute x27, starting transfers between devices: 47.5 us -> 43.4 us  [send(): return lax.ppermute(x, axes, pairs)]
    ppermute x27, waiting for transfers between devices: 36.9 us -> 35.3 us  [send(): return lax.ppermute(x, axes, pairs)]
    pallas_call x1 -> x3, Pallas kernels: 2.98 us -> 4.01 us  [the longest x2 2.68 us: pack(): pl.pallas_call(pack_kernel, out_shape=[jax.ShapeDtypeStruct((experts * fa...]
  transfers between devices with their start and end apart: 27 -> 27, of which waited for: 12 -> 15; matrix products, arithmetic and copies ran while one was open for 6% -> 8% of each run, Pallas kernels for 0% -> 1%
where the time goes in v4:
time: 103 us
  starting transfers between devices  43.4 us (42%)
  waiting for transfers between devices  35.3 us (34%)
  matrix products  12.5 us (12%)
  Pallas kernels  7.02 us (7%)
  local copies, waits for them, and re-layouts  2.14 us (2%)
  other arithmetic  1.3 us (1%)
    ppermute x27, starting transfers between devices, send(): return lax.ppermute(x, axes, pairs)  43.4 us
    ppermute x27, waiting for transfers between devices, send(): return lax.ppermute(x, axes, pairs)  35.3 us
    dot_general x4, matrix products, project(): jnp.einsum('edf,rd->efr', weight, tokens, preferred_element_type=f32)  4.49 us
    dot_general x2, matrix products, per_device(): jnp.einsum('edf,d->ef', w.astype(f32), gain).reshape(y_size, -1)  2.96 us
    pallas_call x2, Pallas kernels, pack(): pl.pallas_call(pack_kernel, out_shape=[jax.ShapeDtypeStruct((experts * fa...  2.68 us
  transfers between devices with their start and end apart: 27, of which 15 were waited for; matrix products, arithmetic and copies ran while one was open for 8% of the time, Pallas kernels for 1%

profile of v4, /device:TPU:1, one launch (start us, length us, event | category | flops | bytes accessed | tf_op | source)
XLA Modules:
  0.0 102.6 jit_solution(16194274339682892099)
XLA Ops:
  0.7 1.6 %copy-done = bf16[8,512,256]{2,1,0:T(8,128)(2,1)S(1)} copy-done((bf16[8,512,256]{2,1,0:T(8,128)(2,1)S(1)}, bf16[8,512,256]{2,1,0:T(8,128)(2,1)}, u32[]{:S(2)}) %copy-start) | copy-done | bytes 2097176
  2.2 1.4 %fusion.16 = f32[8,2,6,512]{3,2,1,0:T(8,128)S(1)} fusion(s32[8]{0:T(128)} %param.14, bf16[8,2,6,128]{3,0,2,1:T(8,128)(2,1)} %bitcast.74, bf16[8,512,256]{2,1,0:T(8,128)(2,1)S(1)} %copy-done), kind=kOutput, calls=%fused_computation.20 | convolution fusion | flops 12730368 | bytes 2318368 | tf_op jit(solution)/shard_map/rhgd,rlhd->rhgl/dot_general | solution.py:26
  3.9 2.0 %fusion.1 = f32[8,2,6,128]{3,2,1,0:T(8,128)S(1)} fusion(f32[8,2,6]{2,1,0:T(2,128)S(1)} %fusion.35, f32[8,2,6,512]{3,2,1,0:T(8,128)S(1)} %fusion.16, bf16[8,512,256]{2,1,0:T(8,128)(2,1)} %param.13), kind=kOutput, calls=%fused_computation.2 | convolution fusion | flops 12730975 | bytes 2343296 | tf_op jit(solution)/shard_map/rhgl,rlhd->rhgd/dot_general | solution.py:36
  6.0 1.3 %shard_map.122 = (bf16[8,1536]{1,0:T(8,128)(2,1)}, bf16[8,1664]{1,0:T(8,128)(2,1)S(1)}) custom-call(s32[2]{0:T(128)S(1)} %pad_add_fusion.place, f32[8,1536]{1,0:T(8,128)S(1)} %reshape.142.attended, bf16[8,1536]{1,0:T(8,128)(2,1)S(1)} %copy-done.1, bf16[6144]{0:T(1024)(128)(2,1)S(1)} %copy-done.2, s32[4,8]{1,0:T(4,128)S(1)} %bitcast.68, f32[4,8]{1,0:T(4,128)S(1)} %bitcast.69), custom_call_target="tpu_custom_call" | custom-call | flops 65536 | bytes 65536 | tf_op jit(solution)/shard_map/pallas_call | solution.py:108
  7.3 3.2 %collective-permute-start.1 = (bf16[8,1664]{1,0:T(8,128)(2,1)S(1)}, bf16[8,1664]{1,0:T(8,128)(2,1)S(1)}, u32[]{:S(2)}, u32[]{:S(2)}) collective-permute-start(bf16[8,1664]{1,0:T(8,128)(2,1)S(1)} %get-tuple-element.42), channel_id=1, source_target_pairs={{0,16},{16,0},{32,48},{48,32},{64,80},{80,64},{96,112},{112,96},{1... | collective-permute-start | bytes 79880 | tf_op jit(solution)/shard_map/ppermute | solution.py:54
  10.5 5.2 %collective-permute-start = (bf16[8,1664]{1,0:T(8,128)(2,1)S(1)}, bf16[8,1664]{1,0:T(8,128)(2,1)S(1)}, u32[]{:S(2)}, u32[]{:S(2)}) collective-permute-start(bf16[8,1664]{1,0:T(8,128)(2,1)S(1)} %get-tuple-element.42), channel_id=1, source_target_pairs={{0,128},{16,144},{32,160},{48,176},{64,192},{80,208},{96,224},{112... | collective-permute-start | bytes 79880 | tf_op jit(solution)/shard_map/ppermute | solution.py:54
  15.8 1.7 %collective-permute-start.4 = (bf16[16,1664]{1,0:T(8,128)(2,1)S(1)}, bf16[16,1664]{1,0:T(8,128)(2,1)S(1)}, u32[]{:S(2)}, u32[]{:S(2)}) collective-permute-start(bf16[16,1664]{1,0:T(8,128)(2,1)S(1)} %constant_dynamic-update-slice_fusion), channel_id=1, source_target_pairs={{0,160},{16,112},{32,192},{48,144},{64,224},{80,176},{96,0},{112,2... | collective-permute-start | bytes 159752 | tf_op jit(solution)/shard_map/ppermute | solution.py:54
  18.1 5.8 %collective-permute-done.2 = bf16[16,1664]{1,0:T(8,128)(2,1)S(1)} collective-permute-done((bf16[16,1664]{1,0:T(8,128)(2,1)S(1)}, bf16[16,1664]{1,0:T(8,128)(2,1)S(1)}, u32[]{:S(2)}, u32[]{:S(2)}) %collective-permute-start.2) | collective-permute-done | bytes 53280 | tf_op jit(solution)/shard_map/ppermute | solution.py:54
  23.9 2.8 %collective-permute-start.7 = (bf16[64,1664]{1,0:T(8,128)(2,1)S(1)}, bf16[64,1664]{1,0:T(8,128)(2,1)S(1)}, u32[]{:S(2)}, u32[]{:S(2)}) collective-permute-start(bf16[64,1664]{1,0:T(8,128)(2,1)S(1)} %constant_dynamic-update-slice_fusion.2.refs_0_), channel_id=1, source_target_pairs={{0,8},{4,12},{8,0},{12,4},{16,24},{20,28},{24,16},{28,20},{32,40},... | collective-permute-start | bytes 638984 | tf_op jit(solution)/shard_map/ppermute | solution.py:54
  27.6 2.2 %fusion.37 = f32[1,2,336]{2,0,1:T(1,128)S(1)} fusion(bf16[1536,1,1]{0,1,2:T(2,128)(2,1)S(1)} %reshape.146, bf16[2,1536,336]{1,2,0:T(8,128)(2,1)} %param.20), kind=kOutput, calls=%fused_computation.62 | convolution fusion | flops 2064384 | bytes 2070144 | tf_op jit(solution)/shard_map/edf,d->ef/dot_general | solution.py:336
  29.9 0.7 fusion.36
  31.2 4.7 %collective-permute-done.6.refs_2_ = bf16[64,1664]{1,0:T(8,128)(2,1)S(1)} collective-permute-done((bf16[64,1664]{1,0:T(8,128)(2,1)S(1)}, bf16[64,1664]{1,0:T(8,128)(2,1)S(1)}, u32[]{:S(2)}, u32[]{:S(2)}) %collective-permute-start.6) | collective-permute-done | bytes 213024 | tf_op jit(solution)/shard_map/ppermute | solution.py:54
  35.9 0.8 collective-permute-done.5.refs_1_
  36.8 1.3 %collective-permute-start.8 = (bf16[256,1664]{1,0:T(8,128)(2,1)S(1)}, bf16[256,1664]{1,0:T(8,128)(2,1)S(1)}, u32[]{:S(2)}, u32[]{:S(2)}) collective-permute-start(bf16[256,1664]{1,0:T(8,128)(2,1)S(1)} %get-tuple-element.48), channel_id=1, source_target_pairs={{0,16},{16,0},{32,48},{48,32},{64,80},{80,64},{96,112},{112,96},{1... | collective-permute-start | bytes 2555912 | tf_op jit(solution)/shard_map/ppermute | solution.py:54
  38.1 2.3 %fusion.10.own = bf16[2,336,256]{2,1,0:T(8,128)(2,1)S(1)} fusion(bf16[2,1536,336]{1,2,0:T(8,128)(2,1)} %param.20, bf16[256,1536]{1,0:T(8,128)(2,1)S(1)} %get-tuple-element.50), kind=kOutput, calls=%fused_computation.16 | convolution fusion | flops 528654336 | bytes 3194880 | tf_op jit(solution)/shard_map/edf,rd->efr/dot_general | solution.py:329
  40.4 0.7 fusion.8.own
  41.2 0.7 fusion.9.other
  42.0 1.3 %shard_map.125 = (bf16[2,512,384]{2,1,0:T(8,128)(2,1)S(1)}, f32[4,8,384]{2,1,0:T(8,128)S(1)}, f32[8,384]{1,0:T(8,128)S(1)}, f32[128,512]{1,0:T(8,128)S(1)}) custom-call(s32[2]{0:T(128)S(1)} %pad_add_fusion.place, bf16[256,128]{1,0:T(8,128)(2,1)S(1)} %get-tuple-element.51.own, bf16[256,128]{1,0:T(8,128)(2,1)S(1)} %get-tuple-element.52.other), custom_call_target="tpu_custom_call" | custom-call | flops 134217728 | bytes 1048576 | tf_op jit(solution)/shard_map/pallas_call | solution.py:162
  43.3 1.3 %shard_map.126 = (bf16[176,384]{1,0:T(8,128)(2,1)S(1)}, bf16[176,384]{1,0:T(8,128)(2,1)S(1)}, bf16[176,384]{1,0:T(8,128)(2,1)S(1)}, bf16[176,384]{1,0:T(8,128)(2,1)S(1)}) custom-call(s32[2]{0:T(128)S(1)} %pad_add_fusion.place, bf16[2,336,256]{2,1,0:T(8,128)(2,1)S(1)} %fusion.8.own, bf16[2,336,256]{2,1,0:T(8,128)(2,1)S(1)} %fusion.9.other, ...), custom_call_target="tpu_custom_call" | custom-call | flops 268435456 | bytes 2097152 | tf_op jit(solution)/shard_map/pallas_call | solution.py:199
  44.6 1.4 %collective-permute-start.9 = (bf16[176,384]{1,0:T(8,128)(2,1)S(1)}, bf16[176,384]{1,0:T(8,128)(2,1)S(1)}, u32[]{:S(2)}, u32[]{:S(2)}) collective-permute-start(bf16[176,384]{1,0:T(8,128)(2,1)S(1)} %get-tuple-element.60), channel_id=1, source_target_pairs={{0,1},{1,2},{2,3},{3,0},{4,5},{5,6},{6,7},{7,4},{8,9},{9,10},{10,1... | collective-permute-start | bytes 405512 | tf_op jit(solution)/shard_map/ppermute | solution.py:54
  46.0 2.6 %collective-permute-start.10 = (bf16[176,384]{1,0:T(8,128)(2,1)S(1)}, bf16[176,384]{1,0:T(8,128)(2,1)S(1)}, u32[]{:S(2)}, u32[]{:S(2)}) collective-permute-start(bf16[176,384]{1,0:T(8,128)(2,1)S(1)} %get-tuple-element.61), channel_id=1, source_target_pairs={{0,2},{1,3},{2,0},{3,1},{4,6},{5,7},{6,4},{7,5},{8,10},{9,11},{10,... | collective-permute-start | bytes 405512 | tf_op jit(solution)/shard_map/ppermute | solution.py:54
  48.6 1.1 %collective-permute-start.11 = (bf16[176,384]{1,0:T(8,128)(2,1)S(1)}, bf16[176,384]{1,0:T(8,128)(2,1)S(1)}, u32[]{:S(2)}, u32[]{:S(2)}) collective-permute-start(bf16[176,384]{1,0:T(8,128)(2,1)S(1)} %get-tuple-element.62), channel_id=1, source_target_pairs={{0,3},{1,0},{2,1},{3,2},{4,7},{5,4},{6,5},{7,6},{8,11},{9,8},{10,9... | collective-permute-start | bytes 405512 | tf_op jit(solution)/shard_map/ppermute | solution.py:54
  49.7 0.7 fusion.11.other
  50.4 1.3 %shard_map.127 = (bf16[176,384]{1,0:T(8,128)(2,1)S(1)}, bf16[176,384]{1,0:T(8,128)(2,1)S(1)}, bf16[176,384]{1,0:T(8,128)(2,1)S(1)}, bf16[176,384]{1,0:T(8,128)(2,1)S(1)}) custom-call(s32[2]{0:T(128)S(1)} %pad_add_fusion.place, bf16[2,336,256]{2,1,0:T(8,128)(2,1)S(1)} %fusion.10.own, bf16[2,336,256]{2,1,0:T(8,128)(2,1)S(1)} %fusion.11.other, ...), custom_call_target="tpu_custom_call" | custom-call | flops 268435456 | bytes 2097152 | tf_op jit(solution)/shard_map/pallas_call | solution.py:199
  52.3 0.8 collective-permute-start.13
  53.1 1.7 %collective-permute-start.14 = (bf16[176,384]{1,0:T(8,128)(2,1)S(1)}, bf16[176,384]{1,0:T(8,128)(2,1)S(1)}, u32[]{:S(2)}, u32[]{:S(2)}) collective-permute-start(bf16[176,384]{1,0:T(8,128)(2,1)S(1)} %get-tuple-element.68), channel_id=1, source_target_pairs={{0,3},{1,0},{2,1},{3,2},{4,7},{5,4},{6,5},{7,6},{8,11},{9,8},{10,9... | collective-permute-start | bytes 405512 | tf_op jit(solution)/shard_map/ppermute | solution.py:54
  55.3 2.3 %collective-permute-done.12.refs_5_ = bf16[176,384]{1,0:T(8,128)(2,1)S(1)} collective-permute-done((bf16[176,384]{1,0:T(8,128)(2,1)S(1)}, bf16[176,384]{1,0:T(8,128)(2,1)S(1)}, u32[]{:S(2)}, u32[]{:S(2)}) %collective-permute-start.12) | collective-permute-done | bytes 135200 | tf_op jit(solution)/shard_map/ppermute | solution.py:54
  57.6 3.5 %collective-permute-done.13.refs_6_ = bf16[176,384]{1,0:T(8,128)(2,1)S(1)} collective-permute-done((bf16[176,384]{1,0:T(8,128)(2,1)S(1)}, bf16[176,384]{1,0:T(8,128)(2,1)S(1)}, u32[]{:S(2)}, u32[]{:S(2)}) %collective-permute-start.13) | collective-permute-done | bytes 135200 | tf_op jit(solution)/shard_map/ppermute | solution.py:54
  61.6 1.8 %collective-permute-start.17 = (bf16[168,384]{1,0:T(8,128)(2,1)S(1)}, bf16[168,384]{1,0:T(8,128)(2,1)S(1)}, u32[]{:S(2)}, u32[]{:S(2)}) collective-permute-start(bf16[168,384]{1,0:T(8,128)(2,1)S(1)} %shard_map.128.hidden0), channel_id=1, source_target_pairs={{0,1},{1,2},{2,3},{3,0},{4,5},{5,6},{6,7},{7,4},{8,9},{9,10},{10,1... | collective-permute-start | bytes 387080 | tf_op jit(solution)/shard_map/ppermute | solution.py:54
  63.3 2.7 %collective-permute-start.16 = (bf16[168,384]{1,0:T(8,128)(2,1)S(1)}, bf16[168,384]{1,0:T(8,128)(2,1)S(1)}, u32[]{:S(2)}, u32[]{:S(2)}) collective-permute-start(bf16[168,384]{1,0:T(8,128)(2,1)S(1)} %shard_map.128.hidden0), channel_id=1, source_target_pairs={{0,2},{1,3},{2,0},{3,1},{4,6},{5,7},{6,4},{7,5},{8,10},{9,11},{10,... | collective-permute-start | bytes 387080 | tf_op jit(solution)/shard_map/ppermute | solution.py:54
  66.0 1.1 %collective-permute-done.17.hidden3 = bf16[168,384]{1,0:T(8,128)(2,1)S(1)} collective-permute-done((bf16[168,384]{1,0:T(8,128)(2,1)S(1)}, bf16[168,384]{1,0:T(8,128)(2,1)S(1)}, u32[]{:S(2)}, u32[]{:S(2)}) %collective-permute-start.17) | collective-permute-done | bytes 129056 | tf_op jit(solution)/shard_map/ppermute | solution.py:54
  67.2 4.6 %collective-permute-done.16.hidden2 = bf16[168,384]{1,0:T(8,128)(2,1)S(1)} collective-permute-done((bf16[168,384]{1,0:T(8,128)(2,1)S(1)}, bf16[168,384]{1,0:T(8,128)(2,1)S(1)}, u32[]{:S(2)}, u32[]{:S(2)}) %collective-permute-start.16) | collective-permute-done | bytes 129056 | tf_op jit(solution)/shard_map/ppermute | solution.py:54
  71.8 1.1 %shard_map.129 = bf16[4,168,512]{2,1,0:T(8,128)(2,1)S(1)} custom-call(s32[2]{0:T(128)S(1)} %pad_add_fusion.place, bf16[168,384]{1,0:T(8,128)(2,1)S(1)} %shard_map.128.hidden0, bf16[168,384]{1,0:T(8,128)(2,1)S(1)} %collective-permute-done.15.hidden1, bf16[168,384]{1,0:T(8,128)(2,1)S(1)} %collective-permute-done.16.hidden2, ...), custom_call_target="tpu_custom_call" | custom-call | flops 268435456 | bytes 1048576 | tf_op jit(solution)/shard_map/pallas_call | solution.py:294
  72.9 0.8 convolution_convert_fusion
  73.7 1.5 %collective-permute-start.18 = (bf16[256,1536]{1,0:T(8,128)(2,1)S(1)}, bf16[256,1536]{1,0:T(8,128)(2,1)S(1)}, u32[]{:S(2)}, u32[]{:S(2)}) collective-permute-start(bf16[256,1536]{1,0:T(8,128)(2,1)S(1)} %convolution_convert_fusion), channel_id=1, source_target_pairs={{0,16},{16,0},{32,48},{48,32},{64,80},{80,64},{96,112},{112,96},{1... | collective-permute-start | bytes 2359304 | tf_op jit(solution)/shard_map/ppermute | solution.py:54
  75.2 0.8 fusion.24
  76.0 1.1 %collective-permute-done.18 = bf16[256,1536]{1,0:T(8,128)(2,1)S(1)} collective-permute-done((bf16[256,1536]{1,0:T(8,128)(2,1)S(1)}, bf16[256,1536]{1,0:T(8,128)(2,1)S(1)}, u32[]{:S(2)}, u32[]{:S(2)}) %collective-permute-start.18) | collective-permute-done | bytes 786464 | tf_op jit(solution)/shard_map/ppermute | solution.py:54
  77.5 2.5 %collective-permute-start.19 = (bf16[64,1536]{1,0:T(8,128)(2,1)S(1)}, bf16[64,1536]{1,0:T(8,128)(2,1)S(1)}, u32[]{:S(2)}, u32[]{:S(2)}) collective-permute-start(bf16[64,1536]{1,0:T(8,128)(2,1)S(1)} %get-tuple-element.72), channel_id=1, source_target_pairs={{0,4},{4,0},{8,12},{12,8},{16,28},{20,24},{24,20},{28,16},{32,36},... | collective-permute-start | bytes 589832 | tf_op jit(solution)/shard_map/ppermute | solution.py:54
  79.9 1.5 %collective-permute-start.21 = (bf16[64,1536]{1,0:T(8,128)(2,1)S(1)}, bf16[64,1536]{1,0:T(8,128)(2,1)S(1)}, u32[]{:S(2)}, u32[]{:S(2)}) collective-permute-start(bf16[64,1536]{1,0:T(8,128)(2,1)S(1)} %get-tuple-element.74), channel_id=1, source_target_pairs={{0,8},{4,12},{8,0},{12,4},{16,24},{20,28},{24,16},{28,20},{32,40},... | collective-permute-start | bytes 589832 | tf_op jit(solution)/shard_map/ppermute | solution.py:54
  81.4 1.9 %collective-permute-done.19 = bf16[64,1536]{1,0:T(8,128)(2,1)S(1)} collective-permute-done((bf16[64,1536]{1,0:T(8,128)(2,1)S(1)}, bf16[64,1536]{1,0:T(8,128)(2,1)S(1)}, u32[]{:S(2)}, u32[]{:S(2)}) %collective-permute-start.19) | collective-permute-done | bytes 196640 | tf_op jit(solution)/shard_map/ppermute | solution.py:54
  83.3 2.6 %collective-permute-done.20 = bf16[64,1536]{1,0:T(8,128)(2,1)S(1)} collective-permute-done((bf16[64,1536]{1,0:T(8,128)(2,1)S(1)}, bf16[64,1536]{1,0:T(8,128)(2,1)S(1)}, u32[]{:S(2)}, u32[]{:S(2)}) %collective-permute-start.20) | collective-permute-done | bytes 196640 | tf_op jit(solution)/shard_map/ppermute | solution.py:54
  85.9 4.7 %collective-permute-done.21 = bf16[64,1536]{1,0:T(8,128)(2,1)S(1)} collective-permute-done((bf16[64,1536]{1,0:T(8,128)(2,1)S(1)}, bf16[64,1536]{1,0:T(8,128)(2,1)S(1)}, u32[]{:S(2)}, u32[]{:S(2)}) %collective-permute-start.21) | collective-permute-done | bytes 196640 | tf_op jit(solution)/shard_map/ppermute | solution.py:54
  90.8 1.3 %collective-permute-start.23 = (bf16[16,1536]{1,0:T(8,128)(2,1)S(1)}, bf16[16,1536]{1,0:T(8,128)(2,1)S(1)}, u32[]{:S(2)}, u32[]{:S(2)}) collective-permute-start(bf16[16,1536]{1,0:T(8,128)(2,1)S(1)} %get-tuple-element.77), channel_id=1, source_target_pairs={{0,32},{16,240},{32,64},{48,16},{64,96},{80,48},{96,128},{112,80},... | collective-permute-start | bytes 147464 | tf_op jit(solution)/shard_map/ppermute | solution.py:54
  92.0 1.1 %collective-permute-start.24 = (bf16[16,1536]{1,0:T(8,128)(2,1)S(1)}, bf16[16,1536]{1,0:T(8,128)(2,1)S(1)}, u32[]{:S(2)}, u32[]{:S(2)}) collective-permute-start(bf16[16,1536]{1,0:T(8,128)(2,1)S(1)} %get-tuple-element.78), channel_id=1, source_target_pairs={{0,64},{16,208},{32,96},{48,240},{64,128},{80,16},{96,160},{112,48... | collective-permute-start | bytes 147464 | tf_op jit(solution)/shard_map/ppermute | solution.py:54
  93.1 2.3 %collective-permute-start.25 = (bf16[16,1536]{1,0:T(8,128)(2,1)S(1)}, bf16[16,1536]{1,0:T(8,128)(2,1)S(1)}, u32[]{:S(2)}, u32[]{:S(2)}) collective-permute-start(bf16[16,1536]{1,0:T(8,128)(2,1)S(1)} %get-tuple-element.79), channel_id=1, source_target_pairs={{0,96},{16,176},{32,128},{48,208},{64,160},{80,240},{96,192},{112,... | collective-permute-start | bytes 147464 | tf_op jit(solution)/shard_map/ppermute | solution.py:54
  95.4 2.5 %collective-permute-start.22 = (bf16[8,1536]{1,0:T(8,128)(2,1)S(1)}, bf16[8,1536]{1,0:T(8,128)(2,1)S(1)}, u32[]{:S(2)}, u32[]{:S(2)}) collective-permute-start(bf16[8,1536]{1,0:T(8,128)(2,1)S(1)} %slice.67), channel_id=1, source_target_pairs={{0,128},{16,144},{32,160},{48,176},{64,192},{80,208},{96,224},{112... | collective-permute-start | bytes 73736 | tf_op jit(solution)/shard_map/ppermute | solution.py:54
  98.2 2.7 %collective-permute-start.26 = (bf16[8,1536]{1,0:T(8,128)(2,1)S(1)}, bf16[8,1536]{1,0:T(8,128)(2,1)S(1)}, u32[]{:S(2)}, u32[]{:S(2)}) collective-permute-start(bf16[8,1536]{1,0:T(8,128)(2,1)S(1)} %slice.83), channel_id=1, source_target_pairs={{0,16},{16,0},{32,48},{48,32},{64,80},{80,64},{96,112},{112,96},{1... | collective-permute-start | bytes 73736 | tf_op jit(solution)/shard_map/ppermute | solution.py:54
  100.9 1.0 %collective-permute-done.22 = bf16[8,1536]{1,0:T(8,128)(2,1)S(1)} collective-permute-done((bf16[8,1536]{1,0:T(8,128)(2,1)S(1)}, bf16[8,1536]{1,0:T(8,128)(2,1)S(1)}, u32[]{:S(2)}, u32[]{:S(2)}) %collective-permute-start.22) | collective-permute-done | bytes 24608 | tf_op jit(solution)/shard_map/ppermute | solution.py:54
  (73 shorter events, 5.5 us)
Async XLA Ops:
  0.6 1.6 %copy-start = (bf16[8,512,256]{2,1,0:T(8,128)(2,1)S(1)}, bf16[8,512,256]{2,1,0:T(8,128)(2,1)}, u32[]{:S(2)}) copy-start(bf16[8,512,256]{2,1,0:T(8,128)(2,1)} %param.12) | copy-start | bytes 6291460
  3.6 2.4 %copy-start.1 = (bf16[8,1536]{1,0:T(8,128)(2,1)S(1)}, bf16[8,1536]{1,0:T(8,128)(2,1)}, u32[]{:S(2)}) copy-start(bf16[8,1536]{1,0:T(8,128)(2,1)} %residual.1) | copy-start | bytes 73732
  3.6 2.4 %copy-start.2 = (bf16[6144]{0:T(1024)(128)(2,1)S(1)}, bf16[6144]{0:T(1024)(128)(2,1)}, u32[]{:S(2)}) copy-start(bf16[6144]{0:T(1024)(128)(2,1)} %gain.1) | copy-start | bytes 36868
  3.6 2.4 %copy-start.3 = (s32[8,4]{0,1:T(4,128)S(1)}, s32[8,4]{0,1:T(4,128)}, u32[]{:S(2)}) copy-start(s32[8,4]{0,1:T(4,128)} %param.17) | copy-start | bytes 388
  3.6 2.4 %copy-start.4 = (f32[8,4]{0,1:T(4,128)S(1)}, f32[8,4]{0,1:T(4,128)}, u32[]{:S(2)}) copy-start(f32[8,4]{0,1:T(4,128)} %param.18) | copy-start | bytes 388
  7.3 8.5 %collective-permute-start.1 = (bf16[8,1664]{1,0:T(8,128)(2,1)S(1)}, bf16[8,1664]{1,0:T(8,128)(2,1)S(1)}, u32[]{:S(2)}, u32[]{:S(2)}) collective-permute-start(bf16[8,1664]{1,0:T(8,128)(2,1)S(1)} %get-tuple-element.42), channel_id=1, source_target_pairs={{0,16},{16,0},{32,48},{48,32},{64,80},{80,64},{96,112},{112,96},{1... | collective-permute-start | bytes 79880 | tf_op jit(solution)/shard_map/ppermute | solution.py:54
  10.5 7.5 %collective-permute-start = (bf16[8,1664]{1,0:T(8,128)(2,1)S(1)}, bf16[8,1664]{1,0:T(8,128)(2,1)S(1)}, u32[]{:S(2)}, u32[]{:S(2)}) collective-permute-start(bf16[8,1664]{1,0:T(8,128)(2,1)S(1)} %get-tuple-element.42), channel_id=1, source_target_pairs={{0,128},{16,144},{32,160},{48,176},{64,192},{80,208},{96,224},{112... | collective-permute-start | bytes 79880 | tf_op jit(solution)/shard_map/ppermute | solution.py:54
  15.7 14.1 %copy-start.6 = (bf16[2,1536,336]{1,2,0:T(8,128)(2,1)S(1)}, bf16[2,1536,336]{1,2,0:T(8,128)(2,1)}, u32[]{:S(2)}) copy-start(bf16[2,1536,336]{1,2,0:T(8,128)(2,1)} %param.19) | copy-start | bytes 6193156
  15.8 8.1 %collective-permute-start.4 = (bf16[16,1664]{1,0:T(8,128)(2,1)S(1)}, bf16[16,1664]{1,0:T(8,128)(2,1)S(1)}, u32[]{:S(2)}, u32[]{:S(2)}) collective-permute-start(bf16[16,1664]{1,0:T(8,128)(2,1)S(1)} %constant_dynamic-update-slice_fusion), channel_id=1, source_target_pairs={{0,160},{16,112},{32,192},{48,144},{64,224},{80,176},{96,0},{112,2... | collective-permute-start | bytes 159752 | tf_op jit(solution)/shard_map/ppermute | solution.py:54
  17.5 6.3 %collective-permute-start.3 = (bf16[16,1664]{1,0:T(8,128)(2,1)S(1)}, bf16[16,1664]{1,0:T(8,128)(2,1)S(1)}, u32[]{:S(2)}, u32[]{:S(2)}) collective-permute-start(bf16[16,1664]{1,0:T(8,128)(2,1)S(1)} %constant_dynamic-update-slice_fusion), channel_id=1, source_target_pairs={{0,192},{16,80},{32,224},{48,112},{64,0},{80,144},{96,32},{112,176... | collective-permute-start | bytes 159752 | tf_op jit(solution)/shard_map/ppermute | solution.py:54
  17.5 6.3 %collective-permute-start.2 = (bf16[16,1664]{1,0:T(8,128)(2,1)S(1)}, bf16[16,1664]{1,0:T(8,128)(2,1)S(1)}, u32[]{:S(2)}, u32[]{:S(2)}) collective-permute-start(bf16[16,1664]{1,0:T(8,128)(2,1)S(1)} %constant_dynamic-update-slice_fusion), channel_id=1, source_target_pairs={{0,224},{16,48},{32,0},{48,80},{64,32},{80,112},{96,64},{112,144},... | collective-permute-start | bytes 159752 | tf_op jit(solution)/shard_map/ppermute | solution.py:54
  23.9 7.3 %collective-permute-start.7 = (bf16[64,1664]{1,0:T(8,128)(2,1)S(1)}, bf16[64,1664]{1,0:T(8,128)(2,1)S(1)}, u32[]{:S(2)}, u32[]{:S(2)}) collective-permute-start(bf16[64,1664]{1,0:T(8,128)(2,1)S(1)} %constant_dynamic-update-slice_fusion.2.refs_0_), channel_id=1, source_target_pairs={{0,8},{4,12},{8,0},{12,4},{16,24},{20,28},{24,16},{28,20},{32,40},... | collective-permute-start | bytes 638984 | tf_op jit(solution)/shard_map/ppermute | solution.py:54
  26.7 9.1 %collective-permute-start.6 = (bf16[64,1664]{1,0:T(8,128)(2,1)S(1)}, bf16[64,1664]{1,0:T(8,128)(2,1)S(1)}, u32[]{:S(2)}, u32[]{:S(2)}) collective-permute-start(bf16[64,1664]{1,0:T(8,128)(2,1)S(1)} %constant_dynamic-update-slice_fusion.2.refs_0_), channel_id=1, source_target_pairs={{0,12},{4,8},{8,4},{12,0},{16,20},{20,16},{24,28},{28,24},{32,44},... | collective-permute-start | bytes 638984 | tf_op jit(solution)/shard_map/ppermute | solution.py:54
  27.0 9.6 %collective-permute-start.5 = (bf16[64,1664]{1,0:T(8,128)(2,1)S(1)}, bf16[64,1664]{1,0:T(8,128)(2,1)S(1)}, u32[]{:S(2)}, u32[]{:S(2)}) collective-permute-start(bf16[64,1664]{1,0:T(8,128)(2,1)S(1)} %constant_dynamic-update-slice_fusion.2.refs_0_), channel_id=1, source_target_pairs={{0,4},{4,0},{8,12},{12,8},{16,28},{20,24},{24,20},{28,16},{32,36},... | collective-permute-start | bytes 638984 | tf_op jit(solution)/shard_map/ppermute | solution.py:54
  30.9 9.5 %copy-start.7 = (bf16[2,1536,336]{1,2,0:T(8,128)(2,1)S(1)}, bf16[2,1536,336]{1,2,0:T(8,128)(2,1)}, u32[]{:S(2)}) copy-start(bf16[2,1536,336]{1,2,0:T(8,128)(2,1)} %param.19) | copy-start | bytes 6193156
  36.8 4.4 %collective-permute-start.8 = (bf16[256,1664]{1,0:T(8,128)(2,1)S(1)}, bf16[256,1664]{1,0:T(8,128)(2,1)S(1)}, u32[]{:S(2)}, u32[]{:S(2)}) collective-permute-start(bf16[256,1664]{1,0:T(8,128)(2,1)S(1)} %get-tuple-element.48), channel_id=1, source_target_pairs={{0,16},{16,0},{32,48},{48,32},{64,80},{80,64},{96,112},{112,96},{1... | collective-permute-start | bytes 2555912 | tf_op jit(solution)/shard_map/ppermute | solution.py:54
  41.2 8.5 %copy-start.8 = (bf16[2,1536,336]{1,2,0:T(8,128)(2,1)S(1)}, bf16[2,1536,336]{1,2,0:T(8,128)(2,1)}, u32[]{:S(2)}) copy-start(bf16[2,1536,336]{1,2,0:T(8,128)(2,1)} %param.20) | copy-start | bytes 6193156
  44.6 8.4 %collective-permute-start.9 = (bf16[176,384]{1,0:T(8,128)(2,1)S(1)}, bf16[176,384]{1,0:T(8,128)(2,1)S(1)}, u32[]{:S(2)}, u32[]{:S(2)}) collective-permute-start(bf16[176,384]{1,0:T(8,128)(2,1)S(1)} %get-tuple-element.60), channel_id=1, source_target_pairs={{0,1},{1,2},{2,3},{3,0},{4,5},{5,6},{6,7},{7,4},{8,9},{9,10},{10,1... | collective-permute-start | bytes 405512 | tf_op jit(solution)/shard_map/ppermute | solution.py:54
  46.0 9.2 %collective-permute-start.10 = (bf16[176,384]{1,0:T(8,128)(2,1)S(1)}, bf16[176,384]{1,0:T(8,128)(2,1)S(1)}, u32[]{:S(2)}, u32[]{:S(2)}) collective-permute-start(bf16[176,384]{1,0:T(8,128)(2,1)S(1)} %get-tuple-element.61), channel_id=1, source_target_pairs={{0,2},{1,3},{2,0},{3,1},{4,6},{5,7},{6,4},{7,5},{8,10},{9,11},{10,... | collective-permute-start | bytes 405512 | tf_op jit(solution)/shard_map/ppermute | solution.py:54
  48.6 6.6 %collective-permute-start.11 = (bf16[176,384]{1,0:T(8,128)(2,1)S(1)}, bf16[176,384]{1,0:T(8,128)(2,1)S(1)}, u32[]{:S(2)}, u32[]{:S(2)}) collective-permute-start(bf16[176,384]{1,0:T(8,128)(2,1)S(1)} %get-tuple-element.62), channel_id=1, source_target_pairs={{0,3},{1,0},{2,1},{3,2},{4,7},{5,4},{6,5},{7,6},{8,11},{9,8},{10,9... | collective-permute-start | bytes 405512 | tf_op jit(solution)/shard_map/ppermute | solution.py:54
  50.4 22.5 %copy-start.5 = (bf16[2,336,1536]{2,1,0:T(8,128)(2,1)S(1)}, bf16[2,336,1536]{2,1,0:T(8,128)(2,1)}, u32[]{:S(2)}) copy-start(bf16[2,336,1536]{2,1,0:T(8,128)(2,1)} %param.21) | copy-start | bytes 6193156
  51.8 5.8 %collective-permute-start.12 = (bf16[176,384]{1,0:T(8,128)(2,1)S(1)}, bf16[176,384]{1,0:T(8,128)(2,1)S(1)}, u32[]{:S(2)}, u32[]{:S(2)}) collective-permute-start(bf16[176,384]{1,0:T(8,128)(2,1)S(1)} %get-tuple-element.66), channel_id=1, source_target_pairs={{0,1},{1,2},{2,3},{3,0},{4,5},{5,6},{6,7},{7,4},{8,9},{9,10},{10,1... | collective-permute-start | bytes 405512 | tf_op jit(solution)/shard_map/ppermute | solution.py:54
  52.3 8.8 %collective-permute-start.13 = (bf16[176,384]{1,0:T(8,128)(2,1)S(1)}, bf16[176,384]{1,0:T(8,128)(2,1)S(1)}, u32[]{:S(2)}, u32[]{:S(2)}) collective-permute-start(bf16[176,384]{1,0:T(8,128)(2,1)S(1)} %get-tuple-element.67), channel_id=1, source_target_pairs={{0,2},{1,3},{2,0},{3,1},{4,6},{5,7},{6,4},{7,5},{8,10},{9,11},{10,... | collective-permute-start | bytes 405512 | tf_op jit(solution)/shard_map/ppermute | solution.py:54
  53.1 8.0 %collective-permute-start.14 = (bf16[176,384]{1,0:T(8,128)(2,1)S(1)}, bf16[176,384]{1,0:T(8,128)(2,1)S(1)}, u32[]{:S(2)}, u32[]{:S(2)}) collective-permute-start(bf16[176,384]{1,0:T(8,128)(2,1)S(1)} %get-tuple-element.68), channel_id=1, source_target_pairs={{0,3},{1,0},{2,1},{3,2},{4,7},{5,4},{6,5},{7,6},{8,11},{9,8},{10,9... | collective-permute-start | bytes 405512 | tf_op jit(solution)/shard_map/ppermute | solution.py:54
  61.6 5.6 %collective-permute-start.17 = (bf16[168,384]{1,0:T(8,128)(2,1)S(1)}, bf16[168,384]{1,0:T(8,128)(2,1)S(1)}, u32[]{:S(2)}, u32[]{:S(2)}) collective-permute-start(bf16[168,384]{1,0:T(8,128)(2,1)S(1)} %shard_map.128.hidden0), channel_id=1, source_target_pairs={{0,1},{1,2},{2,3},{3,0},{4,5},{5,6},{6,7},{7,4},{8,9},{9,10},{10,1... | collective-permute-start | bytes 387080 | tf_op jit(solution)/shard_map/ppermute | solution.py:54
  63.3 8.4 %collective-permute-start.16 = (bf16[168,384]{1,0:T(8,128)(2,1)S(1)}, bf16[168,384]{1,0:T(8,128)(2,1)S(1)}, u32[]{:S(2)}, u32[]{:S(2)}) collective-permute-start(bf16[168,384]{1,0:T(8,128)(2,1)S(1)} %shard_map.128.hidden0), channel_id=1, source_target_pairs={{0,2},{1,3},{2,0},{3,1},{4,6},{5,7},{6,4},{7,5},{8,10},{9,11},{10,... | collective-permute-start | bytes 387080 | tf_op jit(solution)/shard_map/ppermute | solution.py:54
  66.0 5.7 %collective-permute-start.15 = (bf16[168,384]{1,0:T(8,128)(2,1)S(1)}, bf16[168,384]{1,0:T(8,128)(2,1)S(1)}, u32[]{:S(2)}, u32[]{:S(2)}) collective-permute-start(bf16[168,384]{1,0:T(8,128)(2,1)S(1)} %shard_map.128.hidden0), channel_id=1, source_target_pairs={{0,3},{1,0},{2,1},{3,2},{4,7},{5,4},{6,5},{7,6},{8,11},{9,8},{10,9... | collective-permute-start | bytes 387080 | tf_op jit(solution)/shard_map/ppermute | solution.py:54
  73.7 3.4 %collective-permute-start.18 = (bf16[256,1536]{1,0:T(8,128)(2,1)S(1)}, bf16[256,1536]{1,0:T(8,128)(2,1)S(1)}, u32[]{:S(2)}, u32[]{:S(2)}) collective-permute-start(bf16[256,1536]{1,0:T(8,128)(2,1)S(1)} %convolution_convert_fusion), channel_id=1, source_target_pairs={{0,16},{16,0},{32,48},{48,32},{64,80},{80,64},{96,112},{112,96},{1... | collective-permute-start | bytes 2359304 | tf_op jit(solution)/shard_map/ppermute | solution.py:54
  77.5 5.8 %collective-permute-start.19 = (bf16[64,1536]{1,0:T(8,128)(2,1)S(1)}, bf16[64,1536]{1,0:T(8,128)(2,1)S(1)}, u32[]{:S(2)}, u32[]{:S(2)}) collective-permute-start(bf16[64,1536]{1,0:T(8,128)(2,1)S(1)} %get-tuple-element.72), channel_id=1, source_target_pairs={{0,4},{4,0},{8,12},{12,8},{16,28},{20,24},{24,20},{28,16},{32,36},... | collective-permute-start | bytes 589832 | tf_op jit(solution)/shard_map/ppermute | solution.py:54
  79.9 5.9 %collective-permute-start.20 = (bf16[64,1536]{1,0:T(8,128)(2,1)S(1)}, bf16[64,1536]{1,0:T(8,128)(2,1)S(1)}, u32[]{:S(2)}, u32[]{:S(2)}) collective-permute-start(bf16[64,1536]{1,0:T(8,128)(2,1)S(1)} %get-tuple-element.73), channel_id=1, source_target_pairs={{0,12},{4,8},{8,4},{12,0},{16,20},{20,16},{24,28},{28,24},{32,44},... | collective-permute-start | bytes 589832 | tf_op jit(solution)/shard_map/ppermute | solution.py:54
  79.9 10.7 %collective-permute-start.21 = (bf16[64,1536]{1,0:T(8,128)(2,1)S(1)}, bf16[64,1536]{1,0:T(8,128)(2,1)S(1)}, u32[]{:S(2)}, u32[]{:S(2)}) collective-permute-start(bf16[64,1536]{1,0:T(8,128)(2,1)S(1)} %get-tuple-element.74), channel_id=1, source_target_pairs={{0,8},{4,12},{8,0},{12,4},{16,24},{20,28},{24,16},{28,20},{32,40},... | collective-permute-start | bytes 589832 | tf_op jit(solution)/shard_map/ppermute | solution.py:54
  90.8 7.1 %collective-permute-start.23 = (bf16[16,1536]{1,0:T(8,128)(2,1)S(1)}, bf16[16,1536]{1,0:T(8,128)(2,1)S(1)}, u32[]{:S(2)}, u32[]{:S(2)}) collective-permute-start(bf16[16,1536]{1,0:T(8,128)(2,1)S(1)} %get-tuple-element.77), channel_id=1, source_target_pairs={{0,32},{16,240},{32,64},{48,16},{64,96},{80,48},{96,128},{112,80},... | collective-permute-start | bytes 147464 | tf_op jit(solution)/shard_map/ppermute | solution.py:54
  92.0 5.9 %collective-permute-start.24 = (bf16[16,1536]{1,0:T(8,128)(2,1)S(1)}, bf16[16,1536]{1,0:T(8,128)(2,1)S(1)}, u32[]{:S(2)}, u32[]{:S(2)}) collective-permute-start(bf16[16,1536]{1,0:T(8,128)(2,1)S(1)} %get-tuple-element.78), channel_id=1, source_target_pairs={{0,64},{16,208},{32,96},{48,240},{64,128},{80,16},{96,160},{112,48... | collective-permute-start | bytes 147464 | tf_op jit(solution)/shard_map/ppermute | solution.py:54
  93.1 5.1 %collective-permute-start.25 = (bf16[16,1536]{1,0:T(8,128)(2,1)S(1)}, bf16[16,1536]{1,0:T(8,128)(2,1)S(1)}, u32[]{:S(2)}, u32[]{:S(2)}) collective-permute-start(bf16[16,1536]{1,0:T(8,128)(2,1)S(1)} %get-tuple-element.79), channel_id=1, source_target_pairs={{0,96},{16,176},{32,128},{48,208},{64,160},{80,240},{96,192},{112,... | collective-permute-start | bytes 147464 | tf_op jit(solution)/shard_map/ppermute | solution.py:54
  95.4 6.6 %collective-permute-start.22 = (bf16[8,1536]{1,0:T(8,128)(2,1)S(1)}, bf16[8,1536]{1,0:T(8,128)(2,1)S(1)}, u32[]{:S(2)}, u32[]{:S(2)}) collective-permute-start(bf16[8,1536]{1,0:T(8,128)(2,1)S(1)} %slice.67), channel_id=1, source_target_pairs={{0,128},{16,144},{32,160},{48,176},{64,192},{80,208},{96,224},{112... | collective-permute-start | bytes 73736 | tf_op jit(solution)/shard_map/ppermute | solution.py:54
  98.2 3.8 %collective-permute-start.26 = (bf16[8,1536]{1,0:T(8,128)(2,1)S(1)}, bf16[8,1536]{1,0:T(8,128)(2,1)S(1)}, u32[]{:S(2)}, u32[]{:S(2)}) collective-permute-start(bf16[8,1536]{1,0:T(8,128)(2,1)S(1)} %slice.83), channel_id=1, source_target_pairs={{0,16},{16,0},{32,48},{48,32},{64,80},{80,64},{96,112},{112,96},{1... | collective-permute-start | bytes 73736 | tf_op jit(solution)/shard_map/ppermute | solution.py:54

commit v5 on v4

--- a/solution.py
+++ b/solution.py
@@ -350,10 +350,11 @@
     onehots, stats, share, ranks = list_rows(
         place, own_notes, other_notes, w_gate.shape[0], y_size
     )
-    gate_sums, up_sums = project(w_gate, own_rows), project(w_up, own_rows)
-    gate_parts = pack(place, gate_sums, project(w_gate, other_rows), onehots, stats)
-    other_rows, gate_parts = lax.optimization_barrier((other_rows, gate_parts))
-    up_parts = pack(place, up_sums, project(w_up, other_rows), onehots, gains)
+    gate_sums = [project(w_gate, r) for r in (own_rows, other_rows)]
+    gate_parts = pack(place, *gate_sums, onehots, stats)
+    own_rows, other_rows, gate_parts = lax.optimization_barrier((own_rows, other_rows, gate_parts))
+    up_sums = [project(w_up, r) for r in (own_rows, other_rows)]
+    up_parts = pack(place, *up_sums, onehots, gains)
     parts = []
     for packed in (gate_parts, up_parts):
         parts += [packed[0]] + [to_y(packed[k], k) for k in range(1, y_size)]
@@ -361,18 +362,24 @@
     got = {k: to_y(hidden, -k) for k in (1, 3, 2)}
     hidden = scatter(place, [hidden] + [got[k] for k in range(1, y_size)], ranks)
     hidden = hidden.reshape(down.shape[0], -1)
-    n = own.shape[0]
-
-    def back_down(at):
-        return jnp.einsum("fr,fd->rd", hidden[:, at : at + n], down, preferred_element_type=f32)
-
-    other = swap_core(back_down(n).astype(bf16))
-    total = lax.optimization_barrier(back_down(0)) + other.astype(f32)
-    n = n // 4
-    total, sent = lax.optimization_barrier(
-        (total[:n], [total[k * n : (k + 1) * n].astype(bf16) for k in range(1, 4)])
-    )
-    total = total + sum(along_x(sent[k], k).astype(f32) for k in range(3))
+    n = own.shape[0] // 4
+
+    def over_cores(hidden, first, last):
+        def output(at):
+            part = hidden[:, at + first * n : at + last * n]
+            return jnp.einsum("fr,fd->rd", part, down, preferred_element_type=f32)
+
+        other = swap_core(output(4 * n).astype(bf16))
+        return lax.optimization_barrier(output(0)) + other.astype(f32)
+
+    distant = over_cores(hidden, 3, 4).astype(bf16)
+    distant, hidden = lax.optimization_barrier((distant, hidden))
+    total = over_cores(hidden, 0, 3)
+    total, *sent = lax.optimization_barrier(
+        (total[:n], total[n : 2 * n].astype(bf16), total[2 * n :].astype(bf16))
+    )
+    got = [along_x(part, k) for k, part in enumerate(sent + [distant])]
+    total = total + sum(part.astype(f32) for part in got)
     n = 2 * rows
     mine, across, *chip = lax.optimization_barrier(
         (total[:rows], total[rows:n].astype(bf16))

time: 103 us -> 103 us (level); the launches traced: 103 us -> 101 us
  waiting for transfers between devices: 35.3 us -> 32.8 us
    ppermute x27 -> x28, waiting for transfers between devices: 35.3 us -> 32.8 us  [send(): return lax.ppermute(x, axes, pairs)]
    dot_general x2 -> x4, matrix products: 1.58 us -> 2.47 us  [output(): return jnp.einsum('fr,fd->rd', part, down, preferred_element_type=f32)]
    ppermute x27 -> x28, starting transfers between devices: 43.4 us -> 43.6 us  [send(): return lax.ppermute(x, axes, pairs)]
  transfers between devices with their start and end apart: 27 -> 28, of which waited for: 15 -> 15; matrix products, arithmetic and copies ran while one was open for 8% -> 9% of each run, Pallas kernels for 1% -> 1%
where the time goes in v5:
time: 103 us; the launch traced here: 101 us
  starting transfers between devices  43.6 us (42%)
  waiting for transfers between devices  32.8 us (32%)
  matrix products  13.5 us (13%)
  Pallas kernels  7.02 us (7%)
  local copies, waits for them, and re-layouts  2.12 us (2%)
  other arithmetic  1.24 us (1%)
    ppermute x28, starting transfers between devices, send(): return lax.ppermute(x, axes, pairs)  43.6 us
    ppermute x28, waiting for transfers between devices, send(): return lax.ppermute(x, axes, pairs)  32.8 us
    dot_general x4, matrix products, project(): jnp.einsum('edf,rd->efr', weight, tokens, preferred_element_type=f32)  4.66 us
    dot_general x2, matrix products, per_device(): jnp.einsum('edf,d->ef', w.astype(f32), gain).reshape(y_size, -1)  2.96 us
    pallas_call x2, Pallas kernels, pack(): pl.pallas_call(pack_kernel, out_shape=[jax.ShapeDtypeStruct((experts * fa...  2.68 us
    dot_general x4, matrix products, output(): return jnp.einsum('fr,fd->rd', part, down, preferred_element_type=f32)  2.47 us
  transfers between devices with their start and end apart: 28, of which 15 were waited for; matrix products, arithmetic and copies ran while one was open for 9% of the time, Pallas kernels for 1%

profile of v5, /device:TPU:1, one launch (start us, length us, event | category | flops | bytes accessed | tf_op | source)
XLA Modules:
  0.0 101.3 jit_solution(694104510135024652)
XLA Ops:
  0.7 1.6 %copy-done = bf16[8,512,256]{2,1,0:T(8,128)(2,1)S(1)} copy-done((bf16[8,512,256]{2,1,0:T(8,128)(2,1)S(1)}, bf16[8,512,256]{2,1,0:T(8,128)(2,1)}, u32[]{:S(2)}) %copy-start) | copy-done | bytes 2097176
  2.2 1.4 %fusion.16 = f32[8,2,6,512]{3,2,1,0:T(8,128)S(1)} fusion(s32[8]{0:T(128)} %param.14, bf16[8,2,6,128]{3,0,2,1:T(8,128)(2,1)} %bitcast.81, bf16[8,512,256]{2,1,0:T(8,128)(2,1)S(1)} %copy-done), kind=kOutput, calls=%fused_computation.21 | convolution fusion | flops 12730368 | bytes 2318368 | tf_op jit(solution)/shard_map/rhgd,rlhd->rhgl/dot_general | solution.py:26
  3.9 2.0 %fusion.1 = f32[8,2,6,128]{3,2,1,0:T(8,128)S(1)} fusion(f32[8,2,6]{2,1,0:T(2,128)S(1)} %fusion.38, f32[8,2,6,512]{3,2,1,0:T(8,128)S(1)} %fusion.16, bf16[8,512,256]{2,1,0:T(8,128)(2,1)} %param.13), kind=kOutput, calls=%fused_computation.3 | convolution fusion | flops 12730975 | bytes 2343296 | tf_op jit(solution)/shard_map/rhgl,rlhd->rhgd/dot_general | solution.py:36
  6.0 1.3 %shard_map.122 = (bf16[8,1536]{1,0:T(8,128)(2,1)}, bf16[8,1664]{1,0:T(8,128)(2,1)S(1)}) custom-call(s32[2]{0:T(128)S(1)} %pad_add_fusion.place, f32[8,1536]{1,0:T(8,128)S(1)} %reshape.142.attended, bf16[8,1536]{1,0:T(8,128)(2,1)S(1)} %copy-done.1, bf16[6144]{0:T(1024)(128)(2,1)S(1)} %copy-done.2, s32[4,8]{1,0:T(4,128)S(1)} %bitcast.73, f32[4,8]{1,0:T(4,128)S(1)} %bitcast.74), custom_call_target="tpu_custom_call" | custom-call | flops 65536 | bytes 65536 | tf_op jit(solution)/shard_map/pallas_call | solution.py:108
  7.3 3.2 %collective-permute-start.1 = (bf16[8,1664]{1,0:T(8,128)(2,1)S(1)}, bf16[8,1664]{1,0:T(8,128)(2,1)S(1)}, u32[]{:S(2)}, u32[]{:S(2)}) collective-permute-start(bf16[8,1664]{1,0:T(8,128)(2,1)S(1)} %get-tuple-element.44), channel_id=1, source_target_pairs={{0,16},{16,0},{32,48},{48,32},{64,80},{80,64},{96,112},{112,96},{1... | collective-permute-start | bytes 79880 | tf_op jit(solution)/shard_map/ppermute | solution.py:54
  10.5 5.2 %collective-permute-start = (bf16[8,1664]{1,0:T(8,128)(2,1)S(1)}, bf16[8,1664]{1,0:T(8,128)(2,1)S(1)}, u32[]{:S(2)}, u32[]{:S(2)}) collective-permute-start(bf16[8,1664]{1,0:T(8,128)(2,1)S(1)} %get-tuple-element.44), channel_id=1, source_target_pairs={{0,128},{16,144},{32,160},{48,176},{64,192},{80,208},{96,224},{112... | collective-permute-start | bytes 79880 | tf_op jit(solution)/shard_map/ppermute | solution.py:54
  15.8 1.7 %collective-permute-start.4 = (bf16[16,1664]{1,0:T(8,128)(2,1)S(1)}, bf16[16,1664]{1,0:T(8,128)(2,1)S(1)}, u32[]{:S(2)}, u32[]{:S(2)}) collective-permute-start(bf16[16,1664]{1,0:T(8,128)(2,1)S(1)} %constant_dynamic-update-slice_fusion), channel_id=1, source_target_pairs={{0,160},{16,112},{32,192},{48,144},{64,224},{80,176},{96,0},{112,2... | collective-permute-start | bytes 159752 | tf_op jit(solution)/shard_map/ppermute | solution.py:54
  18.1 5.8 %collective-permute-done.2 = bf16[16,1664]{1,0:T(8,128)(2,1)S(1)} collective-permute-done((bf16[16,1664]{1,0:T(8,128)(2,1)S(1)}, bf16[16,1664]{1,0:T(8,128)(2,1)S(1)}, u32[]{:S(2)}, u32[]{:S(2)}) %collective-permute-start.2) | collective-permute-done | bytes 53280 | tf_op jit(solution)/shard_map/ppermute | solution.py:54
  23.9 2.8 %collective-permute-start.7 = (bf16[64,1664]{1,0:T(8,128)(2,1)S(1)}, bf16[64,1664]{1,0:T(8,128)(2,1)S(1)}, u32[]{:S(2)}, u32[]{:S(2)}) collective-permute-start(bf16[64,1664]{1,0:T(8,128)(2,1)S(1)} %constant_dynamic-update-slice_fusion.2.refs_0_), channel_id=1, source_target_pairs={{0,8},{4,12},{8,0},{12,4},{16,24},{20,28},{24,16},{28,20},{32,40},... | collective-permute-start | bytes 638984 | tf_op jit(solution)/shard_map/ppermute | solution.py:54
  27.6 2.2 %fusion.40 = f32[1,2,336]{2,0,1:T(1,128)S(1)} fusion(bf16[1536,1,1]{0,1,2:T(2,128)(2,1)S(1)} %reshape.146, bf16[2,1536,336]{1,2,0:T(8,128)(2,1)} %param.20), kind=kOutput, calls=%fused_computation.67 | convolution fusion | flops 2064384 | bytes 2070144 | tf_op jit(solution)/shard_map/edf,d->ef/dot_general | solution.py:336
  29.9 0.7 fusion.39
  31.2 4.7 %collective-permute-done.6.refs_2_ = bf16[64,1664]{1,0:T(8,128)(2,1)S(1)} collective-permute-done((bf16[64,1664]{1,0:T(8,128)(2,1)S(1)}, bf16[64,1664]{1,0:T(8,128)(2,1)S(1)}, u32[]{:S(2)}, u32[]{:S(2)}) %collective-permute-start.6) | collective-permute-done | bytes 213024 | tf_op jit(solution)/shard_map/ppermute | solution.py:54
  35.9 0.8 collective-permute-done.5.refs_1_
  36.8 1.3 %collective-permute-start.8 = (bf16[256,1664]{1,0:T(8,128)(2,1)S(1)}, bf16[256,1664]{1,0:T(8,128)(2,1)S(1)}, u32[]{:S(2)}, u32[]{:S(2)}) collective-permute-start(bf16[256,1664]{1,0:T(8,128)(2,1)S(1)} %get-tuple-element.51), channel_id=1, source_target_pairs={{0,16},{16,0},{32,48},{48,32},{64,80},{80,64},{96,112},{112,96},{1... | collective-permute-start | bytes 2555912 | tf_op jit(solution)/shard_map/ppermute | solution.py:54
  38.1 2.5 %fusion.8.own = bf16[2,336,256]{2,1,0:T(8,128)(2,1)S(1)} fusion(bf16[2,1536,336]{1,2,0:T(8,128)(2,1)} %param.19, bf16[256,1536]{1,0:T(8,128)(2,1)S(1)} %get-tuple-element.65), kind=kOutput, calls=%fused_computation.14 | convolution fusion | flops 528654336 | bytes 3194880 | tf_op jit(solution)/shard_map/edf,rd->efr/dot_general | solution.py:329
  40.6 0.7 fusion.9.other
  41.4 1.3 %shard_map.125 = (bf16[2,512,384]{2,1,0:T(8,128)(2,1)S(1)}, f32[4,8,384]{2,1,0:T(8,128)S(1)}, f32[8,384]{1,0:T(8,128)S(1)}, f32[128,512]{1,0:T(8,128)S(1)}) custom-call(s32[2]{0:T(128)S(1)} %pad_add_fusion.place, bf16[256,128]{1,0:T(8,128)(2,1)S(1)} %get-tuple-element.53.own, bf16[256,128]{1,0:T(8,128)(2,1)S(1)} %get-tuple-element.54.other), custom_call_target="tpu_custom_call" | custom-call | flops 134217728 | bytes 1048576 | tf_op jit(solution)/shard_map/pallas_call | solution.py:162
  42.7 1.3 %shard_map.126 = (bf16[176,384]{1,0:T(8,128)(2,1)S(1)}, bf16[176,384]{1,0:T(8,128)(2,1)S(1)}, bf16[176,384]{1,0:T(8,128)(2,1)S(1)}, bf16[176,384]{1,0:T(8,128)(2,1)S(1)}) custom-call(s32[2]{0:T(128)S(1)} %pad_add_fusion.place, bf16[2,336,256]{2,1,0:T(8,128)(2,1)S(1)} %fusion.8.own, bf16[2,336,256]{2,1,0:T(8,128)(2,1)S(1)} %fusion.9.other, ...), custom_call_target="tpu_custom_call" | custom-call | flops 268435456 | bytes 2097152 | tf_op jit(solution)/shard_map/pallas_call | solution.py:199
  44.1 1.4 %collective-permute-start.9 = (bf16[176,384]{1,0:T(8,128)(2,1)S(1)}, bf16[176,384]{1,0:T(8,128)(2,1)S(1)}, u32[]{:S(2)}, u32[]{:S(2)}) collective-permute-start(bf16[176,384]{1,0:T(8,128)(2,1)S(1)} %get-tuple-element.62), channel_id=1, source_target_pairs={{0,1},{1,2},{2,3},{3,0},{4,5},{5,6},{6,7},{7,4},{8,9},{9,10},{10,1... | collective-permute-start | bytes 405512 | tf_op jit(solution)/shard_map/ppermute | solution.py:54
  45.4 2.6 %collective-permute-start.10 = (bf16[176,384]{1,0:T(8,128)(2,1)S(1)}, bf16[176,384]{1,0:T(8,128)(2,1)S(1)}, u32[]{:S(2)}, u32[]{:S(2)}) collective-permute-start(bf16[176,384]{1,0:T(8,128)(2,1)S(1)} %get-tuple-element.63), channel_id=1, source_target_pairs={{0,2},{1,3},{2,0},{3,1},{4,6},{5,7},{6,4},{7,5},{8,10},{9,11},{10,... | collective-permute-start | bytes 405512 | tf_op jit(solution)/shard_map/ppermute | solution.py:54
  48.0 1.1 %collective-permute-start.11 = (bf16[176,384]{1,0:T(8,128)(2,1)S(1)}, bf16[176,384]{1,0:T(8,128)(2,1)S(1)}, u32[]{:S(2)}, u32[]{:S(2)}) collective-permute-start(bf16[176,384]{1,0:T(8,128)(2,1)S(1)} %get-tuple-element.64), channel_id=1, source_target_pairs={{0,3},{1,0},{2,1},{3,2},{4,7},{5,4},{6,5},{7,6},{8,11},{9,8},{10,9... | collective-permute-start | bytes 405512 | tf_op jit(solution)/shard_map/ppermute | solution.py:54
  49.1 0.7 fusion.10.own
  49.9 0.7 fusion.11.other
  50.6 1.3 %shard_map.127 = (bf16[176,384]{1,0:T(8,128)(2,1)S(1)}, bf16[176,384]{1,0:T(8,128)(2,1)S(1)}, bf16[176,384]{1,0:T(8,128)(2,1)S(1)}, bf16[176,384]{1,0:T(8,128)(2,1)S(1)}) custom-call(s32[2]{0:T(128)S(1)} %pad_add_fusion.place, bf16[2,336,256]{2,1,0:T(8,128)(2,1)S(1)} %fusion.10.own, bf16[2,336,256]{2,1,0:T(8,128)(2,1)S(1)} %fusion.11.other, ...), custom_call_target="tpu_custom_call" | custom-call | flops 268435456 | bytes 2097152 | tf_op jit(solution)/shard_map/pallas_call | solution.py:199
  52.4 0.8 collective-permute-start.13
  53.2 1.7 %collective-permute-start.14 = (bf16[176,384]{1,0:T(8,128)(2,1)S(1)}, bf16[176,384]{1,0:T(8,128)(2,1)S(1)}, u32[]{:S(2)}, u32[]{:S(2)}) collective-permute-start(bf16[176,384]{1,0:T(8,128)(2,1)S(1)} %get-tuple-element.71), channel_id=1, source_target_pairs={{0,3},{1,0},{2,1},{3,2},{4,7},{5,4},{6,5},{7,6},{8,11},{9,8},{10,9... | collective-permute-start | bytes 405512 | tf_op jit(solution)/shard_map/ppermute | solution.py:54
  54.9 2.6 %collective-permute-done.12.refs_5_ = bf16[176,384]{1,0:T(8,128)(2,1)S(1)} collective-permute-done((bf16[176,384]{1,0:T(8,128)(2,1)S(1)}, bf16[176,384]{1,0:T(8,128)(2,1)S(1)}, u32[]{:S(2)}, u32[]{:S(2)}) %collective-permute-start.12) | collective-permute-done | bytes 135200 | tf_op jit(solution)/shard_map/ppermute | solution.py:54
  57.5 2.9 %collective-permute-done.13.refs_6_ = bf16[176,384]{1,0:T(8,128)(2,1)S(1)} collective-permute-done((bf16[176,384]{1,0:T(8,128)(2,1)S(1)}, bf16[176,384]{1,0:T(8,128)(2,1)S(1)}, u32[]{:S(2)}, u32[]{:S(2)}) %collective-permute-start.13) | collective-permute-done | bytes 135200 | tf_op jit(solution)/shard_map/ppermute | solution.py:54
  61.3 0.9 collective-permute-start.17
  62.3 3.9 %collective-permute-start.16 = (bf16[168,384]{1,0:T(8,128)(2,1)S(1)}, bf16[168,384]{1,0:T(8,128)(2,1)S(1)}, u32[]{:S(2)}, u32[]{:S(2)}) collective-permute-start(bf16[168,384]{1,0:T(8,128)(2,1)S(1)} %shard_map.128.hidden0), channel_id=1, source_target_pairs={{0,2},{1,3},{2,0},{3,1},{4,6},{5,7},{6,4},{7,5},{8,10},{9,11},{10,... | collective-permute-start | bytes 387080 | tf_op jit(solution)/shard_map/ppermute | solution.py:54
  66.2 1.1 %collective-permute-done.17.hidden3 = bf16[168,384]{1,0:T(8,128)(2,1)S(1)} collective-permute-done((bf16[168,384]{1,0:T(8,128)(2,1)S(1)}, bf16[168,384]{1,0:T(8,128)(2,1)S(1)}, u32[]{:S(2)}, u32[]{:S(2)}) %collective-permute-start.17) | collective-permute-done | bytes 129056 | tf_op jit(solution)/shard_map/ppermute | solution.py:54
  67.3 4.6 %collective-permute-done.16.hidden2 = bf16[168,384]{1,0:T(8,128)(2,1)S(1)} collective-permute-done((bf16[168,384]{1,0:T(8,128)(2,1)S(1)}, bf16[168,384]{1,0:T(8,128)(2,1)S(1)}, u32[]{:S(2)}, u32[]{:S(2)}) %collective-permute-start.16) | collective-permute-done | bytes 129056 | tf_op jit(solution)/shard_map/ppermute | solution.py:54
  71.9 1.1 %shard_map.129 = bf16[4,168,512]{2,1,0:T(8,128)(2,1)S(1)} custom-call(s32[2]{0:T(128)S(1)} %pad_add_fusion.place, bf16[168,384]{1,0:T(8,128)(2,1)S(1)} %shard_map.128.hidden0, bf16[168,384]{1,0:T(8,128)(2,1)S(1)} %collective-permute-done.15.hidden1, bf16[168,384]{1,0:T(8,128)(2,1)S(1)} %collective-permute-done.16.hidden2, ...), custom_call_target="tpu_custom_call" | custom-call | flops 268435456 | bytes 1048576 | tf_op jit(solution)/shard_map/pallas_call | solution.py:294
  73.6 1.5 %collective-permute-start.18 = (bf16[64,1536]{1,0:T(8,128)(2,1)S(1)}, bf16[64,1536]{1,0:T(8,128)(2,1)S(1)}, u32[]{:S(2)}, u32[]{:S(2)}) collective-permute-start(bf16[64,1536]{1,0:T(8,128)(2,1)S(1)} %convolution_convert_fusion.1), channel_id=1, source_target_pairs={{0,16},{16,0},{32,48},{48,32},{64,80},{80,64},{96,112},{112,96},{1... | collective-permute-start | bytes 589832 | tf_op jit(solution)/shard_map/ppermute | solution.py:54
  76.2 0.7 convolution_convert_fusion
  77.3 2.6 %collective-permute-start.22 = (bf16[64,1536]{1,0:T(8,128)(2,1)S(1)}, bf16[64,1536]{1,0:T(8,128)(2,1)S(1)}, u32[]{:S(2)}, u32[]{:S(2)}) collective-permute-start(bf16[64,1536]{1,0:T(8,128)(2,1)S(1)} %add_convert_fusion), channel_id=1, source_target_pairs={{0,8},{4,12},{8,0},{12,4},{16,24},{20,28},{24,16},{28,20},{32,40},... | collective-permute-start | bytes 589832 | tf_op jit(solution)/shard_map/ppermute | solution.py:54
  80.0 0.7 fusion.24
  80.9 1.0 %collective-permute-start.20 = (bf16[64,1536]{1,0:T(8,128)(2,1)S(1)}, bf16[64,1536]{1,0:T(8,128)(2,1)S(1)}, u32[]{:S(2)}, u32[]{:S(2)}) collective-permute-start(bf16[64,1536]{1,0:T(8,128)(2,1)S(1)} %get-tuple-element.76), channel_id=1, source_target_pairs={{0,4},{4,0},{8,12},{12,8},{16,28},{20,24},{24,20},{28,16},{32,36},... | collective-permute-start | bytes 589832 | tf_op jit(solution)/shard_map/ppermute | solution.py:54
  81.9 3.3 %collective-permute-done.22 = bf16[64,1536]{1,0:T(8,128)(2,1)S(1)} collective-permute-done((bf16[64,1536]{1,0:T(8,128)(2,1)S(1)}, bf16[64,1536]{1,0:T(8,128)(2,1)S(1)}, u32[]{:S(2)}, u32[]{:S(2)}) %collective-permute-start.22) | collective-permute-done | bytes 196640 | tf_op jit(solution)/shard_map/ppermute | solution.py:54
  85.2 4.1 %collective-permute-done.20 = bf16[64,1536]{1,0:T(8,128)(2,1)S(1)} collective-permute-done((bf16[64,1536]{1,0:T(8,128)(2,1)S(1)}, bf16[64,1536]{1,0:T(8,128)(2,1)S(1)}, u32[]{:S(2)}, u32[]{:S(2)}) %collective-permute-start.20) | collective-permute-done | bytes 196640 | tf_op jit(solution)/shard_map/ppermute | solution.py:54
  89.6 1.2 %collective-permute-start.24 = (bf16[16,1536]{1,0:T(8,128)(2,1)S(1)}, bf16[16,1536]{1,0:T(8,128)(2,1)S(1)}, u32[]{:S(2)}, u32[]{:S(2)}) collective-permute-start(bf16[16,1536]{1,0:T(8,128)(2,1)S(1)} %get-tuple-element.81), channel_id=1, source_target_pairs={{0,32},{16,240},{32,64},{48,16},{64,96},{80,48},{96,128},{112,80},... | collective-permute-start | bytes 147464 | tf_op jit(solution)/shard_map/ppermute | solution.py:54
  90.8 1.1 %collective-permute-start.25 = (bf16[16,1536]{1,0:T(8,128)(2,1)S(1)}, bf16[16,1536]{1,0:T(8,128)(2,1)S(1)}, u32[]{:S(2)}, u32[]{:S(2)}) collective-permute-start(bf16[16,1536]{1,0:T(8,128)(2,1)S(1)} %get-tuple-element.82), channel_id=1, source_target_pairs={{0,64},{16,208},{32,96},{48,240},{64,128},{80,16},{96,160},{112,48... | collective-permute-start | bytes 147464 | tf_op jit(solution)/shard_map/ppermute | solution.py:54
  91.9 2.2 %collective-permute-start.26 = (bf16[16,1536]{1,0:T(8,128)(2,1)S(1)}, bf16[16,1536]{1,0:T(8,128)(2,1)S(1)}, u32[]{:S(2)}, u32[]{:S(2)}) collective-permute-start(bf16[16,1536]{1,0:T(8,128)(2,1)S(1)} %get-tuple-element.83), channel_id=1, source_target_pairs={{0,96},{16,176},{32,128},{48,208},{64,160},{80,240},{96,192},{112,... | collective-permute-start | bytes 147464 | tf_op jit(solution)/shard_map/ppermute | solution.py:54
  94.1 2.6 %collective-permute-start.23 = (bf16[8,1536]{1,0:T(8,128)(2,1)S(1)}, bf16[8,1536]{1,0:T(8,128)(2,1)S(1)}, u32[]{:S(2)}, u32[]{:S(2)}) collective-permute-start(bf16[8,1536]{1,0:T(8,128)(2,1)S(1)} %slice.69), channel_id=1, source_target_pairs={{0,128},{16,144},{32,160},{48,176},{64,192},{80,208},{96,224},{112... | collective-permute-start | bytes 73736 | tf_op jit(solution)/shard_map/ppermute | solution.py:54
  96.7 0.7 collective-permute-done.26
  97.5 2.4 %collective-permute-start.27 = (bf16[8,1536]{1,0:T(8,128)(2,1)S(1)}, bf16[8,1536]{1,0:T(8,128)(2,1)S(1)}, u32[]{:S(2)}, u32[]{:S(2)}) collective-permute-start(bf16[8,1536]{1,0:T(8,128)(2,1)S(1)} %slice.89), channel_id=1, source_target_pairs={{0,16},{16,0},{32,48},{48,32},{64,80},{80,64},{96,112},{112,96},{1... | collective-permute-start | bytes 73736 | tf_op jit(solution)/shard_map/ppermute | solution.py:54
  99.8 0.8 collective-permute-done.23
  100.7 0.6 fusion.31
  (78 shorter events, 6.7 us)
Async XLA Ops:
  0.6 1.6 %copy-start = (bf16[8,512,256]{2,1,0:T(8,128)(2,1)S(1)}, bf16[8,512,256]{2,1,0:T(8,128)(2,1)}, u32[]{:S(2)}) copy-start(bf16[8,512,256]{2,1,0:T(8,128)(2,1)} %param.12) | copy-start | bytes 6291460
  3.6 2.4 %copy-start.1 = (bf16[8,1536]{1,0:T(8,128)(2,1)S(1)}, bf16[8,1536]{1,0:T(8,128)(2,1)}, u32[]{:S(2)}) copy-start(bf16[8,1536]{1,0:T(8,128)(2,1)} %residual.1) | copy-start | bytes 73732
  3.6 2.4 %copy-start.2 = (bf16[6144]{0:T(1024)(128)(2,1)S(1)}, bf16[6144]{0:T(1024)(128)(2,1)}, u32[]{:S(2)}) copy-start(bf16[6144]{0:T(1024)(128)(2,1)} %gain.1) | copy-start | bytes 36868
  3.6 2.4 %copy-start.3 = (s32[8,4]{0,1:T(4,128)S(1)}, s32[8,4]{0,1:T(4,128)}, u32[]{:S(2)}) copy-start(s32[8,4]{0,1:T(4,128)} %param.17) | copy-start | bytes 388
  3.6 2.4 %copy-start.4 = (f32[8,4]{0,1:T(4,128)S(1)}, f32[8,4]{0,1:T(4,128)}, u32[]{:S(2)}) copy-start(f32[8,4]{0,1:T(4,128)} %param.18) | copy-start | bytes 388
  7.3 8.5 %collective-permute-start.1 = (bf16[8,1664]{1,0:T(8,128)(2,1)S(1)}, bf16[8,1664]{1,0:T(8,128)(2,1)S(1)}, u32[]{:S(2)}, u32[]{:S(2)}) collective-permute-start(bf16[8,1664]{1,0:T(8,128)(2,1)S(1)} %get-tuple-element.44), channel_id=1, source_target_pairs={{0,16},{16,0},{32,48},{48,32},{64,80},{80,64},{96,112},{112,96},{1... | collective-permute-start | bytes 79880 | tf_op jit(solution)/shard_map/ppermute | solution.py:54
  10.5 7.5 %collective-permute-start = (bf16[8,1664]{1,0:T(8,128)(2,1)S(1)}, bf16[8,1664]{1,0:T(8,128)(2,1)S(1)}, u32[]{:S(2)}, u32[]{:S(2)}) collective-permute-start(bf16[8,1664]{1,0:T(8,128)(2,1)S(1)} %get-tuple-element.44), channel_id=1, source_target_pairs={{0,128},{16,144},{32,160},{48,176},{64,192},{80,208},{96,224},{112... | collective-permute-start | bytes 79880 | tf_op jit(solution)/shard_map/ppermute | solution.py:54
  15.7 14.1 %copy-start.6 = (bf16[2,1536,336]{1,2,0:T(8,128)(2,1)S(1)}, bf16[2,1536,336]{1,2,0:T(8,128)(2,1)}, u32[]{:S(2)}) copy-start(bf16[2,1536,336]{1,2,0:T(8,128)(2,1)} %param.19) | copy-start | bytes 6193156
  15.8 8.1 %collective-permute-start.4 = (bf16[16,1664]{1,0:T(8,128)(2,1)S(1)}, bf16[16,1664]{1,0:T(8,128)(2,1)S(1)}, u32[]{:S(2)}, u32[]{:S(2)}) collective-permute-start(bf16[16,1664]{1,0:T(8,128)(2,1)S(1)} %constant_dynamic-update-slice_fusion), channel_id=1, source_target_pairs={{0,160},{16,112},{32,192},{48,144},{64,224},{80,176},{96,0},{112,2... | collective-permute-start | bytes 159752 | tf_op jit(solution)/shard_map/ppermute | solution.py:54
  17.5 6.3 %collective-permute-start.3 = (bf16[16,1664]{1,0:T(8,128)(2,1)S(1)}, bf16[16,1664]{1,0:T(8,128)(2,1)S(1)}, u32[]{:S(2)}, u32[]{:S(2)}) collective-permute-start(bf16[16,1664]{1,0:T(8,128)(2,1)S(1)} %constant_dynamic-update-slice_fusion), channel_id=1, source_target_pairs={{0,192},{16,80},{32,224},{48,112},{64,0},{80,144},{96,32},{112,176... | collective-permute-start | bytes 159752 | tf_op jit(solution)/shard_map/ppermute | solution.py:54
  17.5 6.3 %collective-permute-start.2 = (bf16[16,1664]{1,0:T(8,128)(2,1)S(1)}, bf16[16,1664]{1,0:T(8,128)(2,1)S(1)}, u32[]{:S(2)}, u32[]{:S(2)}) collective-permute-start(bf16[16,1664]{1,0:T(8,128)(2,1)S(1)} %constant_dynamic-update-slice_fusion), channel_id=1, source_target_pairs={{0,224},{16,48},{32,0},{48,80},{64,32},{80,112},{96,64},{112,144},... | collective-permute-start | bytes 159752 | tf_op jit(solution)/shard_map/ppermute | solution.py:54
  23.9 7.3 %collective-permute-start.7 = (bf16[64,1664]{1,0:T(8,128)(2,1)S(1)}, bf16[64,1664]{1,0:T(8,128)(2,1)S(1)}, u32[]{:S(2)}, u32[]{:S(2)}) collective-permute-start(bf16[64,1664]{1,0:T(8,128)(2,1)S(1)} %constant_dynamic-update-slice_fusion.2.refs_0_), channel_id=1, source_target_pairs={{0,8},{4,12},{8,0},{12,4},{16,24},{20,28},{24,16},{28,20},{32,40},... | collective-permute-start | bytes 638984 | tf_op jit(solution)/shard_map/ppermute | solution.py:54
  26.7 9.1 %collective-permute-start.6 = (bf16[64,1664]{1,0:T(8,128)(2,1)S(1)}, bf16[64,1664]{1,0:T(8,128)(2,1)S(1)}, u32[]{:S(2)}, u32[]{:S(2)}) collective-permute-start(bf16[64,1664]{1,0:T(8,128)(2,1)S(1)} %constant_dynamic-update-slice_fusion.2.refs_0_), channel_id=1, source_target_pairs={{0,12},{4,8},{8,4},{12,0},{16,20},{20,16},{24,28},{28,24},{32,44},... | collective-permute-start | bytes 638984 | tf_op jit(solution)/shard_map/ppermute | solution.py:54
  27.0 9.6 %collective-permute-start.5 = (bf16[64,1664]{1,0:T(8,128)(2,1)S(1)}, bf16[64,1664]{1,0:T(8,128)(2,1)S(1)}, u32[]{:S(2)}, u32[]{:S(2)}) collective-permute-start(bf16[64,1664]{1,0:T(8,128)(2,1)S(1)} %constant_dynamic-update-slice_fusion.2.refs_0_), channel_id=1, source_target_pairs={{0,4},{4,0},{8,12},{12,8},{16,28},{20,24},{24,20},{28,16},{32,36},... | collective-permute-start | bytes 638984 | tf_op jit(solution)/shard_map/ppermute | solution.py:54
  36.8 3.8 %collective-permute-start.8 = (bf16[256,1664]{1,0:T(8,128)(2,1)S(1)}, bf16[256,1664]{1,0:T(8,128)(2,1)S(1)}, u32[]{:S(2)}, u32[]{:S(2)}) collective-permute-start(bf16[256,1664]{1,0:T(8,128)(2,1)S(1)} %get-tuple-element.51), channel_id=1, source_target_pairs={{0,16},{16,0},{32,48},{48,32},{64,80},{80,64},{96,112},{112,96},{1... | collective-permute-start | bytes 2555912 | tf_op jit(solution)/shard_map/ppermute | solution.py:54
  38.1 2.6 %copy-start.7 = (bf16[2,1536,336]{1,2,0:T(8,128)(2,1)S(1)}, bf16[2,1536,336]{1,2,0:T(8,128)(2,1)}, u32[]{:S(2)}) copy-start(bf16[2,1536,336]{1,2,0:T(8,128)(2,1)} %param.19) | copy-start | bytes 6193156
  40.6 8.5 %copy-start.8 = (bf16[2,1536,336]{1,2,0:T(8,128)(2,1)S(1)}, bf16[2,1536,336]{1,2,0:T(8,128)(2,1)}, u32[]{:S(2)}) copy-start(bf16[2,1536,336]{1,2,0:T(8,128)(2,1)} %param.20) | copy-start | bytes 6193156
  44.1 9.1 %collective-permute-start.9 = (bf16[176,384]{1,0:T(8,128)(2,1)S(1)}, bf16[176,384]{1,0:T(8,128)(2,1)S(1)}, u32[]{:S(2)}, u32[]{:S(2)}) collective-permute-start(bf16[176,384]{1,0:T(8,128)(2,1)S(1)} %get-tuple-element.62), channel_id=1, source_target_pairs={{0,1},{1,2},{2,3},{3,0},{4,5},{5,6},{6,7},{7,4},{8,9},{9,10},{10,1... | collective-permute-start | bytes 405512 | tf_op jit(solution)/shard_map/ppermute | solution.py:54
  45.4 9.5 %collective-permute-start.10 = (bf16[176,384]{1,0:T(8,128)(2,1)S(1)}, bf16[176,384]{1,0:T(8,128)(2,1)S(1)}, u32[]{:S(2)}, u32[]{:S(2)}) collective-permute-start(bf16[176,384]{1,0:T(8,128)(2,1)S(1)} %get-tuple-element.63), channel_id=1, source_target_pairs={{0,2},{1,3},{2,0},{3,1},{4,6},{5,7},{6,4},{7,5},{8,10},{9,11},{10,... | collective-permute-start | bytes 405512 | tf_op jit(solution)/shard_map/ppermute | solution.py:54
  48.0 6.9 %collective-permute-start.11 = (bf16[176,384]{1,0:T(8,128)(2,1)S(1)}, bf16[176,384]{1,0:T(8,128)(2,1)S(1)}, u32[]{:S(2)}, u32[]{:S(2)}) collective-permute-start(bf16[176,384]{1,0:T(8,128)(2,1)S(1)} %get-tuple-element.64), channel_id=1, source_target_pairs={{0,3},{1,0},{2,1},{3,2},{4,7},{5,4},{6,5},{7,6},{8,11},{9,8},{10,9... | collective-permute-start | bytes 405512 | tf_op jit(solution)/shard_map/ppermute | solution.py:54
  50.6 22.4 %copy-start.5 = (bf16[2,336,1536]{2,1,0:T(8,128)(2,1)S(1)}, bf16[2,336,1536]{2,1,0:T(8,128)(2,1)}, u32[]{:S(2)}) copy-start(bf16[2,336,1536]{2,1,0:T(8,128)(2,1)} %param.21) | copy-start | bytes 6193156
  52.0 5.5 %collective-permute-start.12 = (bf16[176,384]{1,0:T(8,128)(2,1)S(1)}, bf16[176,384]{1,0:T(8,128)(2,1)S(1)}, u32[]{:S(2)}, u32[]{:S(2)}) collective-permute-start(bf16[176,384]{1,0:T(8,128)(2,1)S(1)} %get-tuple-element.69), channel_id=1, source_target_pairs={{0,1},{1,2},{2,3},{3,0},{4,5},{5,6},{6,7},{7,4},{8,9},{9,10},{10,1... | collective-permute-start | bytes 405512 | tf_op jit(solution)/shard_map/ppermute | solution.py:54
  52.4 8.0 %collective-permute-start.13 = (bf16[176,384]{1,0:T(8,128)(2,1)S(1)}, bf16[176,384]{1,0:T(8,128)(2,1)S(1)}, u32[]{:S(2)}, u32[]{:S(2)}) collective-permute-start(bf16[176,384]{1,0:T(8,128)(2,1)S(1)} %get-tuple-element.70), channel_id=1, source_target_pairs={{0,2},{1,3},{2,0},{3,1},{4,6},{5,7},{6,4},{7,5},{8,10},{9,11},{10,... | collective-permute-start | bytes 405512 | tf_op jit(solution)/shard_map/ppermute | solution.py:54
  53.2 7.7 %collective-permute-start.14 = (bf16[176,384]{1,0:T(8,128)(2,1)S(1)}, bf16[176,384]{1,0:T(8,128)(2,1)S(1)}, u32[]{:S(2)}, u32[]{:S(2)}) collective-permute-start(bf16[176,384]{1,0:T(8,128)(2,1)S(1)} %get-tuple-element.71), channel_id=1, source_target_pairs={{0,3},{1,0},{2,1},{3,2},{4,7},{5,4},{6,5},{7,6},{8,11},{9,8},{10,9... | collective-permute-start | bytes 405512 | tf_op jit(solution)/shard_map/ppermute | solution.py:54
  61.3 6.0 %collective-permute-start.17 = (bf16[168,384]{1,0:T(8,128)(2,1)S(1)}, bf16[168,384]{1,0:T(8,128)(2,1)S(1)}, u32[]{:S(2)}, u32[]{:S(2)}) collective-permute-start(bf16[168,384]{1,0:T(8,128)(2,1)S(1)} %shard_map.128.hidden0), channel_id=1, source_target_pairs={{0,1},{1,2},{2,3},{3,0},{4,5},{5,6},{6,7},{7,4},{8,9},{9,10},{10,1... | collective-permute-start | bytes 387080 | tf_op jit(solution)/shard_map/ppermute | solution.py:54
  62.3 9.6 %collective-permute-start.16 = (bf16[168,384]{1,0:T(8,128)(2,1)S(1)}, bf16[168,384]{1,0:T(8,128)(2,1)S(1)}, u32[]{:S(2)}, u32[]{:S(2)}) collective-permute-start(bf16[168,384]{1,0:T(8,128)(2,1)S(1)} %shard_map.128.hidden0), channel_id=1, source_target_pairs={{0,2},{1,3},{2,0},{3,1},{4,6},{5,7},{6,4},{7,5},{8,10},{9,11},{10,... | collective-permute-start | bytes 387080 | tf_op jit(solution)/shard_map/ppermute | solution.py:54
  66.2 5.7 %collective-permute-start.15 = (bf16[168,384]{1,0:T(8,128)(2,1)S(1)}, bf16[168,384]{1,0:T(8,128)(2,1)S(1)}, u32[]{:S(2)}, u32[]{:S(2)}) collective-permute-start(bf16[168,384]{1,0:T(8,128)(2,1)S(1)} %shard_map.128.hidden0), channel_id=1, source_target_pairs={{0,3},{1,0},{2,1},{3,2},{4,7},{5,4},{6,5},{7,6},{8,11},{9,8},{10,9... | collective-permute-start | bytes 387080 | tf_op jit(solution)/shard_map/ppermute | solution.py:54
  73.6 2.6 %collective-permute-start.18 = (bf16[64,1536]{1,0:T(8,128)(2,1)S(1)}, bf16[64,1536]{1,0:T(8,128)(2,1)S(1)}, u32[]{:S(2)}, u32[]{:S(2)}) collective-permute-start(bf16[64,1536]{1,0:T(8,128)(2,1)S(1)} %convolution_convert_fusion.1), channel_id=1, source_target_pairs={{0,16},{16,0},{32,48},{48,32},{64,80},{80,64},{96,112},{112,96},{1... | collective-permute-start | bytes 589832 | tf_op jit(solution)/shard_map/ppermute | solution.py:54
  76.9 3.7 %collective-permute-start.19 = (bf16[192,1536]{1,0:T(8,128)(2,1)S(1)}, bf16[192,1536]{1,0:T(8,128)(2,1)S(1)}, u32[]{:S(2)}, u32[]{:S(2)}) collective-permute-start(bf16[192,1536]{1,0:T(8,128)(2,1)S(1)} %convolution_convert_fusion), channel_id=1, source_target_pairs={{0,16},{16,0},{32,48},{48,32},{64,80},{80,64},{96,112},{112,96},{1... | collective-permute-start | bytes 1769480 | tf_op jit(solution)/shard_map/ppermute | solution.py:54
  77.3 7.9 %collective-permute-start.22 = (bf16[64,1536]{1,0:T(8,128)(2,1)S(1)}, bf16[64,1536]{1,0:T(8,128)(2,1)S(1)}, u32[]{:S(2)}, u32[]{:S(2)}) collective-permute-start(bf16[64,1536]{1,0:T(8,128)(2,1)S(1)} %add_convert_fusion), channel_id=1, source_target_pairs={{0,8},{4,12},{8,0},{12,4},{16,24},{20,28},{24,16},{28,20},{32,40},... | collective-permute-start | bytes 589832 | tf_op jit(solution)/shard_map/ppermute | solution.py:54
  80.9 8.4 %collective-permute-start.20 = (bf16[64,1536]{1,0:T(8,128)(2,1)S(1)}, bf16[64,1536]{1,0:T(8,128)(2,1)S(1)}, u32[]{:S(2)}, u32[]{:S(2)}) collective-permute-start(bf16[64,1536]{1,0:T(8,128)(2,1)S(1)} %get-tuple-element.76), channel_id=1, source_target_pairs={{0,4},{4,0},{8,12},{12,8},{16,28},{20,24},{24,20},{28,16},{32,36},... | collective-permute-start | bytes 589832 | tf_op jit(solution)/shard_map/ppermute | solution.py:54
  81.9 7.5 %collective-permute-start.21 = (bf16[64,1536]{1,0:T(8,128)(2,1)S(1)}, bf16[64,1536]{1,0:T(8,128)(2,1)S(1)}, u32[]{:S(2)}, u32[]{:S(2)}) collective-permute-start(bf16[64,1536]{1,0:T(8,128)(2,1)S(1)} %get-tuple-element.77), channel_id=1, source_target_pairs={{0,12},{4,8},{8,4},{12,0},{16,20},{20,16},{24,28},{28,24},{32,44},... | collective-permute-start | bytes 589832 | tf_op jit(solution)/shard_map/ppermute | solution.py:54
  89.6 7.1 %collective-permute-start.24 = (bf16[16,1536]{1,0:T(8,128)(2,1)S(1)}, bf16[16,1536]{1,0:T(8,128)(2,1)S(1)}, u32[]{:S(2)}, u32[]{:S(2)}) collective-permute-start(bf16[16,1536]{1,0:T(8,128)(2,1)S(1)} %get-tuple-element.81), channel_id=1, source_target_pairs={{0,32},{16,240},{32,64},{48,16},{64,96},{80,48},{96,128},{112,80},... | collective-permute-start | bytes 147464 | tf_op jit(solution)/shard_map/ppermute | solution.py:54
  90.8 5.9 %collective-permute-start.25 = (bf16[16,1536]{1,0:T(8,128)(2,1)S(1)}, bf16[16,1536]{1,0:T(8,128)(2,1)S(1)}, u32[]{:S(2)}, u32[]{:S(2)}) collective-permute-start(bf16[16,1536]{1,0:T(8,128)(2,1)S(1)} %get-tuple-element.82), channel_id=1, source_target_pairs={{0,64},{16,208},{32,96},{48,240},{64,128},{80,16},{96,160},{112,48... | collective-permute-start | bytes 147464 | tf_op jit(solution)/shard_map/ppermute | solution.py:54
  91.9 5.5 %collective-permute-start.26 = (bf16[16,1536]{1,0:T(8,128)(2,1)S(1)}, bf16[16,1536]{1,0:T(8,128)(2,1)S(1)}, u32[]{:S(2)}, u32[]{:S(2)}) collective-permute-start(bf16[16,1536]{1,0:T(8,128)(2,1)S(1)} %get-tuple-element.83), channel_id=1, source_target_pairs={{0,96},{16,176},{32,128},{48,208},{64,160},{80,240},{96,192},{112,... | collective-permute-start | bytes 147464 | tf_op jit(solution)/shard_map/ppermute | solution.py:54
  94.1 6.6 %collective-permute-start.23 = (bf16[8,1536]{1,0:T(8,128)(2,1)S(1)}, bf16[8,1536]{1,0:T(8,128)(2,1)S(1)}, u32[]{:S(2)}, u32[]{:S(2)}) collective-permute-start(bf16[8,1536]{1,0:T(8,128)(2,1)S(1)} %slice.69), channel_id=1, source_target_pairs={{0,128},{16,144},{32,160},{48,176},{64,192},{80,208},{96,224},{112... | collective-permute-start | bytes 73736 | tf_op jit(solution)/shard_map/ppermute | solution.py:54
  97.5 3.2 %collective-permute-start.27 = (bf16[8,1536]{1,0:T(8,128)(2,1)S(1)}, bf16[8,1536]{1,0:T(8,128)(2,1)S(1)}, u32[]{:S(2)}, u32[]{:S(2)}) collective-permute-start(bf16[8,1536]{1,0:T(8,128)(2,1)S(1)} %slice.89), channel_id=1, source_target_pairs={{0,16},{16,0},{32,48},{48,32},{64,80},{80,64},{96,112},{112,96},{1... | collective-permute-start | bytes 73736 | tf_op jit(solution)/shard_map/ppermute | solution.py:54

commit v6 on v5

--- a/solution.py
+++ b/solution.py
@@ -138,8 +138,13 @@
     placed = jnp.where(named, counts - 1.0, -1.0)
     column = lax.broadcasted_iota(jnp.int32, (rows, extra), 1)
     slot = lax.broadcasted_iota(jnp.int32, (rows, slots), 1).astype(f32)
-    ranks[...] = jnp.transpose(placed)
-    turned = jnp.transpose(notes)[: 2 * EXPERTS].astype(bf16)
+    turned = jnp.transpose(notes)[: 2 * EXPERTS]
+    listing = turned > 0.0
+    counts = lax.dot_general(
+        jnp.where(listing, 1.0, 0.0).astype(bf16), before.astype(bf16), NT, preferred_element_type=f32
+    )
+    ranks[...] = jnp.where(listing, counts - 1.0, -1.0)
+    turned = turned.astype(bf16)
     line = lax.broadcasted_iota(jnp.int32, (2 * EXPERTS, slots), 0)
     for e in range(experts):
         rank = jnp.sum(jnp.where(column == first + e, placed, 0.0), axis=1, keepdims=True)
@@ -156,7 +161,7 @@
 
 
 def list_rows(place, own, other, experts, parts):
-    rows, extra = 2 * own.shape[0], own.shape[1]
+    rows = 2 * own.shape[0]
     slots = rows * CAPACITY_OF_512 // 512
     whole = pl.BlockSpec(memory_space=VMEM)
     return pl.pallas_call(
@@ -165,7 +170,7 @@
             jax.ShapeDtypeStruct((experts, rows, slots), bf16),
             jax.ShapeDtypeStruct((parts, EXPERTS, slots), f32),
             jax.ShapeDtypeStruct((EXPERTS, slots), f32),
-            jax.ShapeDtypeStruct((extra, rows), f32),
+            jax.ShapeDtypeStruct((2 * EXPERTS, rows), f32),
         ],
         in_specs=[pl.BlockSpec(memory_space=SMEM)] + [whole] * 2,
         out_specs=[whole] * 4,

time: 103 us -> 103 us (level)
  no operation moved by 1% of the time
where the time goes in v6:
time: 103 us; the launch traced here: 101 us
  starting transfers between devices  43.6 us (42%)
  waiting for transfers between devices  32.8 us (32%)
  matrix products  13.5 us (13%)
  Pallas kernels  7.05 us (7%)
  local copies, waits for them, and re-layouts  2.12 us (2%)
  other arithmetic  1.24 us (1%)
    ppermute x28, starting transfers between devices, send(): return lax.ppermute(x, axes, pairs)  43.6 us
    ppermute x28, waiting for transfers between devices, send(): return lax.ppermute(x, axes, pairs)  32.8 us
    dot_general x4, matrix products, project(): jnp.einsum('edf,rd->efr', weight, tokens, preferred_element_type=f32)  4.65 us
    dot_general x2, matrix products, per_device(): jnp.einsum('edf,d->ef', w.astype(f32), gain).reshape(y_size, -1)  2.96 us
    pallas_call x2, Pallas kernels, pack(): pl.pallas_call(pack_kernel, out_shape=[jax.ShapeDtypeStruct((experts * fa...  2.68 us
    dot_general x4, matrix products, output(): return jnp.einsum('fr,fd->rd', part, down, preferred_element_type=f32)  2.46 us
  transfers between devices with their start and end apart: 28, of which 15 were waited for; matrix products, arithmetic and copies ran while one was open for 9% of the time, Pallas kernels for 1%

profile of v6, /device:TPU:1, one launch (start us, length us, event | category | flops | bytes accessed | tf_op | source)
XLA Modules:
  0.0 101.3 jit_solution(5018412937617659604)
XLA Ops:
  0.7 1.6 %copy-done = bf16[8,512,256]{2,1,0:T(8,128)(2,1)S(1)} copy-done((bf16[8,512,256]{2,1,0:T(8,128)(2,1)S(1)}, bf16[8,512,256]{2,1,0:T(8,128)(2,1)}, u32[]{:S(2)}) %copy-start) | copy-done | bytes 2097176
  2.2 1.4 %fusion.16 = f32[8,2,6,512]{3,2,1,0:T(8,128)S(1)} fusion(s32[8]{0:T(128)} %param.14, bf16[8,2,6,128]{3,0,2,1:T(8,128)(2,1)} %bitcast.81, bf16[8,512,256]{2,1,0:T(8,128)(2,1)S(1)} %copy-done), kind=kOutput, calls=%fused_computation.21 | convolution fusion | flops 12730368 | bytes 2318368 | tf_op jit(solution)/shard_map/rhgd,rlhd->rhgl/dot_general | solution.py:26
  3.9 2.0 %fusion.1 = f32[8,2,6,128]{3,2,1,0:T(8,128)S(1)} fusion(f32[8,2,6]{2,1,0:T(2,128)S(1)} %fusion.38, f32[8,2,6,512]{3,2,1,0:T(8,128)S(1)} %fusion.16, bf16[8,512,256]{2,1,0:T(8,128)(2,1)} %param.13), kind=kOutput, calls=%fused_computation.3 | convolution fusion | flops 12730975 | bytes 2343296 | tf_op jit(solution)/shard_map/rhgl,rlhd->rhgd/dot_general | solution.py:36
  6.0 1.3 %shard_map.122 = (bf16[8,1536]{1,0:T(8,128)(2,1)}, bf16[8,1664]{1,0:T(8,128)(2,1)S(1)}) custom-call(s32[2]{0:T(128)S(1)} %pad_add_fusion.place, f32[8,1536]{1,0:T(8,128)S(1)} %reshape.142.attended, bf16[8,1536]{1,0:T(8,128)(2,1)S(1)} %copy-done.1, bf16[6144]{0:T(1024)(128)(2,1)S(1)} %copy-done.2, s32[4,8]{1,0:T(4,128)S(1)} %bitcast.73, f32[4,8]{1,0:T(4,128)S(1)} %bitcast.74), custom_call_target="tpu_custom_call" | custom-call | flops 65536 | bytes 65536 | tf_op jit(solution)/shard_map/pallas_call | solution.py:108
  7.3 3.2 %collective-permute-start.1 = (bf16[8,1664]{1,0:T(8,128)(2,1)S(1)}, bf16[8,1664]{1,0:T(8,128)(2,1)S(1)}, u32[]{:S(2)}, u32[]{:S(2)}) collective-permute-start(bf16[8,1664]{1,0:T(8,128)(2,1)S(1)} %get-tuple-element.44), channel_id=1, source_target_pairs={{0,16},{16,0},{32,48},{48,32},{64,80},{80,64},{96,112},{112,96},{1... | collective-permute-start | bytes 79880 | tf_op jit(solution)/shard_map/ppermute | solution.py:54
  10.5 5.2 %collective-permute-start = (bf16[8,1664]{1,0:T(8,128)(2,1)S(1)}, bf16[8,1664]{1,0:T(8,128)(2,1)S(1)}, u32[]{:S(2)}, u32[]{:S(2)}) collective-permute-start(bf16[8,1664]{1,0:T(8,128)(2,1)S(1)} %get-tuple-element.44), channel_id=1, source_target_pairs={{0,128},{16,144},{32,160},{48,176},{64,192},{80,208},{96,224},{112... | collective-permute-start | bytes 79880 | tf_op jit(solution)/shard_map/ppermute | solution.py:54
  15.8 1.7 %collective-permute-start.4 = (bf16[16,1664]{1,0:T(8,128)(2,1)S(1)}, bf16[16,1664]{1,0:T(8,128)(2,1)S(1)}, u32[]{:S(2)}, u32[]{:S(2)}) collective-permute-start(bf16[16,1664]{1,0:T(8,128)(2,1)S(1)} %constant_dynamic-update-slice_fusion), channel_id=1, source_target_pairs={{0,160},{16,112},{32,192},{48,144},{64,224},{80,176},{96,0},{112,2... | collective-permute-start | bytes 159752 | tf_op jit(solution)/shard_map/ppermute | solution.py:54
  18.1 5.8 %collective-permute-done.2 = bf16[16,1664]{1,0:T(8,128)(2,1)S(1)} collective-permute-done((bf16[16,1664]{1,0:T(8,128)(2,1)S(1)}, bf16[16,1664]{1,0:T(8,128)(2,1)S(1)}, u32[]{:S(2)}, u32[]{:S(2)}) %collective-permute-start.2) | collective-permute-done | bytes 53280 | tf_op jit(solution)/shard_map/ppermute | solution.py:54
  23.9 2.8 %collective-permute-start.7 = (bf16[64,1664]{1,0:T(8,128)(2,1)S(1)}, bf16[64,1664]{1,0:T(8,128)(2,1)S(1)}, u32[]{:S(2)}, u32[]{:S(2)}) collective-permute-start(bf16[64,1664]{1,0:T(8,128)(2,1)S(1)} %constant_dynamic-update-slice_fusion.2.refs_0_), channel_id=1, source_target_pairs={{0,8},{4,12},{8,0},{12,4},{16,24},{20,28},{24,16},{28,20},{32,40},... | collective-permute-start | bytes 638984 | tf_op jit(solution)/shard_map/ppermute | solution.py:54
  27.6 2.2 %fusion.40 = f32[1,2,336]{2,0,1:T(1,128)S(1)} fusion(bf16[1536,1,1]{0,1,2:T(2,128)(2,1)S(1)} %reshape.146, bf16[2,1536,336]{1,2,0:T(8,128)(2,1)} %param.20), kind=kOutput, calls=%fused_computation.67 | convolution fusion | flops 2064384 | bytes 2070144 | tf_op jit(solution)/shard_map/edf,d->ef/dot_general | solution.py:341
  29.9 0.7 fusion.39
  31.2 4.7 %collective-permute-done.6.refs_2_ = bf16[64,1664]{1,0:T(8,128)(2,1)S(1)} collective-permute-done((bf16[64,1664]{1,0:T(8,128)(2,1)S(1)}, bf16[64,1664]{1,0:T(8,128)(2,1)S(1)}, u32[]{:S(2)}, u32[]{:S(2)}) %collective-permute-start.6) | collective-permute-done | bytes 213024 | tf_op jit(solution)/shard_map/ppermute | solution.py:54
  35.9 0.8 collective-permute-done.5.refs_1_
  36.8 1.3 %collective-permute-start.8 = (bf16[256,1664]{1,0:T(8,128)(2,1)S(1)}, bf16[256,1664]{1,0:T(8,128)(2,1)S(1)}, u32[]{:S(2)}, u32[]{:S(2)}) collective-permute-start(bf16[256,1664]{1,0:T(8,128)(2,1)S(1)} %get-tuple-element.51), channel_id=1, source_target_pairs={{0,16},{16,0},{32,48},{48,32},{64,80},{80,64},{96,112},{112,96},{1... | collective-permute-start | bytes 2555912 | tf_op jit(solution)/shard_map/ppermute | solution.py:54
  38.1 2.5 %fusion.8.own = bf16[2,336,256]{2,1,0:T(8,128)(2,1)S(1)} fusion(bf16[2,1536,336]{1,2,0:T(8,128)(2,1)} %param.19, bf16[256,1536]{1,0:T(8,128)(2,1)S(1)} %get-tuple-element.65), kind=kOutput, calls=%fused_computation.14 | convolution fusion | flops 528654336 | bytes 3194880 | tf_op jit(solution)/shard_map/edf,rd->efr/dot_general | solution.py:334
  40.6 0.7 fusion.9.other
  41.4 1.4 %shard_map.125 = (bf16[2,512,384]{2,1,0:T(8,128)(2,1)S(1)}, f32[4,8,384]{2,1,0:T(8,128)S(1)}, f32[8,384]{1,0:T(8,128)S(1)}, f32[16,512]{1,0:T(8,128)S(1)}) custom-call(s32[2]{0:T(128)S(1)} %pad_add_fusion.place, bf16[256,128]{1,0:T(8,128)(2,1)S(1)} %get-tuple-element.53.own, bf16[256,128]{1,0:T(8,128)(2,1)S(1)} %get-tuple-element.54.other), custom_call_target="tpu_custom_call" | custom-call | flops 134217728 | bytes 1048576 | tf_op jit(solution)/shard_map/pallas_call | solution.py:167
  42.7 1.3 %shard_map.126 = (bf16[176,384]{1,0:T(8,128)(2,1)S(1)}, bf16[176,384]{1,0:T(8,128)(2,1)S(1)}, bf16[176,384]{1,0:T(8,128)(2,1)S(1)}, bf16[176,384]{1,0:T(8,128)(2,1)S(1)}) custom-call(s32[2]{0:T(128)S(1)} %pad_add_fusion.place, bf16[2,336,256]{2,1,0:T(8,128)(2,1)S(1)} %fusion.8.own, bf16[2,336,256]{2,1,0:T(8,128)(2,1)S(1)} %fusion.9.other, ...), custom_call_target="tpu_custom_call" | custom-call | flops 268435456 | bytes 2097152 | tf_op jit(solution)/shard_map/pallas_call | solution.py:204
  44.1 1.4 %collective-permute-start.9 = (bf16[176,384]{1,0:T(8,128)(2,1)S(1)}, bf16[176,384]{1,0:T(8,128)(2,1)S(1)}, u32[]{:S(2)}, u32[]{:S(2)}) collective-permute-start(bf16[176,384]{1,0:T(8,128)(2,1)S(1)} %get-tuple-element.62), channel_id=1, source_target_pairs={{0,1},{1,2},{2,3},{3,0},{4,5},{5,6},{6,7},{7,4},{8,9},{9,10},{10,1... | collective-permute-start | bytes 405512 | tf_op jit(solution)/shard_map/ppermute | solution.py:54
  45.5 2.6 %collective-permute-start.10 = (bf16[176,384]{1,0:T(8,128)(2,1)S(1)}, bf16[176,384]{1,0:T(8,128)(2,1)S(1)}, u32[]{:S(2)}, u32[]{:S(2)}) collective-permute-start(bf16[176,384]{1,0:T(8,128)(2,1)S(1)} %get-tuple-element.63), channel_id=1, source_target_pairs={{0,2},{1,3},{2,0},{3,1},{4,6},{5,7},{6,4},{7,5},{8,10},{9,11},{10,... | collective-permute-start | bytes 405512 | tf_op jit(solution)/shard_map/ppermute | solution.py:54
  48.1 1.1 %collective-permute-start.11 = (bf16[176,384]{1,0:T(8,128)(2,1)S(1)}, bf16[176,384]{1,0:T(8,128)(2,1)S(1)}, u32[]{:S(2)}, u32[]{:S(2)}) collective-permute-start(bf16[176,384]{1,0:T(8,128)(2,1)S(1)} %get-tuple-element.64), channel_id=1, source_target_pairs={{0,3},{1,0},{2,1},{3,2},{4,7},{5,4},{6,5},{7,6},{8,11},{9,8},{10,9... | collective-permute-start | bytes 405512 | tf_op jit(solution)/shard_map/ppermute | solution.py:54
  49.1 0.7 fusion.10.own
  49.9 0.7 fusion.11.other
  50.6 1.3 %shard_map.127 = (bf16[176,384]{1,0:T(8,128)(2,1)S(1)}, bf16[176,384]{1,0:T(8,128)(2,1)S(1)}, bf16[176,384]{1,0:T(8,128)(2,1)S(1)}, bf16[176,384]{1,0:T(8,128)(2,1)S(1)}) custom-call(s32[2]{0:T(128)S(1)} %pad_add_fusion.place, bf16[2,336,256]{2,1,0:T(8,128)(2,1)S(1)} %fusion.10.own, bf16[2,336,256]{2,1,0:T(8,128)(2,1)S(1)} %fusion.11.other, ...), custom_call_target="tpu_custom_call" | custom-call | flops 268435456 | bytes 2097152 | tf_op jit(solution)/shard_map/pallas_call | solution.py:204
  52.4 0.8 collective-permute-start.13
  53.2 1.7 %collective-permute-start.14 = (bf16[176,384]{1,0:T(8,128)(2,1)S(1)}, bf16[176,384]{1,0:T(8,128)(2,1)S(1)}, u32[]{:S(2)}, u32[]{:S(2)}) collective-permute-start(bf16[176,384]{1,0:T(8,128)(2,1)S(1)} %get-tuple-element.71), channel_id=1, source_target_pairs={{0,3},{1,0},{2,1},{3,2},{4,7},{5,4},{6,5},{7,6},{8,11},{9,8},{10,9... | collective-permute-start | bytes 405512 | tf_op jit(solution)/shard_map/ppermute | solution.py:54
  54.9 2.6 %collective-permute-done.12.refs_5_ = bf16[176,384]{1,0:T(8,128)(2,1)S(1)} collective-permute-done((bf16[176,384]{1,0:T(8,128)(2,1)S(1)}, bf16[176,384]{1,0:T(8,128)(2,1)S(1)}, u32[]{:S(2)}, u32[]{:S(2)}) %collective-permute-start.12) | collective-permute-done | bytes 135200 | tf_op jit(solution)/shard_map/ppermute | solution.py:54
  57.5 3.0 %collective-permute-done.13.refs_6_ = bf16[176,384]{1,0:T(8,128)(2,1)S(1)} collective-permute-done((bf16[176,384]{1,0:T(8,128)(2,1)S(1)}, bf16[176,384]{1,0:T(8,128)(2,1)S(1)}, u32[]{:S(2)}, u32[]{:S(2)}) %collective-permute-start.13) | collective-permute-done | bytes 135200 | tf_op jit(solution)/shard_map/ppermute | solution.py:54
  61.4 0.9 collective-permute-start.17
  62.3 3.9 %collective-permute-start.16 = (bf16[168,384]{1,0:T(8,128)(2,1)S(1)}, bf16[168,384]{1,0:T(8,128)(2,1)S(1)}, u32[]{:S(2)}, u32[]{:S(2)}) collective-permute-start(bf16[168,384]{1,0:T(8,128)(2,1)S(1)} %shard_map.128.hidden0), channel_id=1, source_target_pairs={{0,2},{1,3},{2,0},{3,1},{4,6},{5,7},{6,4},{7,5},{8,10},{9,11},{10,... | collective-permute-start | bytes 387080 | tf_op jit(solution)/shard_map/ppermute | solution.py:54
  66.2 1.1 %collective-permute-done.17.hidden3 = bf16[168,384]{1,0:T(8,128)(2,1)S(1)} collective-permute-done((bf16[168,384]{1,0:T(8,128)(2,1)S(1)}, bf16[168,384]{1,0:T(8,128)(2,1)S(1)}, u32[]{:S(2)}, u32[]{:S(2)}) %collective-permute-start.17) | collective-permute-done | bytes 129056 | tf_op jit(solution)/shard_map/ppermute | solution.py:54
  67.3 4.6 %collective-permute-done.16.hidden2 = bf16[168,384]{1,0:T(8,128)(2,1)S(1)} collective-permute-done((bf16[168,384]{1,0:T(8,128)(2,1)S(1)}, bf16[168,384]{1,0:T(8,128)(2,1)S(1)}, u32[]{:S(2)}, u32[]{:S(2)}) %collective-permute-start.16) | collective-permute-done | bytes 129056 | tf_op jit(solution)/shard_map/ppermute | solution.py:54
  71.9 1.1 %shard_map.129 = bf16[4,168,512]{2,1,0:T(8,128)(2,1)S(1)} custom-call(s32[2]{0:T(128)S(1)} %pad_add_fusion.place, bf16[168,384]{1,0:T(8,128)(2,1)S(1)} %shard_map.128.hidden0, bf16[168,384]{1,0:T(8,128)(2,1)S(1)} %collective-permute-done.15.hidden1, bf16[168,384]{1,0:T(8,128)(2,1)S(1)} %collective-permute-done.16.hidden2, ...), custom_call_target="tpu_custom_call" | custom-call | flops 268435456 | bytes 1048576 | tf_op jit(solution)/shard_map/pallas_call | solution.py:299
  73.6 1.5 %collective-permute-start.18 = (bf16[64,1536]{1,0:T(8,128)(2,1)S(1)}, bf16[64,1536]{1,0:T(8,128)(2,1)S(1)}, u32[]{:S(2)}, u32[]{:S(2)}) collective-permute-start(bf16[64,1536]{1,0:T(8,128)(2,1)S(1)} %convolution_convert_fusion.1), channel_id=1, source_target_pairs={{0,16},{16,0},{32,48},{48,32},{64,80},{80,64},{96,112},{112,96},{1... | collective-permute-start | bytes 589832 | tf_op jit(solution)/shard_map/ppermute | solution.py:54
  76.2 0.7 convolution_convert_fusion
  77.4 2.6 %collective-permute-start.22 = (bf16[64,1536]{1,0:T(8,128)(2,1)S(1)}, bf16[64,1536]{1,0:T(8,128)(2,1)S(1)}, u32[]{:S(2)}, u32[]{:S(2)}) collective-permute-start(bf16[64,1536]{1,0:T(8,128)(2,1)S(1)} %add_convert_fusion), channel_id=1, source_target_pairs={{0,8},{4,12},{8,0},{12,4},{16,24},{20,28},{24,16},{28,20},{32,40},... | collective-permute-start | bytes 589832 | tf_op jit(solution)/shard_map/ppermute | solution.py:54
  80.0 0.6 fusion.24
  80.9 1.0 collective-permute-start.20
  81.9 3.3 %collective-permute-done.22 = bf16[64,1536]{1,0:T(8,128)(2,1)S(1)} collective-permute-done((bf16[64,1536]{1,0:T(8,128)(2,1)S(1)}, bf16[64,1536]{1,0:T(8,128)(2,1)S(1)}, u32[]{:S(2)}, u32[]{:S(2)}) %collective-permute-start.22) | collective-permute-done | bytes 196640 | tf_op jit(solution)/shard_map/ppermute | solution.py:54
  85.2 4.1 %collective-permute-done.20 = bf16[64,1536]{1,0:T(8,128)(2,1)S(1)} collective-permute-done((bf16[64,1536]{1,0:T(8,128)(2,1)S(1)}, bf16[64,1536]{1,0:T(8,128)(2,1)S(1)}, u32[]{:S(2)}, u32[]{:S(2)}) %collective-permute-start.20) | collective-permute-done | bytes 196640 | tf_op jit(solution)/shard_map/ppermute | solution.py:54
  89.6 1.3 %collective-permute-start.24 = (bf16[16,1536]{1,0:T(8,128)(2,1)S(1)}, bf16[16,1536]{1,0:T(8,128)(2,1)S(1)}, u32[]{:S(2)}, u32[]{:S(2)}) collective-permute-start(bf16[16,1536]{1,0:T(8,128)(2,1)S(1)} %get-tuple-element.81), channel_id=1, source_target_pairs={{0,32},{16,240},{32,64},{48,16},{64,96},{80,48},{96,128},{112,80},... | collective-permute-start | bytes 147464 | tf_op jit(solution)/shard_map/ppermute | solution.py:54
  90.9 1.0 %collective-permute-start.25 = (bf16[16,1536]{1,0:T(8,128)(2,1)S(1)}, bf16[16,1536]{1,0:T(8,128)(2,1)S(1)}, u32[]{:S(2)}, u32[]{:S(2)}) collective-permute-start(bf16[16,1536]{1,0:T(8,128)(2,1)S(1)} %get-tuple-element.82), channel_id=1, source_target_pairs={{0,64},{16,208},{32,96},{48,240},{64,128},{80,16},{96,160},{112,48... | collective-permute-start | bytes 147464 | tf_op jit(solution)/shard_map/ppermute | solution.py:54
  91.9 2.1 %collective-permute-start.26 = (bf16[16,1536]{1,0:T(8,128)(2,1)S(1)}, bf16[16,1536]{1,0:T(8,128)(2,1)S(1)}, u32[]{:S(2)}, u32[]{:S(2)}) collective-permute-start(bf16[16,1536]{1,0:T(8,128)(2,1)S(1)} %get-tuple-element.83), channel_id=1, source_target_pairs={{0,96},{16,176},{32,128},{48,208},{64,160},{80,240},{96,192},{112,... | collective-permute-start | bytes 147464 | tf_op jit(solution)/shard_map/ppermute | solution.py:54
  94.0 2.7 %collective-permute-start.23 = (bf16[8,1536]{1,0:T(8,128)(2,1)S(1)}, bf16[8,1536]{1,0:T(8,128)(2,1)S(1)}, u32[]{:S(2)}, u32[]{:S(2)}) collective-permute-start(bf16[8,1536]{1,0:T(8,128)(2,1)S(1)} %slice.69), channel_id=1, source_target_pairs={{0,128},{16,144},{32,160},{48,176},{64,192},{80,208},{96,224},{112... | collective-permute-start | bytes 73736 | tf_op jit(solution)/shard_map/ppermute | solution.py:54
  96.8 0.7 collective-permute-done.26
  97.5 2.3 %collective-permute-start.27 = (bf16[8,1536]{1,0:T(8,128)(2,1)S(1)}, bf16[8,1536]{1,0:T(8,128)(2,1)S(1)}, u32[]{:S(2)}, u32[]{:S(2)}) collective-permute-start(bf16[8,1536]{1,0:T(8,128)(2,1)S(1)} %slice.89), channel_id=1, source_target_pairs={{0,16},{16,0},{32,48},{48,32},{64,80},{80,64},{96,112},{112,96},{1... | collective-permute-start | bytes 73736 | tf_op jit(solution)/shard_map/ppermute | solution.py:54
  99.8 0.8 collective-permute-done.23
  100.7 0.6 fusion.31
  (78 shorter events, 6.6 us)
Async XLA Ops:
  0.6 1.6 %copy-start = (bf16[8,512,256]{2,1,0:T(8,128)(2,1)S(1)}, bf16[8,512,256]{2,1,0:T(8,128)(2,1)}, u32[]{:S(2)}) copy-start(bf16[8,512,256]{2,1,0:T(8,128)(2,1)} %param.12) | copy-start | bytes 6291460
  3.6 2.4 %copy-start.1 = (bf16[8,1536]{1,0:T(8,128)(2,1)S(1)}, bf16[8,1536]{1,0:T(8,128)(2,1)}, u32[]{:S(2)}) copy-start(bf16[8,1536]{1,0:T(8,128)(2,1)} %residual.1) | copy-start | bytes 73732
  3.6 2.4 %copy-start.2 = (bf16[6144]{0:T(1024)(128)(2,1)S(1)}, bf16[6144]{0:T(1024)(128)(2,1)}, u32[]{:S(2)}) copy-start(bf16[6144]{0:T(1024)(128)(2,1)} %gain.1) | copy-start | bytes 36868
  3.6 2.4 %copy-start.3 = (s32[8,4]{0,1:T(4,128)S(1)}, s32[8,4]{0,1:T(4,128)}, u32[]{:S(2)}) copy-start(s32[8,4]{0,1:T(4,128)} %param.17) | copy-start | bytes 388
  3.6 2.4 %copy-start.4 = (f32[8,4]{0,1:T(4,128)S(1)}, f32[8,4]{0,1:T(4,128)}, u32[]{:S(2)}) copy-start(f32[8,4]{0,1:T(4,128)} %param.18) | copy-start | bytes 388
  7.3 8.5 %collective-permute-start.1 = (bf16[8,1664]{1,0:T(8,128)(2,1)S(1)}, bf16[8,1664]{1,0:T(8,128)(2,1)S(1)}, u32[]{:S(2)}, u32[]{:S(2)}) collective-permute-start(bf16[8,1664]{1,0:T(8,128)(2,1)S(1)} %get-tuple-element.44), channel_id=1, source_target_pairs={{0,16},{16,0},{32,48},{48,32},{64,80},{80,64},{96,112},{112,96},{1... | collective-permute-start | bytes 79880 | tf_op jit(solution)/shard_map/ppermute | solution.py:54
  10.5 7.5 %collective-permute-start = (bf16[8,1664]{1,0:T(8,128)(2,1)S(1)}, bf16[8,1664]{1,0:T(8,128)(2,1)S(1)}, u32[]{:S(2)}, u32[]{:S(2)}) collective-permute-start(bf16[8,1664]{1,0:T(8,128)(2,1)S(1)} %get-tuple-element.44), channel_id=1, source_target_pairs={{0,128},{16,144},{32,160},{48,176},{64,192},{80,208},{96,224},{112... | collective-permute-start | bytes 79880 | tf_op jit(solution)/shard_map/ppermute | solution.py:54
  15.7 14.1 %copy-start.6 = (bf16[2,1536,336]{1,2,0:T(8,128)(2,1)S(1)}, bf16[2,1536,336]{1,2,0:T(8,128)(2,1)}, u32[]{:S(2)}) copy-start(bf16[2,1536,336]{1,2,0:T(8,128)(2,1)} %param.19) | copy-start | bytes 6193156
  15.8 8.1 %collective-permute-start.4 = (bf16[16,1664]{1,0:T(8,128)(2,1)S(1)}, bf16[16,1664]{1,0:T(8,128)(2,1)S(1)}, u32[]{:S(2)}, u32[]{:S(2)}) collective-permute-start(bf16[16,1664]{1,0:T(8,128)(2,1)S(1)} %constant_dynamic-update-slice_fusion), channel_id=1, source_target_pairs={{0,160},{16,112},{32,192},{48,144},{64,224},{80,176},{96,0},{112,2... | collective-permute-start | bytes 159752 | tf_op jit(solution)/shard_map/ppermute | solution.py:54
  17.5 6.3 %collective-permute-start.3 = (bf16[16,1664]{1,0:T(8,128)(2,1)S(1)}, bf16[16,1664]{1,0:T(8,128)(2,1)S(1)}, u32[]{:S(2)}, u32[]{:S(2)}) collective-permute-start(bf16[16,1664]{1,0:T(8,128)(2,1)S(1)} %constant_dynamic-update-slice_fusion), channel_id=1, source_target_pairs={{0,192},{16,80},{32,224},{48,112},{64,0},{80,144},{96,32},{112,176... | collective-permute-start | bytes 159752 | tf_op jit(solution)/shard_map/ppermute | solution.py:54
  17.5 6.3 %collective-permute-start.2 = (bf16[16,1664]{1,0:T(8,128)(2,1)S(1)}, bf16[16,1664]{1,0:T(8,128)(2,1)S(1)}, u32[]{:S(2)}, u32[]{:S(2)}) collective-permute-start(bf16[16,1664]{1,0:T(8,128)(2,1)S(1)} %constant_dynamic-update-slice_fusion), channel_id=1, source_target_pairs={{0,224},{16,48},{32,0},{48,80},{64,32},{80,112},{96,64},{112,144},... | collective-permute-start | bytes 159752 | tf_op jit(solution)/shard_map/ppermute | solution.py:54
  23.9 7.3 %collective-permute-start.7 = (bf16[64,1664]{1,0:T(8,128)(2,1)S(1)}, bf16[64,1664]{1,0:T(8,128)(2,1)S(1)}, u32[]{:S(2)}, u32[]{:S(2)}) collective-permute-start(bf16[64,1664]{1,0:T(8,128)(2,1)S(1)} %constant_dynamic-update-slice_fusion.2.refs_0_), channel_id=1, source_target_pairs={{0,8},{4,12},{8,0},{12,4},{16,24},{20,28},{24,16},{28,20},{32,40},... | collective-permute-start | bytes 638984 | tf_op jit(solution)/shard_map/ppermute | solution.py:54
  26.7 9.1 %collective-permute-start.6 = (bf16[64,1664]{1,0:T(8,128)(2,1)S(1)}, bf16[64,1664]{1,0:T(8,128)(2,1)S(1)}, u32[]{:S(2)}, u32[]{:S(2)}) collective-permute-start(bf16[64,1664]{1,0:T(8,128)(2,1)S(1)} %constant_dynamic-update-slice_fusion.2.refs_0_), channel_id=1, source_target_pairs={{0,12},{4,8},{8,4},{12,0},{16,20},{20,16},{24,28},{28,24},{32,44},... | collective-permute-start | bytes 638984 | tf_op jit(solution)/shard_map/ppermute | solution.py:54
  27.0 9.6 %collective-permute-start.5 = (bf16[64,1664]{1,0:T(8,128)(2,1)S(1)}, bf16[64,1664]{1,0:T(8,128)(2,1)S(1)}, u32[]{:S(2)}, u32[]{:S(2)}) collective-permute-start(bf16[64,1664]{1,0:T(8,128)(2,1)S(1)} %constant_dynamic-update-slice_fusion.2.refs_0_), channel_id=1, source_target_pairs={{0,4},{4,0},{8,12},{12,8},{16,28},{20,24},{24,20},{28,16},{32,36},... | collective-permute-start | bytes 638984 | tf_op jit(solution)/shard_map/ppermute | solution.py:54
  36.8 3.8 %collective-permute-start.8 = (bf16[256,1664]{1,0:T(8,128)(2,1)S(1)}, bf16[256,1664]{1,0:T(8,128)(2,1)S(1)}, u32[]{:S(2)}, u32[]{:S(2)}) collective-permute-start(bf16[256,1664]{1,0:T(8,128)(2,1)S(1)} %get-tuple-element.51), channel_id=1, source_target_pairs={{0,16},{16,0},{32,48},{48,32},{64,80},{80,64},{96,112},{112,96},{1... | collective-permute-start | bytes 2555912 | tf_op jit(solution)/shard_map/ppermute | solution.py:54
  38.1 2.6 %copy-start.7 = (bf16[2,1536,336]{1,2,0:T(8,128)(2,1)S(1)}, bf16[2,1536,336]{1,2,0:T(8,128)(2,1)}, u32[]{:S(2)}) copy-start(bf16[2,1536,336]{1,2,0:T(8,128)(2,1)} %param.19) | copy-start | bytes 6193156
  40.6 8.5 %copy-start.8 = (bf16[2,1536,336]{1,2,0:T(8,128)(2,1)S(1)}, bf16[2,1536,336]{1,2,0:T(8,128)(2,1)}, u32[]{:S(2)}) copy-start(bf16[2,1536,336]{1,2,0:T(8,128)(2,1)} %param.20) | copy-start | bytes 6193156
  44.1 9.2 %collective-permute-start.9 = (bf16[176,384]{1,0:T(8,128)(2,1)S(1)}, bf16[176,384]{1,0:T(8,128)(2,1)S(1)}, u32[]{:S(2)}, u32[]{:S(2)}) collective-permute-start(bf16[176,384]{1,0:T(8,128)(2,1)S(1)} %get-tuple-element.62), channel_id=1, source_target_pairs={{0,1},{1,2},{2,3},{3,0},{4,5},{5,6},{6,7},{7,4},{8,9},{9,10},{10,1... | collective-permute-start | bytes 405512 | tf_op jit(solution)/shard_map/ppermute | solution.py:54
  45.5 9.5 %collective-permute-start.10 = (bf16[176,384]{1,0:T(8,128)(2,1)S(1)}, bf16[176,384]{1,0:T(8,128)(2,1)S(1)}, u32[]{:S(2)}, u32[]{:S(2)}) collective-permute-start(bf16[176,384]{1,0:T(8,128)(2,1)S(1)} %get-tuple-element.63), channel_id=1, source_target_pairs={{0,2},{1,3},{2,0},{3,1},{4,6},{5,7},{6,4},{7,5},{8,10},{9,11},{10,... | collective-permute-start | bytes 405512 | tf_op jit(solution)/shard_map/ppermute | solution.py:54
  48.1 6.9 %collective-permute-start.11 = (bf16[176,384]{1,0:T(8,128)(2,1)S(1)}, bf16[176,384]{1,0:T(8,128)(2,1)S(1)}, u32[]{:S(2)}, u32[]{:S(2)}) collective-permute-start(bf16[176,384]{1,0:T(8,128)(2,1)S(1)} %get-tuple-element.64), channel_id=1, source_target_pairs={{0,3},{1,0},{2,1},{3,2},{4,7},{5,4},{6,5},{7,6},{8,11},{9,8},{10,9... | collective-permute-start | bytes 405512 | tf_op jit(solution)/shard_map/ppermute | solution.py:54
  50.6 22.4 %copy-start.5 = (bf16[2,336,1536]{2,1,0:T(8,128)(2,1)S(1)}, bf16[2,336,1536]{2,1,0:T(8,128)(2,1)}, u32[]{:S(2)}) copy-start(bf16[2,336,1536]{2,1,0:T(8,128)(2,1)} %param.21) | copy-start | bytes 6193156
  52.0 5.5 %collective-permute-start.12 = (bf16[176,384]{1,0:T(8,128)(2,1)S(1)}, bf16[176,384]{1,0:T(8,128)(2,1)S(1)}, u32[]{:S(2)}, u32[]{:S(2)}) collective-permute-start(bf16[176,384]{1,0:T(8,128)(2,1)S(1)} %get-tuple-element.69), channel_id=1, source_target_pairs={{0,1},{1,2},{2,3},{3,0},{4,5},{5,6},{6,7},{7,4},{8,9},{9,10},{10,1... | collective-permute-start | bytes 405512 | tf_op jit(solution)/shard_map/ppermute | solution.py:54
  52.4 8.1 %collective-permute-start.13 = (bf16[176,384]{1,0:T(8,128)(2,1)S(1)}, bf16[176,384]{1,0:T(8,128)(2,1)S(1)}, u32[]{:S(2)}, u32[]{:S(2)}) collective-permute-start(bf16[176,384]{1,0:T(8,128)(2,1)S(1)} %get-tuple-element.70), channel_id=1, source_target_pairs={{0,2},{1,3},{2,0},{3,1},{4,6},{5,7},{6,4},{7,5},{8,10},{9,11},{10,... | collective-permute-start | bytes 405512 | tf_op jit(solution)/shard_map/ppermute | solution.py:54
  53.2 7.7 %collective-permute-start.14 = (bf16[176,384]{1,0:T(8,128)(2,1)S(1)}, bf16[176,384]{1,0:T(8,128)(2,1)S(1)}, u32[]{:S(2)}, u32[]{:S(2)}) collective-permute-start(bf16[176,384]{1,0:T(8,128)(2,1)S(1)} %get-tuple-element.71), channel_id=1, source_target_pairs={{0,3},{1,0},{2,1},{3,2},{4,7},{5,4},{6,5},{7,6},{8,11},{9,8},{10,9... | collective-permute-start | bytes 405512 | tf_op jit(solution)/shard_map/ppermute | solution.py:54
  61.4 6.0 %collective-permute-start.17 = (bf16[168,384]{1,0:T(8,128)(2,1)S(1)}, bf16[168,384]{1,0:T(8,128)(2,1)S(1)}, u32[]{:S(2)}, u32[]{:S(2)}) collective-permute-start(bf16[168,384]{1,0:T(8,128)(2,1)S(1)} %shard_map.128.hidden0), channel_id=1, source_target_pairs={{0,1},{1,2},{2,3},{3,0},{4,5},{5,6},{6,7},{7,4},{8,9},{9,10},{10,1... | collective-permute-start | bytes 387080 | tf_op jit(solution)/shard_map/ppermute | solution.py:54
  62.3 9.6 %collective-permute-start.16 = (bf16[168,384]{1,0:T(8,128)(2,1)S(1)}, bf16[168,384]{1,0:T(8,128)(2,1)S(1)}, u32[]{:S(2)}, u32[]{:S(2)}) collective-permute-start(bf16[168,384]{1,0:T(8,128)(2,1)S(1)} %shard_map.128.hidden0), channel_id=1, source_target_pairs={{0,2},{1,3},{2,0},{3,1},{4,6},{5,7},{6,4},{7,5},{8,10},{9,11},{10,... | collective-permute-start | bytes 387080 | tf_op jit(solution)/shard_map/ppermute | solution.py:54
  66.2 5.7 %collective-permute-start.15 = (bf16[168,384]{1,0:T(8,128)(2,1)S(1)}, bf16[168,384]{1,0:T(8,128)(2,1)S(1)}, u32[]{:S(2)}, u32[]{:S(2)}) collective-permute-start(bf16[168,384]{1,0:T(8,128)(2,1)S(1)} %shard_map.128.hidden0), channel_id=1, source_target_pairs={{0,3},{1,0},{2,1},{3,2},{4,7},{5,4},{6,5},{7,6},{8,11},{9,8},{10,9... | collective-permute-start | bytes 387080 | tf_op jit(solution)/shard_map/ppermute | solution.py:54
  73.6 2.6 %collective-permute-start.18 = (bf16[64,1536]{1,0:T(8,128)(2,1)S(1)}, bf16[64,1536]{1,0:T(8,128)(2,1)S(1)}, u32[]{:S(2)}, u32[]{:S(2)}) collective-permute-start(bf16[64,1536]{1,0:T(8,128)(2,1)S(1)} %convolution_convert_fusion.1), channel_id=1, source_target_pairs={{0,16},{16,0},{32,48},{48,32},{64,80},{80,64},{96,112},{112,96},{1... | collective-permute-start | bytes 589832 | tf_op jit(solution)/shard_map/ppermute | solution.py:54
  76.9 3.8 %collective-permute-start.19 = (bf16[192,1536]{1,0:T(8,128)(2,1)S(1)}, bf16[192,1536]{1,0:T(8,128)(2,1)S(1)}, u32[]{:S(2)}, u32[]{:S(2)}) collective-permute-start(bf16[192,1536]{1,0:T(8,128)(2,1)S(1)} %convolution_convert_fusion), channel_id=1, source_target_pairs={{0,16},{16,0},{32,48},{48,32},{64,80},{80,64},{96,112},{112,96},{1... | collective-permute-start | bytes 1769480 | tf_op jit(solution)/shard_map/ppermute | solution.py:54
  77.4 7.9 %collective-permute-start.22 = (bf16[64,1536]{1,0:T(8,128)(2,1)S(1)}, bf16[64,1536]{1,0:T(8,128)(2,1)S(1)}, u32[]{:S(2)}, u32[]{:S(2)}) collective-permute-start(bf16[64,1536]{1,0:T(8,128)(2,1)S(1)} %add_convert_fusion), channel_id=1, source_target_pairs={{0,8},{4,12},{8,0},{12,4},{16,24},{20,28},{24,16},{28,20},{32,40},... | collective-permute-start | bytes 589832 | tf_op jit(solution)/shard_map/ppermute | solution.py:54
  80.9 8.4 %collective-permute-start.20 = (bf16[64,1536]{1,0:T(8,128)(2,1)S(1)}, bf16[64,1536]{1,0:T(8,128)(2,1)S(1)}, u32[]{:S(2)}, u32[]{:S(2)}) collective-permute-start(bf16[64,1536]{1,0:T(8,128)(2,1)S(1)} %get-tuple-element.76), channel_id=1, source_target_pairs={{0,4},{4,0},{8,12},{12,8},{16,28},{20,24},{24,20},{28,16},{32,36},... | collective-permute-start | bytes 589832 | tf_op jit(solution)/shard_map/ppermute | solution.py:54
  81.9 7.5 %collective-permute-start.21 = (bf16[64,1536]{1,0:T(8,128)(2,1)S(1)}, bf16[64,1536]{1,0:T(8,128)(2,1)S(1)}, u32[]{:S(2)}, u32[]{:S(2)}) collective-permute-start(bf16[64,1536]{1,0:T(8,128)(2,1)S(1)} %get-tuple-element.77), channel_id=1, source_target_pairs={{0,12},{4,8},{8,4},{12,0},{16,20},{20,16},{24,28},{28,24},{32,44},... | collective-permute-start | bytes 589832 | tf_op jit(solution)/shard_map/ppermute | solution.py:54
  89.6 7.2 %collective-permute-start.24 = (bf16[16,1536]{1,0:T(8,128)(2,1)S(1)}, bf16[16,1536]{1,0:T(8,128)(2,1)S(1)}, u32[]{:S(2)}, u32[]{:S(2)}) collective-permute-start(bf16[16,1536]{1,0:T(8,128)(2,1)S(1)} %get-tuple-element.81), channel_id=1, source_target_pairs={{0,32},{16,240},{32,64},{48,16},{64,96},{80,48},{96,128},{112,80},... | collective-permute-start | bytes 147464 | tf_op jit(solution)/shard_map/ppermute | solution.py:54
  90.9 5.9 %collective-permute-start.25 = (bf16[16,1536]{1,0:T(8,128)(2,1)S(1)}, bf16[16,1536]{1,0:T(8,128)(2,1)S(1)}, u32[]{:S(2)}, u32[]{:S(2)}) collective-permute-start(bf16[16,1536]{1,0:T(8,128)(2,1)S(1)} %get-tuple-element.82), channel_id=1, source_target_pairs={{0,64},{16,208},{32,96},{48,240},{64,128},{80,16},{96,160},{112,48... | collective-permute-start | bytes 147464 | tf_op jit(solution)/shard_map/ppermute | solution.py:54
  91.9 5.5 %collective-permute-start.26 = (bf16[16,1536]{1,0:T(8,128)(2,1)S(1)}, bf16[16,1536]{1,0:T(8,128)(2,1)S(1)}, u32[]{:S(2)}, u32[]{:S(2)}) collective-permute-start(bf16[16,1536]{1,0:T(8,128)(2,1)S(1)} %get-tuple-element.83), channel_id=1, source_target_pairs={{0,96},{16,176},{32,128},{48,208},{64,160},{80,240},{96,192},{112,... | collective-permute-start | bytes 147464 | tf_op jit(solution)/shard_map/ppermute | solution.py:54
  94.0 6.6 %collective-permute-start.23 = (bf16[8,1536]{1,0:T(8,128)(2,1)S(1)}, bf16[8,1536]{1,0:T(8,128)(2,1)S(1)}, u32[]{:S(2)}, u32[]{:S(2)}) collective-permute-start(bf16[8,1536]{1,0:T(8,128)(2,1)S(1)} %slice.69), channel_id=1, source_target_pairs={{0,128},{16,144},{32,160},{48,176},{64,192},{80,208},{96,224},{112... | collective-permute-start | bytes 73736 | tf_op jit(solution)/shard_map/ppermute | solution.py:54
  97.5 3.2 %collective-permute-start.27 = (bf16[8,1536]{1,0:T(8,128)(2,1)S(1)}, bf16[8,1536]{1,0:T(8,128)(2,1)S(1)}, u32[]{:S(2)}, u32[]{:S(2)}) collective-permute-start(bf16[8,1536]{1,0:T(8,128)(2,1)S(1)} %slice.89), channel_id=1, source_target_pairs={{0,16},{16,0},{32,48},{48,32},{64,80},{80,64},{96,112},{112,96},{1... | collective-permute-start | bytes 73736 | tf_op jit(solution)/shard_map/ppermute | solution.py:54
